TPU v7x, 512 devices: a whole 4x4x16 slice. The times are simulated.
512 devices in a mesh: dp: 32 (over z, y_hi), seq: 16 (over y_lo, x, core).
Axes of the slice: x: 4, y: 4 (y_hi: 2, y_lo: 2; y = y_hi * 2 + y_lo), z: 16, core: 2. Of those that a mesh axis runs over, the one named last changes fastest.
Arguments:
- inputs: bfloat16 [32, 2048, 4096], P('dp', 'seq'), may hold values from -6 to 6
- raw_step: bfloat16 [32, 2048, 64], P('dp', 'seq'), may hold values from -5 to 5
- write_keys: bfloat16 [32, 2048, 128], P('dp', 'seq'), may hold values from -0.5 to 0.5
- read_keys: bfloat16 [32, 2048, 128], P('dp', 'seq'), may hold values from -0.5 to 0.5
- grad_out: bfloat16 [32, 2048, 4096], P('dp', 'seq'), may hold values from -6 to 6
- decay_log: float32 [64], P('seq'), as said below
- skip_gain: float32 [64], P('seq'), may hold values from 0.5 to 1.5
- step_bias: float32 [64], P('seq'), may hold values from -1 to 1
Outputs:
- grad_x: bfloat16 [32, 2048, 4096], P('dp', 'seq')
- grad_step: bfloat16 [32, 2048, 64], P('dp', 'seq')
- grad_write: bfloat16 [32, 2048, 128], P('dp', 'seq')
- grad_read: bfloat16 [32, 2048, 128], P('dp', 'seq')
- grad_params: float32 [3, 64], P(None, 'seq')
Inputs may be any that keep to these rules, and one draw needn't show every extreme that they name: exp(decay_log) lies between 0.2 / 2048 and 1 / 20.
All inputs are finite; a program needn't handle non-finite values.
Results may differ from a plain program's by a relative error of at most 0.002.
Values may be sent and summed in bfloat16 or wider, within the bound.
No kernel may reach another device: no remote copies, remote signals or barrier semaphores. Data moves between devices by JAX's collectives and lax.ppermute only.
A program may use at most 128 MiB of HBM per device.

v0:
```python
import jax
import jax.numpy as jnp
from jax import lax
from jax.experimental import pallas as pl
from jax.experimental.pallas import tpu as pltpu
from jax.sharding import PartitionSpec as P

CHUNK = 128
LANES = 128
HDIM = 64
NSTATE = 128
ROWS = 8
MIB = 1 << 20

f32 = jnp.float32
bf16 = jnp.bfloat16


def mm(a, b):
    return jnp.dot(a, b, preferred_element_type=f32)


def mm_nt(a, b):
    return lax.dot_general(a, b, (((1,), (1,)), ((), ())), preferred_element_type=f32)


def mm_tn(a, b):
    return lax.dot_general(a, b, (((0,), (0,)), ((), ())), preferred_element_type=f32)


def split2(v):
    high = v.astype(bf16)
    return high, (v - high.astype(f32)).astype(bf16)


def split3(v):
    high = v.astype(bf16).astype(f32)
    rest = v - high
    mid = rest.astype(bf16).astype(f32)
    return high, mid, rest - mid


def iota(shape, axis):
    return lax.broadcasted_iota(jnp.int32, shape, axis)


def one_hot(cond):
    return jnp.where(cond, 1.0, 0.0)


def mm_exact(v, ones):
    parts = mm(jnp.concatenate(split3(v), axis=0).astype(bf16), ones.astype(bf16))
    n = v.shape[0]
    return parts[:n] + parts[n : 2 * n] + parts[2 * n :]


def pack_kernel(heads, x_ref, g_ref, b_ref, c_ref, s_ref, out_ref):
    group = pl.program_id(0)
    width = heads * HDIM
    for i in range(width // LANES):
        lanes = slice(i * LANES, (i + 1) * LANES)
        out_ref[0, i * CHUNK : (i + 1) * CHUNK] = x_ref[:, lanes]
        out_ref[0, width + i * CHUNK : width + (i + 1) * CHUNK] = g_ref[:, lanes]
    out_ref[0, 2 * width : 2 * width + CHUNK] = b_ref[...]
    out_ref[0, 2 * width + CHUNK : 2 * width + 2 * CHUNK] = c_ref[...]
    shape = (16, s_ref.shape[1])
    pick = one_hot((iota(shape, 1) == iota(shape, 0) + group * heads) & (iota(shape, 0) < heads))
    out_ref[0, 2 * width + 2 * CHUNK :] = mm_nt(pick.astype(bf16), s_ref[...]).astype(bf16)


def pack(x, g, b, c, s, groups):
    heads = s.shape[1] // groups
    width = heads * HDIM
    rows = 2 * width + 2 * CHUNK + 16
    whole = lambda a: pl.BlockSpec(a.shape, lambda j: (0, 0))
    cut = pl.BlockSpec((CHUNK, width), lambda j: (0, j))
    return pl.pallas_call(
        lambda *refs: pack_kernel(heads, *refs),
        grid=(groups,),
        in_specs=[cut, cut, whole(b), whole(c), whole(s)],
        out_specs=pl.BlockSpec((1, rows, LANES), lambda j: (j, 0, 0)),
        out_shape=jax.ShapeDtypeStruct((groups, rows, LANES), bf16),
        name="pack",
    )(x, g, b, c, s)


def scan_kernel(heads, chunks, in_ref, par_ref, out_ref, pout_ref,
                alpha_ref, gamma_ref, total_ref, gh_ref, gl_ref, xh_ref, xl_ref,
                hh_ref, hl_ref, dloc_ref, r_ref, c_ref, skip_ref):
    width = heads * HDIM
    blocks = width // LANES
    at_b, at_c, at_s = 2 * width, 2 * width + CHUNK, 2 * width + 2 * CHUNK
    flat = (chunks * ROWS, LANES)
    cube = (chunks, ROWS, LANES)

    raw = jnp.concatenate([in_ref[k, at_s : at_s + 16].astype(f32)[None, :ROWS] for k in range(chunks)], axis=0)
    rate = -jnp.exp(par_ref[0])
    z = raw + par_ref[2][None]
    step = jnp.maximum(z, 0.0) + jnp.log1p(jnp.exp(-jnp.abs(z)))
    slope = jnp.exp(z - step)
    decay = rate[None] * step
    square = (LANES, LANES)
    upto = one_hot(iota(square, 0) <= iota(square, 1))
    since = one_hot(iota(square, 0) >= iota(square, 1))
    level = mm_exact(decay.reshape(flat), upto)
    total = jnp.exp(jnp.broadcast_to(level[:, LANES - 1 :], flat))
    alpha = jnp.exp(level)
    gamma = jnp.exp(-level) * step.reshape(flat)
    nothing = jnp.zeros(cube, f32)
    for ref, v in ((alpha_ref, alpha), (gamma_ref, gamma)):
        parts = [p.reshape(cube) for p in split3(v)]
        ref[...] = jnp.concatenate(parts + [nothing], axis=1).astype(bf16)
    total_ref[...] = total.reshape(cube)

    of_head = lambda rows: iota((rows, width), 1) // HDIM == iota((rows, width), 0) % ROWS
    spread = one_hot(of_head(ROWS))
    spread4 = one_hot(of_head(4 * ROWS)).astype(bf16)
    gather = one_hot((iota((16, width), 1) // HDIM) == iota((16, width), 0)).astype(bf16)

    def to_lanes(tile):
        return jnp.sum(jnp.concatenate([tile] * blocks, axis=1) * spread, axis=0, keepdims=True)

    def wide(k, start):
        return jnp.concatenate(
            [in_ref[k, start + i * CHUNK : start + (i + 1) * CHUNK] for i in range(blocks)], axis=1
        )

    skip_ref[...] = jnp.zeros_like(skip_ref)

    def forward(k, state):
        x = wide(k, 0).astype(f32)
        g = wide(k, width).astype(f32)
        gt_high, gt_low = split2(mm_tn(alpha_ref[k], spread4) * g)
        xt_high, xt_low = split2(mm_tn(gamma_ref[k], spread4) * x)
        gh_ref[k], gl_ref[k], xh_ref[k], xl_ref[k] = gt_high, gt_low, xt_high, xt_low
        skip_ref[...] += jnp.sum((x * g).reshape(CHUNK // ROWS, ROWS, width), axis=0)
        hh_ref[k], hl_ref[k] = split2(state)
        keys_in, keys_out = in_ref[k, at_b : at_b + CHUNK], in_ref[k, at_c : at_c + CHUNK]
        dloc_ref[k] = mm_tn(keys_out, gt_high) + mm_tn(keys_out, gt_low)
        return to_lanes(total_ref[k]) * (state + mm_tn(keys_in, xt_high) + mm_tn(keys_in, xt_low))

    lax.fori_loop(0, chunks, forward, jnp.zeros((NSTATE, width), f32))

    skip_wide = to_lanes(par_ref[1])
    causal = iota(square, 0) >= iota(square, 1)

    def backward(i, dstate):
        k = chunks - 1 - i
        through = to_lanes(total_ref[k]) * dstate
        dh, dl = split2(through)
        hh, hl = hh_ref[k], hl_ref[k]
        gh, gl, xh, xl = gh_ref[k], gl_ref[k], xh_ref[k], xl_ref[k]
        keys_in, keys_out = in_ref[k, at_b : at_b + CHUNK], in_ref[k, at_c : at_c + CHUNK]

        sh, sl = split2(jnp.where(causal, mm_nt(keys_out, keys_in), 0.0))
        th, tl = split2(jnp.where(causal.T, mm_nt(keys_in, keys_out), 0.0))
        along = lambda *parts: jnp.concatenate(parts, axis=1)
        under = lambda *parts: jnp.concatenate(parts, axis=0)
        y = mm(along(sh, keys_out), under(xh, hh)) + mm(along(sl, keys_out), under(xh, hl)) + mm(sh, xl)
        dx = mm(along(th, keys_in), under(gh, dh)) + mm(along(tl, keys_in), under(gh, dl)) + mm(th, gl)

        ds = mm_nt(gh, xh) + mm_nt(gh, xl) + mm_nt(gl, xh)
        ds = jnp.where(causal, ds, 0.0)
        ph, plow = split2(ds)
        qh, qlow = split2(ds.T)
        d_out = mm(along(ph, plow), under(keys_in, keys_in)) + mm_nt(gh, hh) + mm_nt(gh, hl) + mm_nt(gl, hh)
        d_in = mm(along(qh, qlow), under(keys_out, keys_out)) + mm_nt(xh, dh) + mm_nt(xh, dl) + mm_nt(xl, dh)

        gt = gh.astype(f32) + gl.astype(f32)
        xt = xh.astype(f32) + xl.astype(f32)

        def per_head(v):
            high, low = split2(v)
            return (mm_nt(gather, high) + mm_nt(gather, low))[:ROWS]

        r_ref[k] = per_head(gt * y)
        c_ref[k] = per_head(xt * dx)

        grad_x = mm_tn(gamma_ref[k], spread4) * dx + skip_wide * wide(k, width).astype(f32)
        grad_x = grad_x.astype(bf16)
        for j in range(blocks):
            out_ref[k, j * CHUNK : (j + 1) * CHUNK] = grad_x[:, j * LANES : (j + 1) * LANES]
        for j, part in enumerate(split2(d_in) + split2(d_out)):
            out_ref[k, width + j * CHUNK : width + (j + 1) * CHUNK] = part
        return dloc_ref[k] + through

    lax.fori_loop(0, chunks, backward, jnp.zeros((NSTATE, width), f32))

    col = c_ref[...]
    suffix = mm_exact((r_ref[...] - col).reshape(flat), since).reshape(cube)
    sums = jnp.broadcast_to(suffix[:, :, :1], cube)
    later = jnp.zeros((ROWS, LANES), f32)
    carried = [None] * chunks
    for k in reversed(range(chunks)):
        carried[k] = later[None]
        later = later + sums[k]
    d_decay = suffix + jnp.concatenate(carried, axis=0)
    d_raw = slope * (col / step + rate[None] * d_decay)
    pad = jnp.zeros((ROWS, LANES), f32)
    for k in range(chunks):
        out_ref[k, width + 4 * CHUNK :] = jnp.concatenate([d_raw[k], pad], axis=0).astype(bf16)

    d_skip = jnp.sum(spread * jnp.sum(skip_ref[...], axis=0, keepdims=True), axis=1, keepdims=True)
    tile = (ROWS, LANES)
    result = jnp.zeros(tile, f32)
    per = (
        jnp.sum(jnp.sum(d_decay * decay, axis=0), axis=1, keepdims=True),
        d_skip,
        jnp.sum(jnp.sum(d_raw, axis=0), axis=1, keepdims=True),
    )
    for i, v in enumerate(per):
        row = jnp.sum(jnp.where(iota(tile, 0) == iota(tile, 1), jnp.broadcast_to(v, tile), 0.0), axis=0, keepdims=True)
        result = jnp.where(iota(tile, 0) == i, jnp.broadcast_to(row, tile), result)
    pout_ref[...] = result


def scan_grads(received, params, heads):
    chunks = received.shape[0]
    width = heads * HDIM
    rows = width + 4 * CHUNK + 16
    vmem = pl.BlockSpec(memory_space=pltpu.VMEM)
    wide = lambda dtype: pltpu.VMEM((chunks, CHUNK, width), dtype)
    small = lambda dtype, n: pltpu.VMEM((chunks, n, LANES), dtype)
    return pl.pallas_call(
        lambda *refs: scan_kernel(heads, chunks, *refs),
        in_specs=[vmem, vmem],
        out_specs=[vmem, vmem],
        out_shape=[
            jax.ShapeDtypeStruct((chunks, rows, LANES), bf16),
            jax.ShapeDtypeStruct((ROWS, LANES), f32),
        ],
        scratch_shapes=[
            small(bf16, 4 * ROWS), small(bf16, 4 * ROWS), small(f32, ROWS),
            wide(bf16), wide(bf16), wide(bf16), wide(bf16),
            wide(bf16), wide(bf16), wide(f32),
            small(f32, ROWS), small(f32, ROWS), pltpu.VMEM((ROWS, width), f32),
        ],
        compiler_params=pltpu.CompilerParams(vmem_limit_bytes=40 * MIB),
        name="scan_grads",
    )(received, params)


def unpack_kernel(heads, in_ref, x_ref, s_ref, b_ref, c_ref, b_sum, c_sum, s_sum):
    group = pl.program_id(0)
    width = heads * HDIM

    @pl.when(group == 0)
    def _():
        for ref in (b_sum, c_sum, s_sum):
            ref[...] = jnp.zeros_like(ref)

    for i in range(width // LANES):
        x_ref[:, i * LANES : (i + 1) * LANES] = in_ref[0, i * CHUNK : (i + 1) * CHUNK]
    part = lambda j: in_ref[0, width + j * CHUNK : width + (j + 1) * CHUNK].astype(f32)
    b_sum[...] += part(0) + part(1)
    c_sum[...] += part(2) + part(3)
    shape = (16, s_sum.shape[1])
    pick = one_hot((iota(shape, 1) == iota(shape, 0) + group * heads) & (iota(shape, 0) < heads))
    s_sum[...] += mm_tn(in_ref[0, width + 4 * CHUNK :], pick.astype(bf16))

    @pl.when(group == pl.num_programs(0) - 1)
    def _():
        b_ref[...] = b_sum[...].astype(bf16)
        c_ref[...] = c_sum[...].astype(bf16)
        s_ref[...] = s_sum[...].astype(bf16)


def unpack(received, heads):
    groups, rows, _ = received.shape
    width = heads * HDIM
    whole = lambda *shape: pl.BlockSpec(shape, lambda j: (0, 0))
    shapes = [(CHUNK, groups * width), (CHUNK, groups * heads), (CHUNK, NSTATE), (CHUNK, NSTATE)]
    return pl.pallas_call(
        lambda *refs: unpack_kernel(heads, *refs),
        grid=(groups,),
        in_specs=[pl.BlockSpec((1, rows, LANES), lambda j: (j, 0, 0))],
        out_specs=[pl.BlockSpec((CHUNK, width), lambda j: (0, j))] + [whole(*s) for s in shapes[1:]],
        out_shape=[jax.ShapeDtypeStruct(s, bf16) for s in shapes],
        scratch_shapes=[pltpu.VMEM(shapes[2], f32), pltpu.VMEM(shapes[2], f32), pltpu.VMEM(shapes[1], f32)],
        name="unpack",
    )(received)


def exchange(v):
    return lax.all_to_all(v, "seq", split_axis=0, concat_axis=0, tiled=True)


def replica_sum(v):
    replicas = lax.axis_size("dp")
    if replicas == 1:
        return v
    v = v + lax.ppermute(v, "dp", [(i, i ^ 1) for i in range(replicas)])
    if replicas == 2:
        return v
    lines = [[2 * i + half for i in range(replicas // 2)] for half in range(2)]
    return lax.psum(v, "dp", axis_index_groups=lines)


def shards(inputs, raw_step, write_keys, read_keys, grad_out, decay_log, skip_gain, step_bias):
    groups = lax.axis_size("seq")
    heads = decay_log.shape[0]
    send = pack(inputs[0], grad_out[0], write_keys[0], read_keys[0], raw_step[0], groups)
    params = jnp.stack([decay_log, skip_gain, step_bias])
    params = jnp.concatenate([params] * (ROWS // heads), axis=1)
    params = jnp.broadcast_to(params[:, :, None], (3, ROWS, LANES))
    back, per_head = scan_grads(exchange(send), params, heads)
    grad_x, grad_step, grad_write, grad_read = unpack(exchange(back), heads)
    totals = replica_sum(per_head)[:3, :heads] / lax.axis_size("dp")
    return grad_x[None], grad_step[None], grad_write[None], grad_read[None], totals


def solution(mesh):
    rows = P("dp", "seq", None)
    heads = P("seq")
    return jax.shard_map(
        shards,
        mesh=mesh,
        in_specs=(rows,) * 5 + (heads,) * 3,
        out_specs=(rows,) * 4 + (P(None, "seq"),),
        check_vma=False,
    )
```

profile of v0, /device:TPU:2, one launch (start us, length us, event | category | flops | bytes accessed | tf_op | source)
XLA Modules:
  0.0 177.0 jit_solution(10912835592485345035)
XLA Ops:
  0.6 1.4 copy.13
  2.1 10.3 %pack.1 = bf16[16,784,128]{2,1,0:T(8,128)(2,1)} custom-call(bf16[128,4096]{1,0:T(8,128)(2,1)} %bitcast.12, bf16[128,4096]{1,0:T(8,128)(2,1)} %bitcast.13, bf16[128,128]{1,0:T(8,128)(2,1)} %bitcast.15, bf16[128,128]{1,0:T(8,128)(2,1)} %bitcast.16, bf16[128,64]{1,0:T(8,128)(2,1)} %bitcast.14), custom_call_target="tpu_custom_call" | custom-call | tf_op jit(solution)/shard_map/pack/pallas_call | solution.py:77
  12.3 0.0 copy-start.2
  12.3 0.0 copy-start.3
  12.3 0.0 copy-start.4
  12.3 9.6 %all-to-all-start = ((bf16[16,784,128]{2,1,0:T(8,128)(2,1)}), bf16[16,784,128]{2,1,0:T(8,128)(2,1)S(1)}, u32[]{:S(2)}, u32[]{:S(2)}) async-start(bf16[16,784,128]{2,1,0:T(8,128)(2,1)} %pack.1), calls=%async_computation | async-start | bytes 6422528 | tf_op jit(solution)/shard_map/all_to_all | solution.py:285
  21.9 0.0 copy-done.2
  21.9 0.0 copy-done.3
  21.9 0.0 copy-done.4
  22.0 0.1 maximum_maximum_fusion
  22.0 43.6 %all-to-all-done.refs_0_ = bf16[16,784,128]{2,1,0:T(8,128)(2,1)S(1)} async-done(((bf16[16,784,128]{2,1,0:T(8,128)(2,1)}), bf16[16,784,128]{2,1,0:T(8,128)(2,1)S(1)}, u32[]{:S(2)}, u32[]{:S(2)}) %all-to-all-start) | async-done | bytes 3211296 | tf_op jit(solution)/shard_map/all_to_all | solution.py:285
  65.7 0.1 broadcast_in_dim.18.refs_1_
  65.7 19.8 %scan_grads.1 = (bf16[16,784,128]{2,1,0:T(8,128)(2,1)S(1)}, f32[8,128]{1,0:T(8,128)S(1)}) custom-call(bf16[16,784,128]{2,1,0:T(8,128)(2,1)S(1)} %all-to-all-done.refs_0_, f32[3,8,128]{2,1,0:T(8,128)S(1)} %broadcast_in_dim.18.refs_1_), custom_call_target="tpu_custom_call" | custom-call | tf_op jit(solution)/shard_map/scan_grads/pallas_call | solution.py:224
  85.6 0.0 copy-start
  85.6 1.7 copy-done
  87.2 4.0 %all-to-all-start.1 = ((bf16[16,784,128]{2,1,0:T(8,128)(2,1)}), bf16[16,784,128]{2,1,0:T(8,128)(2,1)S(1)}, u32[]{:S(2)}, u32[]{:S(2)}) async-start(bf16[16,784,128]{2,1,0:T(8,128)(2,1)} %copy-done), calls=%async_computation.1 | async-start | bytes 6422528 | tf_op jit(solution)/shard_map/all_to_all | solution.py:285
  91.2 1.9 %collective-permute-start = (f32[8,128]{1,0:T(8,128)S(1)}, f32[8,128]{1,0:T(8,128)S(1)}, u32[]{:S(2)}, u32[]{:S(2)}) collective-permute-start(f32[8,128]{1,0:T(8,128)S(1)} %get-tuple-element.16), channel_id=1, source_target_pairs={{0,16},{16,0},{32,48},{48,32},{64,80},{80,64},{96,112},{112,96},{1... | collective-permute-start | bytes 12296 | tf_op jit(solution)/shard_map/ppermute | solution.py:292
  93.2 33.4 %collective-permute-done = f32[8,128]{1,0:T(8,128)S(1)} collective-permute-done((f32[8,128]{1,0:T(8,128)S(1)}, f32[8,128]{1,0:T(8,128)S(1)}, u32[]{:S(2)}, u32[]{:S(2)}) %collective-permute-start) | collective-permute-done | bytes 4128 | tf_op jit(solution)/shard_map/ppermute | solution.py:292
  126.5 36.1 %psum.7 = f32[8,128]{1,0:T(8,128)S(1)} all-reduce(f32[8,128]{1,0:T(8,128)S(1)} %add.5), channel_id=1, replica_groups={{0,32,64,96,128,160,192,224,256,288,320,352,384,416,448,480},{16,48,80,..., use_global_device_ids=true, to_apply=%region_0.0 | all-reduce | flops 1024 | bytes 8192 | tf_op jit(solution)/shard_map/psum | solution.py:296
  162.6 0.6 slice_multiply_fusion
  163.2 0.0 all-to-all-done.1.refs_0_
  163.2 0.0 copy-start.1
  163.2 1.7 copy-done.1
  164.9 10.6 %unpack.1 = (bf16[128,4096]{1,0:T(8,128)(2,1)}, bf16[128,64]{1,0:T(8,128)(2,1)}, bf16[128,128]{1,0:T(8,128)(2,1)}, bf16[128,128]{1,0:T(8,128)(2,1)}) custom-call(bf16[16,784,128]{2,1,0:T(8,128)(2,1)} %copy-done.1), custom_call_target="tpu_custom_call" | custom-call | tf_op jit(solution)/shard_map/unpack/pallas_call | solution.py:273
  175.5 1.4 copy.14
  (1 shorter events, 0.0 us)
Async XLA Ops:
  12.3 9.6 %copy-start.2 = (f32[4]{0:T(128)S(1)}, f32[4]{0:T(128)}, u32[]{:S(2)}) copy-start(f32[4]{0:T(128)} %param.15) | copy-start | bytes 52
  12.3 9.6 %copy-start.3 = (f32[4]{0:T(128)S(1)}, f32[4]{0:T(128)}, u32[]{:S(2)}) copy-start(f32[4]{0:T(128)} %param.14) | copy-start | bytes 52
  12.3 9.6 %copy-start.4 = (f32[4]{0:T(128)S(1)}, f32[4]{0:T(128)}, u32[]{:S(2)}) copy-start(f32[4]{0:T(128)} %param.13) | copy-start | bytes 52
  12.3 53.3 %all-to-all-start = ((bf16[16,784,128]{2,1,0:T(8,128)(2,1)}), bf16[16,784,128]{2,1,0:T(8,128)(2,1)S(1)}, u32[]{:S(2)}, u32[]{:S(2)}) async-start(bf16[16,784,128]{2,1,0:T(8,128)(2,1)} %pack.1), calls=%async_computation | async-start | bytes 6422528 | tf_op jit(solution)/shard_map/all_to_all | solution.py:285
  85.6 1.7 copy-start
  87.2 76.0 %all-to-all-start.1 = ((bf16[16,784,128]{2,1,0:T(8,128)(2,1)}), bf16[16,784,128]{2,1,0:T(8,128)(2,1)S(1)}, u32[]{:S(2)}, u32[]{:S(2)}) async-start(bf16[16,784,128]{2,1,0:T(8,128)(2,1)} %copy-done), calls=%async_computation.1 | async-start | bytes 6422528 | tf_op jit(solution)/shard_map/all_to_all | solution.py:285
  91.2 35.3 %collective-permute-start = (f32[8,128]{1,0:T(8,128)S(1)}, f32[8,128]{1,0:T(8,128)S(1)}, u32[]{:S(2)}, u32[]{:S(2)}) collective-permute-start(f32[8,128]{1,0:T(8,128)S(1)} %get-tuple-element.16), channel_id=1, source_target_pairs={{0,16},{16,0},{32,48},{48,32},{64,80},{80,64},{96,112},{112,96},{1... | collective-permute-start | bytes 12296 | tf_op jit(solution)/shard_map/ppermute | solution.py:292
  163.2 1.7 copy-start.1
where the time goes:
time: 178 us; the launch traced here: 177 us
  waiting for transfers between devices  77 us (43%)
  Pallas kernels  40.7 us (23%)
  blocking collectives  36.1 us (20%)
  starting transfers between devices  15.5 us (9%)
  local copies, waits for them, and re-layouts  6.27 us (4%)
    all_to_all x2, waiting for transfers between devices, exchange(): return lax.all_to_all(v, 'seq', split_axis=0, concat_axis=0, tiled=True)  43.6 us
    psum x1, blocking collectives, replica_sum(): return lax.psum(v, 'dp', axis_index_groups=lines)  36.1 us
    ppermute x1, waiting for transfers between devices, replica_sum(): v = v + lax.ppermute(v, 'dp', [(i, i ^ 1) for i in range(replicas)])  33.4 us
    pallas_call x1, Pallas kernels, scan_grads(): pl.pallas_call(lambda *refs: scan_kernel(heads, chunks, *refs), in_specs=...  19.8 us
    all_to_all x2, starting transfers between devices, exchange(): return lax.all_to_all(v, 'seq', split_axis=0, concat_axis=0, tiled=True)  13.6 us
    pallas_call x1, Pallas kernels, unpack(): pl.pallas_call(lambda *refs: unpack_kernel(heads, *refs), grid=(groups,),...  10.6 us
    pallas_call x1, Pallas kernels, pack(): pl.pallas_call(lambda *refs: pack_kernel(heads, *refs), grid=(groups,), i...  10.3 us
    unnamed x12, local copies, waits for them, and re-layouts  6.2 us
  transfers between devices with their start and end apart: 3, of which 2 were waited for; matrix products, arithmetic and copies ran while one was open for 0% of the time, Pallas kernels for 0%

commit v1 on v0

v1 whole, which is shorter than its diff:
```python
import jax
import jax.numpy as jnp
from jax import lax
from jax.experimental import pallas as pl
from jax.experimental.pallas import tpu as pltpu
from jax.sharding import PartitionSpec as P

CHUNK = 128
LANES = 128
HDIM = 64
NSTATE = 128
ROWS = 8
MIB = 1 << 20
PACK_STEPS = 2
UNPACK_STEPS = 2
PER_TILE = LANES // (2 * ROWS)
UNROLL = 4
SCAN_VMEM = 44
UNPACK_VMEM = 24

f32 = jnp.float32
bf16 = jnp.bfloat16


def mm(a, b):
    return jnp.dot(a, b, preferred_element_type=f32)


def mm_nt(a, b):
    return lax.dot_general(a, b, (((1,), (1,)), ((), ())), preferred_element_type=f32)


def mm_tn(a, b):
    return lax.dot_general(a, b, (((0,), (0,)), ((), ())), preferred_element_type=f32)


def split2(v):
    high = v.astype(bf16)
    return high, (v - high.astype(f32)).astype(bf16)


def split3(v):
    high = v.astype(bf16).astype(f32)
    rest = v - high
    mid = rest.astype(bf16).astype(f32)
    return high, mid, rest - mid


def iota(shape, axis):
    return lax.broadcasted_iota(jnp.int32, shape, axis)


def one_hot(cond):
    return jnp.where(cond, 1.0, 0.0)


def mm_exact(v, ones):
    parts = mm(jnp.concatenate(split3(v), axis=0).astype(bf16), ones.astype(bf16))
    n = v.shape[0]
    return parts[:n] + parts[n : 2 * n] + parts[2 * n :]


def pack_kernel(heads, x_ref, g_ref, b_ref, c_ref, s_ref, out_ref):
    width = heads * HDIM
    tall = 2 * width + 2 * CHUNK
    for n in range(out_ref.shape[0]):
        for i in range(width // LANES):
            lanes = slice(n * width + i * LANES, n * width + (i + 1) * LANES)
            out_ref[n, i * CHUNK : (i + 1) * CHUNK] = x_ref[:, lanes]
            out_ref[n, width + i * CHUNK : width + (i + 1) * CHUNK] = g_ref[:, lanes]
        out_ref[n, 2 * width : 2 * width + CHUNK] = b_ref[...]
        out_ref[n, 2 * width + CHUNK : tall] = c_ref[...]
        group = pl.program_id(0) * out_ref.shape[0] + n
        shape = (16, s_ref.shape[0])
        pick = one_hot((iota(shape, 1) == iota(shape, 0) + group * heads) & (iota(shape, 0) < heads))
        out_ref[n, tall:] = mm(pick.astype(bf16), s_ref[...]).astype(bf16)


def pack(x, g, b, c, s, groups):
    heads = s.shape[0] // groups
    width = heads * HDIM
    rows = 2 * width + 2 * CHUNK + 16
    part = groups // PACK_STEPS
    whole = lambda a: pl.BlockSpec(a.shape, lambda j: (0, 0))
    cut = pl.BlockSpec((CHUNK, part * width), lambda j: (0, j))
    return pl.pallas_call(
        lambda *refs: pack_kernel(heads, *refs),
        grid=(PACK_STEPS,),
        in_specs=[cut, cut, whole(b), whole(c), whole(s)],
        out_specs=pl.BlockSpec((part, rows, LANES), lambda j: (j, 0, 0)),
        out_shape=jax.ShapeDtypeStruct((groups, rows, LANES), bf16),
        compiler_params=pltpu.CompilerParams(vmem_limit_bytes=56 * MIB),
        name="pack",
    )(x, g, b, c, s)


def scan_kernel(heads, chunks, in_ref, given_ref, out_hbm, pout_ref,
                out_ref, dstep_ref, par_ref, alpha_ref, gamma_ref, total_ref,
                gh_ref, gl_ref, xh_ref, xl_ref, hh_ref, hl_ref, dloc_ref, wide_ref, pick_ref, r_ref, c_ref, skip_ref,
                step_sem, out_sem):
    width = heads * HDIM
    blocks = width // LANES
    at_b, at_c, at_s = 2 * width, 2 * width + CHUNK, 2 * width + 2 * CHUNK
    flat = (chunks * ROWS, LANES)
    cube = (chunks, ROWS, LANES)
    body = width + 4 * CHUNK

    put_steps = pltpu.make_async_copy(dstep_ref, out_hbm.at[:, body : body + 16], step_sem)
    put = lambda k: pltpu.make_async_copy(out_ref.at[k], out_hbm.at[k, :body], out_sem.at[k])

    tile = (ROWS, LANES)
    for i in range(3):
        row = jnp.broadcast_to(given_ref[i : i + 1], tile)
        mine = jnp.where(iota(tile, 1) == iota(tile, 0), row, 0.0)
        par_ref[i] = jnp.broadcast_to(jnp.sum(mine, axis=1, keepdims=True), tile)

    raw = in_ref[:, at_s : at_s + 16].astype(f32)[:, :ROWS]
    rate = -jnp.exp(par_ref[0])
    z = raw + par_ref[2][None]
    step = jnp.maximum(z, 0.0) + jnp.log1p(jnp.exp(-jnp.abs(z)))
    slope = jnp.exp(z - step)
    decay = rate[None] * step
    square = (LANES, LANES)
    upto = one_hot(iota(square, 0) <= iota(square, 1))
    since = one_hot(iota(square, 0) >= iota(square, 1))
    level = mm_exact(decay.reshape(flat), upto)
    total = jnp.exp(jnp.broadcast_to(level[:, LANES - 1 :], flat))
    alpha = jnp.exp(level)
    gamma = jnp.exp(-level) * step.reshape(flat)
    for ref, v in ((alpha_ref, alpha), (gamma_ref, gamma)):
        high = v.astype(bf16).astype(f32)
        parts = jnp.concatenate([high.reshape(cube), (v - high).reshape(cube)], axis=1)
        parts = parts.reshape(chunks // PER_TILE, LANES, LANES)
        for i in range(chunks // PER_TILE):
            ref[i] = parts[i].T.astype(bf16)
    total_ref[...] = total.reshape(cube)

    of_head = lambda rows: iota((rows, width), 1) // HDIM == iota((rows, width), 0) % ROWS
    spread = one_hot(of_head(ROWS))
    in_tile = (LANES, width)
    at_head = iota(in_tile, 1) // HDIM == iota(in_tile, 0) % ROWS
    eye = one_hot(iota(square, 0) == iota(square, 1)).astype(bf16)
    gather = one_hot((iota((16, width), 1) // HDIM) == iota((16, width), 0)).astype(bf16)

    def to_lanes(tile):
        return jnp.sum(jnp.concatenate([tile] * blocks, axis=1) * spread, axis=0, keepdims=True)

    for i in range(PER_TILE):
        pick_ref[i] = one_hot(at_head & (iota(in_tile, 0) // (2 * ROWS) == i)).astype(bf16)

    def expand(ref, k):
        return mm(ref[k // PER_TILE], pick_ref[k % PER_TILE])

    def flip(v):
        return mm_nt(eye, v).astype(bf16)

    along = lambda *parts: jnp.concatenate(parts, axis=1)
    under = lambda *parts: jnp.concatenate(parts, axis=0)

    def wide(k, start):
        return jnp.concatenate(
            [in_ref[k, start + i * CHUNK : start + (i + 1) * CHUNK] for i in range(blocks)], axis=1
        )

    skip_ref[...] = jnp.zeros_like(skip_ref)

    def forward(k, state):
        x = wide(k, 0).astype(f32)
        g = wide(k, width).astype(f32)
        gt_high, gt_low = split2(expand(alpha_ref, k) * g)
        wide_ref[k] = expand(gamma_ref, k)
        xt_high, xt_low = split2(wide_ref[k] * x)
        gh_ref[k], gl_ref[k], xh_ref[k], xl_ref[k] = gt_high, gt_low, xt_high, xt_low
        skip_ref[...] += jnp.sum((x * g).reshape(CHUNK // ROWS, ROWS, width), axis=0)
        hh_ref[k], hl_ref[k] = split2(state)
        keys_in, keys_out = in_ref[k, at_b : at_b + CHUNK], in_ref[k, at_c : at_c + CHUNK]
        keys_in, keys_out = flip(keys_in), flip(keys_out)
        dloc_ref[k] = mm(along(keys_out, keys_out), under(gt_high, gt_low))
        return to_lanes(total_ref[k]) * (state + mm(along(keys_in, keys_in), under(xt_high, xt_low)))

    def forwards(i, state):
        for n in range(UNROLL):
            state = forward(i * UNROLL + n, state)
        return state

    nothing = jnp.zeros((NSTATE, width), f32)
    lax.fori_loop(0, chunks // UNROLL, forwards, nothing)

    skip_wide = to_lanes(par_ref[1])
    causal = iota(square, 0) >= iota(square, 1)

    def backward(k, dstate):
        through = to_lanes(total_ref[k]) * dstate
        dh, dl = split2(through)
        hh, hl = hh_ref[k], hl_ref[k]
        gh, gl, xh, xl = gh_ref[k], gl_ref[k], xh_ref[k], xl_ref[k]
        keys_in, keys_out = in_ref[k, at_b : at_b + CHUNK], in_ref[k, at_c : at_c + CHUNK]

        sh, sl = split2(jnp.where(causal, mm_nt(keys_out, keys_in), 0.0))
        th, tl = split2(jnp.where(causal.T, mm_nt(keys_in, keys_out), 0.0))
        xhh, xhl, gdh, gdl = under(xh, hh), under(xl, hl), under(gh, dh), under(gl, dl)
        out_h, in_h = along(sh, keys_out), along(th, keys_in)
        y = mm(out_h, xhh) + mm(out_h, xhl) + mm(sl, xh)
        dx = mm(in_h, gdh) + mm(in_h, gdl) + mm(tl, gh)

        ds = mm_nt(gh, xh) + mm_nt(gh, xl) + mm_nt(gl, xh)
        ds = jnp.where(causal, ds, 0.0)
        ph, plow = split2(ds)
        qh, qlow = split2(ds.T)
        d_out = mm(along(ph, plow), under(keys_in, keys_in)) + mm_nt(gh, hh) + mm_nt(gh, hl) + mm_nt(gl, hh)
        d_in = mm(along(qh, qlow), under(keys_out, keys_out)) + mm_nt(xh, dh) + mm_nt(xh, dl) + mm_nt(xl, dh)

        gt = gh.astype(f32) + gl.astype(f32)
        xt = xh.astype(f32) + xl.astype(f32)

        high, low = split2(under(gt * y, xt * dx))
        sums = mm_nt(gather, high) + mm_nt(gather, low)
        r_ref[k], c_ref[k] = sums[:ROWS, :CHUNK], sums[:ROWS, CHUNK:]

        grad_x = wide_ref[k] * dx + skip_wide * wide(k, width).astype(f32)
        grad_x = grad_x.astype(bf16)
        for j in range(blocks):
            out_ref[k, j * CHUNK : (j + 1) * CHUNK] = grad_x[:, j * LANES : (j + 1) * LANES]
        for j, part in enumerate(split2(d_in) + split2(d_out)):
            out_ref[k, width + j * CHUNK : width + (j + 1) * CHUNK] = part
        return dloc_ref[k] + through

    def backwards(i, dstate):
        top = chunks - 1 - i * UNROLL
        for n in range(UNROLL):
            dstate = backward(top - n, dstate)
        for n in range(UNROLL):
            put(top - n).start()
        return dstate

    lax.fori_loop(0, chunks // UNROLL, backwards, nothing)

    col = c_ref[...]
    suffix = mm_exact((r_ref[...] - col).reshape(flat), since).reshape(cube)
    sums = jnp.broadcast_to(suffix[:, :, :1], cube)
    later = jnp.zeros((ROWS, LANES), f32)
    carried = [None] * chunks
    for k in reversed(range(chunks)):
        carried[k] = later[None]
        later = later + sums[k]
    d_decay = suffix + jnp.concatenate(carried, axis=0)
    d_raw = slope * (col / step + rate[None] * d_decay)
    dstep_ref[...] = jnp.concatenate([d_raw, jnp.zeros(cube, f32)], axis=1).astype(bf16)
    put_steps.start()

    d_skip = jnp.sum(spread * jnp.sum(skip_ref[...], axis=0, keepdims=True), axis=1, keepdims=True)
    result = jnp.zeros(tile, f32)
    per = (
        jnp.sum(jnp.sum(d_decay * decay, axis=0), axis=1, keepdims=True),
        d_skip,
        jnp.sum(jnp.sum(d_raw, axis=0), axis=1, keepdims=True),
    )
    for i, v in enumerate(per):
        row = jnp.sum(jnp.where(iota(tile, 0) == iota(tile, 1), jnp.broadcast_to(v, tile), 0.0), axis=0, keepdims=True)
        result = jnp.where(iota(tile, 0) == i, jnp.broadcast_to(row, tile), result)
    pout_ref[...] = result
    put_steps.wait()
    for k in range(chunks):
        put(k).wait()


def scan_grads(received, params, heads):
    chunks = received.shape[0]
    width = heads * HDIM
    rows = width + 4 * CHUNK + 16
    vmem = pl.BlockSpec(memory_space=pltpu.VMEM)
    wide = lambda dtype: pltpu.VMEM((chunks, CHUNK, width), dtype)
    tiles = pltpu.VMEM((chunks // PER_TILE, LANES, LANES), bf16)
    small = lambda dtype, n: pltpu.VMEM((chunks, n, LANES), dtype)
    return pl.pallas_call(
        lambda *refs: scan_kernel(heads, chunks, *refs),
        in_specs=[vmem, vmem],
        out_specs=[pl.BlockSpec(memory_space=pltpu.HBM), vmem],
        out_shape=[
            jax.ShapeDtypeStruct((chunks, rows, LANES), bf16),
            jax.ShapeDtypeStruct((ROWS, LANES), f32),
        ],
        scratch_shapes=[
            pltpu.VMEM((chunks, rows - 16, LANES), bf16), small(bf16, 16), pltpu.VMEM((3, ROWS, LANES), f32), tiles, tiles, small(f32, ROWS),
            wide(bf16), wide(bf16), wide(bf16), wide(bf16),
            wide(bf16), wide(bf16), wide(f32), wide(f32), pltpu.VMEM((PER_TILE, LANES, width), bf16),
            small(f32, ROWS), small(f32, ROWS), pltpu.VMEM((ROWS, width), f32),
            pltpu.SemaphoreType.DMA, pltpu.SemaphoreType.DMA((chunks,)),
        ],
        compiler_params=pltpu.CompilerParams(vmem_limit_bytes=SCAN_VMEM * MIB),
        name="scan_grads",
    )(received, params)


def unpack_kernel(heads, in_ref, x_ref, s_ref, b_ref, c_ref, b_sum, c_sum, s_sum):
    width = heads * HDIM

    @pl.when(pl.program_id(0) == 0)
    def _():
        for ref in (b_sum, c_sum, s_sum):
            ref[...] = jnp.zeros_like(ref)

    for n in range(in_ref.shape[0]):
        for i in range(width // LANES):
            lanes = slice(n * width + i * LANES, n * width + (i + 1) * LANES)
            x_ref[:, lanes] = in_ref[n, i * CHUNK : (i + 1) * CHUNK]
    part = lambda n, j: in_ref[n, width + j * CHUNK : width + (j + 1) * CHUNK].astype(f32)
    every = range(in_ref.shape[0])
    b_sum[...] += sum(part(n, 0) + part(n, 1) for n in every)
    c_sum[...] += sum(part(n, 2) + part(n, 3) for n in every)
    shape = (s_sum.shape[0], 16)
    for n in every:
        group = pl.program_id(0) * in_ref.shape[0] + n
        place = one_hot((iota(shape, 0) == iota(shape, 1) + group * heads) & (iota(shape, 1) < heads))
        s_sum[...] += mm(place.astype(bf16), in_ref[n, width + 4 * CHUNK :])

    @pl.when(pl.program_id(0) == pl.num_programs(0) - 1)
    def _():
        b_ref[...] = b_sum[...].astype(bf16)
        c_ref[...] = c_sum[...].astype(bf16)
        s_ref[...] = s_sum[...].astype(bf16)


def unpack(received, heads):
    groups, rows, _ = received.shape
    width = heads * HDIM
    part = groups // UNPACK_STEPS
    whole = lambda *shape: pl.BlockSpec(shape, lambda j: (0, 0))
    shapes = [(CHUNK, groups * width), (groups * heads, CHUNK), (CHUNK, NSTATE), (CHUNK, NSTATE)]
    return pl.pallas_call(
        lambda *refs: unpack_kernel(heads, *refs),
        grid=(UNPACK_STEPS,),
        in_specs=[pl.BlockSpec((part, rows, LANES), lambda j: (j, 0, 0))],
        out_specs=[pl.BlockSpec((CHUNK, part * width), lambda j: (0, j))] + [whole(*s) for s in shapes[1:]],
        out_shape=[jax.ShapeDtypeStruct(s, bf16) for s in shapes],
        scratch_shapes=[pltpu.VMEM(shapes[2], f32), pltpu.VMEM(shapes[2], f32), pltpu.VMEM(shapes[1], f32)],
        compiler_params=pltpu.CompilerParams(vmem_limit_bytes=UNPACK_VMEM * MIB),
        name="unpack",
    )(received)


def exchange(v):
    return lax.all_to_all(v, "seq", split_axis=0, concat_axis=0, tiled=True)


def pair_sum(v):
    replicas = lax.axis_size("dp")
    if replicas == 1:
        return v
    return v + lax.ppermute(v, "dp", [(i, i ^ 1) for i in range(replicas)])


def line_sum(v):
    half = lax.axis_size("dp") // 2
    if half <= 1:
        return v
    return lax.psum(v, "dp", axis_index_groups=[[2 * i + bit for i in range(half)] for bit in range(2)])


def shards(inputs, raw_step, write_keys, read_keys, grad_out, decay_log, skip_gain, step_bias):
    groups = lax.axis_size("seq")
    heads = decay_log.shape[0]
    send = pack(inputs[0], grad_out[0], write_keys[0], read_keys[0], raw_step[0].T, groups)
    params = jnp.stack([decay_log, skip_gain, step_bias])
    params = jnp.pad(jnp.concatenate([params] * (ROWS // heads), axis=1), ((0, 0), (0, LANES - ROWS)))
    back, per_head = scan_grads(exchange(send), params, heads)
    back, per_head = lax.optimization_barrier((back, pair_sum(per_head)))
    grad_x, grad_step, grad_write, grad_read = unpack(exchange(back), heads)
    totals = line_sum(per_head)[:3, :heads] / lax.axis_size("dp")
    return grad_x[None], grad_step.T[None], grad_write[None], grad_read[None], totals


def solution(mesh):
    rows = P("dp", "seq", None)
    heads = P("seq")
    return jax.shard_map(
        shards,
        mesh=mesh,
        in_specs=(rows,) * 5 + (heads,) * 3,
        out_specs=(rows,) * 4 + (P(None, "seq"),),
        check_vma=False,
    )
```

time: 178 us -> 135 us (0.76)
  waiting for transfers between devices: 77 us -> 59.1 us
  Pallas kernels: 40.7 us -> 24.4 us
  local copies, waits for them, and re-layouts: 6.27 us -> 1.65 us
  blocking collectives: 36.1 us -> 32.8 us
    ppermute x1, waiting for transfers between devices: 33.4 us -> 5.08 us  [pair_sum(): return v + lax.ppermute(v, 'dp', [(i, i ^ 1) for i in range(replicas)])]
    pallas_call x2, Pallas kernels: 20.9 us -> 4.84 us  [the longest x1 3.13 us: pack(): pl.pallas_call(lambda *refs: pack_kernel(heads, *refs), grid=(PACK_STEPS,...]
    all_to_all x2, waiting for transfers between devices: 43.6 us -> 54 us  [exchange(): return lax.all_to_all(v, 'seq', split_axis=0, concat_axis=0, tiled=True)]
    unnamed x12 -> x8, local copies, waits for them, and re-layouts: 6.2 us -> 1.65 us
    psum x1, blocking collectives: 36.1 us -> 32.8 us  [line_sum(): lax.psum(v, 'dp', axis_index_groups=[[2 * i + bit for i in range(half)] f...]
  transfers between devices with their start and end apart: 3 -> 3, of which waited for: 2 -> 3; matrix products, arithmetic and copies ran while one was open for 0% -> 0% of each run, Pallas kernels for 0% -> 0%
where the time goes in v1:
time: 135 us
  waiting for transfers between devices  59.1 us (44%)
  blocking collectives  32.8 us (24%)
  Pallas kernels  24.4 us (18%)
  starting transfers between devices  15.5 us (11%)
  local copies, waits for them, and re-layouts  1.65 us (1%)
    all_to_all x2, waiting for transfers between devices, exchange(): return lax.all_to_all(v, 'seq', split_axis=0, concat_axis=0, tiled=True)  54 us
    psum x1, blocking collectives, line_sum(): lax.psum(v, 'dp', axis_index_groups=[[2 * i + bit for i in range(half)] f...  32.8 us
    pallas_call x1, Pallas kernels, scan_grads(): pl.pallas_call(lambda *refs: scan_kernel(heads, chunks, *refs), in_specs=...  19.6 us
    all_to_all x2, starting transfers between devices, exchange(): return lax.all_to_all(v, 'seq', split_axis=0, concat_axis=0, tiled=True)  13.6 us
    ppermute x1, waiting for transfers between devices, pair_sum(): return v + lax.ppermute(v, 'dp', [(i, i ^ 1) for i in range(replicas)])  5.08 us
    pallas_call x1, Pallas kernels, pack(): pl.pallas_call(lambda *refs: pack_kernel(heads, *refs), grid=(PACK_STEPS,...  3.13 us
  transfers between devices with their start and end apart: 3, of which 3 were waited for; matrix products, arithmetic and copies ran while one was open for 0% of the time, Pallas kernels for 0%

profile of v1, /device:TPU:2, one launch (start us, length us, event | category | flops | bytes accessed | tf_op | source)
XLA Modules:
  0.0 134.9 jit_solution(7926779125250996847)
XLA Ops:
  0.6 3.1 %pack.1 = bf16[16,784,128]{2,1,0:T(8,128)(2,1)} custom-call(bf16[128,4096]{1,0:T(8,128)(2,1)} %bitcast.16, bf16[128,4096]{1,0:T(8,128)(2,1)} %bitcast.17, bf16[128,128]{1,0:T(8,128)(2,1)} %bitcast.18, bf16[128,128]{1,0:T(8,128)(2,1)} %bitcast.19, bf16[64,128]{1,0:T(8,128)(2,1)} %bitcast.20), custom_call_target="tpu_custom_call" | custom-call | tf_op jit(solution)/shard_map/pack/pallas_call | solution.py:86
  3.8 0.0 copy-start.1
  3.8 0.0 copy-start.2
  3.8 0.0 copy-start.3
  3.8 9.6 %all-to-all-start = ((bf16[16,784,128]{2,1,0:T(8,128)(2,1)}), bf16[16,784,128]{2,1,0:T(8,128)(2,1)S(1)}, u32[]{:S(2)}, u32[]{:S(2)}) async-start(bf16[16,784,128]{2,1,0:T(8,128)(2,1)} %pack.1), calls=%async_computation | async-start | bytes 6422528 | tf_op jit(solution)/shard_map/all_to_all | solution.py:343
  13.4 0.0 copy-done.1
  13.4 0.0 copy-done.2
  13.4 0.0 copy-done.3
  13.4 0.1 fusion.refs_1_
  13.5 43.6 %all-to-all-done.refs_0_ = bf16[16,784,128]{2,1,0:T(8,128)(2,1)S(1)} async-done(((bf16[16,784,128]{2,1,0:T(8,128)(2,1)}), bf16[16,784,128]{2,1,0:T(8,128)(2,1)S(1)}, u32[]{:S(2)}, u32[]{:S(2)}) %all-to-all-start) | async-done | bytes 3211296 | tf_op jit(solution)/shard_map/all_to_all | solution.py:343
  57.1 19.6 %scan_grads.1 = (bf16[16,784,128]{2,1,0:T(8,128)(2,1)S(1)}, f32[8,128]{1,0:T(8,128)S(1)}) custom-call(bf16[16,784,128]{2,1,0:T(8,128)(2,1)S(1)} %all-to-all-done.refs_0_, f32[3,128]{1,0:T(4,128)S(1)} %fusion.refs_1_), custom_call_target="tpu_custom_call" | custom-call | tf_op jit(solution)/shard_map/scan_grads/pallas_call | solution.py:275
  76.7 0.0 copy-start
  76.7 1.6 %copy-done = bf16[16,784,128]{2,1,0:T(8,128)(2,1)} copy-done((bf16[16,784,128]{2,1,0:T(8,128)(2,1)}, bf16[16,784,128]{2,1,0:T(8,128)(2,1)S(1)}, u32[]{:S(2)}) %copy-start) | copy-done | bytes 3211288
  78.3 1.9 %collective-permute-start = (f32[8,128]{1,0:T(8,128)S(1)}, f32[8,128]{1,0:T(8,128)S(1)}, u32[]{:S(2)}, u32[]{:S(2)}) collective-permute-start(f32[8,128]{1,0:T(8,128)S(1)} %get-tuple-element.14), channel_id=1, source_target_pairs={{0,16},{16,0},{32,48},{48,32},{64,80},{80,64},{96,112},{112,96},{1... | collective-permute-start | bytes 12296 | tf_op jit(solution)/shard_map/ppermute | solution.py:350
  80.2 5.1 %collective-permute-done = f32[8,128]{1,0:T(8,128)S(1)} collective-permute-done((f32[8,128]{1,0:T(8,128)S(1)}, f32[8,128]{1,0:T(8,128)S(1)}, u32[]{:S(2)}, u32[]{:S(2)}) %collective-permute-start) | collective-permute-done | bytes 4128 | tf_op jit(solution)/shard_map/ppermute | solution.py:350
  85.3 4.0 %all-to-all-start.1 = ((bf16[16,784,128]{2,1,0:T(8,128)(2,1)}), bf16[16,784,128]{2,1,0:T(8,128)(2,1)S(1)}, u32[]{:S(2)}, u32[]{:S(2)}) async-start(bf16[16,784,128]{2,1,0:T(8,128)(2,1)} %copy-done), calls=%async_computation.1 | async-start | bytes 6422528 | tf_op jit(solution)/shard_map/all_to_all | solution.py:343
  89.3 32.8 %psum.7 = f32[8,128]{1,0:T(8,128)S(1)} all-reduce(f32[8,128]{1,0:T(8,128)S(1)} %add.7), channel_id=1, replica_groups={{0,32,64,96,128,160,192,224,256,288,320,352,384,416,448,480},{16,48,80,..., use_global_device_ids=true, to_apply=%region_0.1 | all-reduce | flops 1024 | bytes 8192 | tf_op jit(solution)/shard_map/psum | solution.py:357
  122.2 0.6 slice_multiply_fusion
  122.7 10.4 %all-to-all-done.1.refs_0_ = bf16[16,784,128]{2,1,0:T(8,128)(2,1)S(1)} async-done(((bf16[16,784,128]{2,1,0:T(8,128)(2,1)}), bf16[16,784,128]{2,1,0:T(8,128)(2,1)S(1)}, u32[]{:S(2)}, u32[]{:S(2)}) %all-to-all-start.1) | async-done | bytes 3211296 | tf_op jit(solution)/shard_map/all_to_all | solution.py:343
  133.1 1.7 %unpack.1 = (bf16[128,4096]{1,0:T(8,128)(2,1)}, bf16[64,128]{1,0:T(8,128)(2,1)}, bf16[128,128]{1,0:T(8,128)(2,1)}, bf16[128,128]{1,0:T(8,128)(2,1)}) custom-call(bf16[16,784,128]{2,1,0:T(8,128)(2,1)S(1)} %all-to-all-done.1.refs_0_), custom_call_target="tpu_custom_call" | custom-call | tf_op jit(solution)/shard_map/unpack/pallas_call | solution.py:330
  (1 shorter events, 0.0 us)
Async XLA Ops:
  3.8 9.6 %copy-start.1 = (f32[4]{0:T(128)S(1)}, f32[4]{0:T(128)}, u32[]{:S(2)}) copy-start(f32[4]{0:T(128)} %param.15) | copy-start | bytes 52
  3.8 9.6 %copy-start.2 = (f32[4]{0:T(128)S(1)}, f32[4]{0:T(128)}, u32[]{:S(2)}) copy-start(f32[4]{0:T(128)} %param.14) | copy-start | bytes 52
  3.8 9.6 %copy-start.3 = (f32[4]{0:T(128)S(1)}, f32[4]{0:T(128)}, u32[]{:S(2)}) copy-start(f32[4]{0:T(128)} %param.13) | copy-start | bytes 52
  3.8 53.3 %all-to-all-start = ((bf16[16,784,128]{2,1,0:T(8,128)(2,1)}), bf16[16,784,128]{2,1,0:T(8,128)(2,1)S(1)}, u32[]{:S(2)}, u32[]{:S(2)}) async-start(bf16[16,784,128]{2,1,0:T(8,128)(2,1)} %pack.1), calls=%async_computation | async-start | bytes 6422528 | tf_op jit(solution)/shard_map/all_to_all | solution.py:343
  76.7 1.6 %copy-start = (bf16[16,784,128]{2,1,0:T(8,128)(2,1)}, bf16[16,784,128]{2,1,0:T(8,128)(2,1)S(1)}, u32[]{:S(2)}) copy-start(bf16[16,784,128]{2,1,0:T(8,128)(2,1)S(1)} %get-tuple-element.15) | copy-start | bytes 9633796
  78.3 7.0 %collective-permute-start = (f32[8,128]{1,0:T(8,128)S(1)}, f32[8,128]{1,0:T(8,128)S(1)}, u32[]{:S(2)}, u32[]{:S(2)}) collective-permute-start(f32[8,128]{1,0:T(8,128)S(1)} %get-tuple-element.14), channel_id=1, source_target_pairs={{0,16},{16,0},{32,48},{48,32},{64,80},{80,64},{96,112},{112,96},{1... | collective-permute-start | bytes 12296 | tf_op jit(solution)/shard_map/ppermute | solution.py:350
  85.3 47.8 %all-to-all-start.1 = ((bf16[16,784,128]{2,1,0:T(8,128)(2,1)}), bf16[16,784,128]{2,1,0:T(8,128)(2,1)S(1)}, u32[]{:S(2)}, u32[]{:S(2)}) async-start(bf16[16,784,128]{2,1,0:T(8,128)(2,1)} %copy-done), calls=%async_computation.1 | async-start | bytes 6422528 | tf_op jit(solution)/shard_map/all_to_all | solution.py:343

commit v2 on v1

v2 whole, which is shorter than its diff:
```python
import jax
import jax.numpy as jnp
from jax import lax
from jax.experimental import pallas as pl
from jax.experimental.pallas import tpu as pltpu
from jax.sharding import PartitionSpec as P

CHUNK = 128
LANES = 128
HDIM = 64
NSTATE = 128
ROWS = 8
MIB = 1 << 20
PACK_STEPS = 2
HALVES = 2
PER_TILE = LANES // (2 * ROWS)
UNROLL = 4
STATES_VMEM = 24
LOCAL_VMEM = 24
FINISH_VMEM = 24

f32 = jnp.float32
bf16 = jnp.bfloat16


def mm(a, b):
    return jnp.dot(a, b, preferred_element_type=f32)


def mm_nt(a, b):
    return lax.dot_general(a, b, (((1,), (1,)), ((), ())), preferred_element_type=f32)


def mm_tn(a, b):
    return lax.dot_general(a, b, (((0,), (0,)), ((), ())), preferred_element_type=f32)


def split2(v):
    high = v.astype(bf16)
    return high, (v - high.astype(f32)).astype(bf16)


def split3(v):
    high = v.astype(bf16).astype(f32)
    rest = v - high
    mid = rest.astype(bf16).astype(f32)
    return high, mid, rest - mid


def iota(shape, axis):
    return lax.broadcasted_iota(jnp.int32, shape, axis)


def one_hot(cond):
    return jnp.where(cond, 1.0, 0.0)


def mm_exact(v, ones):
    parts = mm(jnp.concatenate(split3(v), axis=0).astype(bf16), ones.astype(bf16))
    n = v.shape[0]
    return parts[:n] + parts[n : 2 * n] + parts[2 * n :]


def pack_kernel(groups, xa_ref, xb_ref, ga_ref, gb_ref, b_ref, c_ref, s_ref, out_ref):
    some = s_ref.shape[0] // (HALVES * groups)
    narrow = some * HDIM
    width = HALVES * narrow
    tall = 2 * width + 2 * CHUNK
    for n in range(out_ref.shape[0]):
        row = 0
        for ref in (xa_ref, xb_ref, ga_ref, gb_ref):
            for i in range(narrow // LANES):
                start = n * narrow + i * LANES
                out_ref[n, row : row + CHUNK] = ref[:, start : start + LANES]
                row += CHUNK
        out_ref[n, 2 * width : 2 * width + CHUNK] = b_ref[...]
        out_ref[n, 2 * width + CHUNK : tall] = c_ref[...]
        group = pl.program_id(0) * out_ref.shape[0] + n
        out_ref[n, tall:] = mm(head_pick(16, s_ref.shape[0], group, some, groups), s_ref[...]).astype(bf16)


def head_pick(rows, heads, group, some, groups):
    shape = (rows, heads)
    row, head = iota(shape, 0), iota(shape, 1)
    owner = group + groups * (row // some)
    return one_hot((head == owner * some + row % some) & (row < HALVES * some)).astype(bf16)


def pack(x, g, b, c, s, groups):
    narrow = s.shape[0] // (HALVES * groups) * HDIM
    rows = 2 * HALVES * narrow + 2 * CHUNK + 16
    part = groups // PACK_STEPS
    whole = lambda a: pl.BlockSpec(a.shape, lambda j: (0, 0))
    first = pl.BlockSpec((CHUNK, part * narrow), lambda j: (0, j))
    second = pl.BlockSpec((CHUNK, part * narrow), lambda j: (0, PACK_STEPS + j))
    return pl.pallas_call(
        lambda *refs: pack_kernel(groups, *refs),
        grid=(PACK_STEPS,),
        in_specs=[first, second, first, second, whole(b), whole(c), whole(s)],
        out_specs=pl.BlockSpec((part, rows, LANES), lambda j: (j, 0, 0)),
        out_shape=jax.ShapeDtypeStruct((groups, rows, LANES), bf16),
        compiler_params=pltpu.CompilerParams(vmem_limit_bytes=56 * MIB),
        name="pack",
    )(x, x, g, g, b, c, s)


class Layout:
    def __init__(self, heads, chunks):
        self.heads, self.chunks, self.width = heads, chunks, heads * HDIM
        self.blocks = self.width // LANES
        self.at_b = 2 * self.width
        self.at_c = self.at_b + CHUNK
        self.at_s = self.at_c + CHUNK
        self.body = self.width + 4 * CHUNK
        self.flat = (chunks * ROWS, LANES)
        self.cube = (chunks, ROWS, LANES)
        self.wide = (chunks, CHUNK, self.width)

    def spread(self):
        shape = (ROWS, self.width)
        return one_hot(iota(shape, 1) // HDIM == iota(shape, 0))

    def to_lanes(self, tile):
        return jnp.sum(jnp.concatenate([tile] * self.blocks, axis=1) * self.spread(), axis=0, keepdims=True)

    def columns(self, ref, k, start):
        return jnp.concatenate(
            [ref[k, start + i * CHUNK : start + (i + 1) * CHUNK] for i in range(self.blocks)], axis=1
        )

    def keys(self, ref, k):
        return ref[k, self.at_b : self.at_b + CHUNK], ref[k, self.at_c : self.at_c + CHUNK]

    def by_head(self):
        shape = (16, self.width)
        return one_hot(iota(shape, 1) // HDIM == iota(shape, 0)).astype(bf16)


SQUARE = (LANES, LANES)
TILE = (ROWS, LANES)


def along(*parts):
    return jnp.concatenate(parts, axis=1)


def under(*parts):
    return jnp.concatenate(parts, axis=0)


def grouped(chunks, step, carry, reverse=False):
    def turn(i, carry):
        for n in range(UNROLL):
            k = i * UNROLL + n
            carry = step(chunks - 1 - k if reverse else k, carry)
        return carry

    return lax.fori_loop(0, chunks // UNROLL, turn, carry)


def states_kernel(lay, in_ref, given_ref, flag_ref,
                  gh_ref, gl_ref, xh_ref, xl_ref, hs_ref, dl_ref, wide_ref,
                  step_ref, slope_ref, decay_ref, total_ref, par_ref, skip_ref, send_ref,
                  alpha_ref, gamma_ref, pick_ref):
    chunks, width = lay.chunks, lay.width

    for i in range(3):
        row = jnp.broadcast_to(given_ref[i : i + 1], TILE)
        mine = jnp.where(iota(TILE, 1) == iota(TILE, 0), row, 0.0)
        par_ref[i] = jnp.broadcast_to(jnp.sum(mine, axis=1, keepdims=True), TILE)

    raw = in_ref[:, lay.at_s : lay.at_s + 16].astype(f32)[:, :ROWS]
    z = raw + par_ref[2][None]
    step = jnp.maximum(z, 0.0) + jnp.log1p(jnp.exp(-jnp.abs(z)))
    decay = -jnp.exp(par_ref[0])[None] * step
    step_ref[...], slope_ref[...], decay_ref[...] = step, jnp.exp(z - step), decay
    upto = one_hot(iota(SQUARE, 0) <= iota(SQUARE, 1))
    level = mm_exact(decay.reshape(lay.flat), upto)
    total_ref[...] = jnp.exp(jnp.broadcast_to(level[:, LANES - 1 :], lay.flat)).reshape(lay.cube)
    for ref, v in ((alpha_ref, jnp.exp(level)), (gamma_ref, jnp.exp(-level) * step.reshape(lay.flat))):
        high = v.astype(bf16).astype(f32)
        parts = jnp.concatenate([high.reshape(lay.cube), (v - high).reshape(lay.cube)], axis=1)
        parts = parts.reshape(chunks // PER_TILE, LANES, LANES)
        for i in range(chunks // PER_TILE):
            ref[i] = parts[i].T.astype(bf16)

    in_tile = (LANES, width)
    at_head = iota(in_tile, 1) // HDIM == iota(in_tile, 0) % ROWS
    eye = one_hot(iota(SQUARE, 0) == iota(SQUARE, 1)).astype(bf16)
    for i in range(PER_TILE):
        pick_ref[i] = one_hot(at_head & (iota(in_tile, 0) // (2 * ROWS) == i)).astype(bf16)

    def expand(ref, k):
        return mm(ref[k // PER_TILE], pick_ref[k % PER_TILE])

    def flip(v):
        return mm_nt(eye, v).astype(bf16)

    skip_ref[...] = jnp.zeros_like(skip_ref)

    def forward(k, carry):
        state, early, prefix = carry
        x = lay.columns(in_ref, k, 0).astype(f32)
        g = lay.columns(in_ref, k, width).astype(f32)
        gt_high, gt_low = split2(expand(alpha_ref, k) * g)
        wide = expand(gamma_ref, k)
        xt_high, xt_low = split2(wide * x)
        wide_ref[k] = wide
        gh_ref[k], gl_ref[k], xh_ref[k], xl_ref[k] = gt_high, gt_low, xt_high, xt_low
        skip_ref[...] += jnp.sum((x * g).reshape(CHUNK // ROWS, ROWS, width), axis=0)
        hs_ref[k] = state
        keys_in, keys_out = lay.keys(in_ref, k)
        keys_in, keys_out = flip(keys_in), flip(keys_out)
        back = mm(along(keys_out, keys_out), under(gt_high, gt_low))
        dl_ref[k] = back
        total = lay.to_lanes(total_ref[k])
        state = total * (state + mm(along(keys_in, keys_in), under(xt_high, xt_low)))
        return state, early + prefix * back, prefix * total

    nothing = jnp.zeros((NSTATE, width), f32)
    state, early, _ = grouped(chunks, forward, (nothing, nothing, jnp.ones((1, width), f32)))
    send_ref[...] = jnp.where(flag_ref[0] == 0, state, early)


def scan_states(received, params, flag, lay):
    vmem = pl.BlockSpec(memory_space=pltpu.VMEM)
    shape = jax.ShapeDtypeStruct
    wide, cube = lay.wide, lay.cube
    tiles = pltpu.VMEM((lay.chunks // PER_TILE, LANES, LANES), bf16)
    return pl.pallas_call(
        lambda *refs: states_kernel(lay, *refs),
        in_specs=[vmem, vmem, pl.BlockSpec(memory_space=pltpu.SMEM)],
        out_specs=[vmem] * 14,
        out_shape=[shape(wide, bf16)] * 4 + [shape(wide, f32)] * 3 + [shape(cube, f32)] * 4
        + [shape((3, ROWS, LANES), f32), shape((ROWS, lay.width), f32), shape((NSTATE, lay.width), f32)],
        scratch_shapes=[tiles, tiles, pltpu.VMEM((PER_TILE, LANES, lay.width), bf16)],
        compiler_params=pltpu.CompilerParams(vmem_limit_bytes=STATES_VMEM * MIB),
        name="scan_states",
    )(received, params, flag)


def local_kernel(lay, in_ref, gh_ref, gl_ref, xh_ref, xl_ref, hs_ref, dl_ref, wide_ref, total_ref, par_ref,
                 gx_ref, din_ref, dout_ref, r_ref, c_ref):
    width = lay.width
    gather = lay.by_head()
    skip_wide = lay.to_lanes(par_ref[1])
    causal = iota(SQUARE, 0) >= iota(SQUARE, 1)

    def backward(k, dstate):
        through = lay.to_lanes(total_ref[k]) * dstate
        dh, dl = split2(through)
        hh, hl = split2(hs_ref[k])
        gh, gl, xh, xl = gh_ref[k], gl_ref[k], xh_ref[k], xl_ref[k]
        keys_in, keys_out = lay.keys(in_ref, k)

        sh, sl = split2(jnp.where(causal, mm_nt(keys_out, keys_in), 0.0))
        th, tl = split2(jnp.where(causal.T, mm_nt(keys_in, keys_out), 0.0))
        out_h, in_h = along(sh, keys_out), along(th, keys_in)
        y = mm(out_h, under(xh, hh)) + mm(out_h, under(xl, hl)) + mm(sl, xh)
        dx = mm(in_h, under(gh, dh)) + mm(in_h, under(gl, dl)) + mm(tl, gh)

        ds = mm_nt(gh, xh) + mm_nt(gh, xl) + mm_nt(gl, xh)
        ds = jnp.where(causal, ds, 0.0)
        ph, plow = split2(ds)
        qh, qlow = split2(ds.T)
        dout_ref[k] = mm(along(ph, plow), under(keys_in, keys_in)) + mm_nt(gh, hh) + mm_nt(gh, hl) + mm_nt(gl, hh)
        din_ref[k] = mm(along(qh, qlow), under(keys_out, keys_out)) + mm_nt(xh, dh) + mm_nt(xh, dl) + mm_nt(xl, dh)

        gt = gh.astype(f32) + gl.astype(f32)
        xt = xh.astype(f32) + xl.astype(f32)
        high, low = split2(under(gt * y, xt * dx))
        sums = mm_nt(gather, high) + mm_nt(gather, low)
        r_ref[k], c_ref[k] = sums[:ROWS, :CHUNK], sums[:ROWS, CHUNK:]
        gx_ref[k] = wide_ref[k] * dx + skip_wide * lay.columns(in_ref, k, width).astype(f32)
        return dl_ref[k] + through

    grouped(lay.chunks, backward, jnp.zeros((NSTATE, width), f32), reverse=True)


def scan_local(received, own, lay):
    gh, gl, xh, xl, hs, dl, wide, _, _, _, total, par, _, _ = own
    vmem = pl.BlockSpec(memory_space=pltpu.VMEM)
    shape = jax.ShapeDtypeStruct
    keys = (lay.chunks, CHUNK, NSTATE)
    return pl.pallas_call(
        lambda *refs: local_kernel(lay, *refs),
        in_specs=[vmem] * 10,
        out_specs=[vmem] * 5,
        out_shape=[shape(lay.wide, f32), shape(keys, f32), shape(keys, f32), shape(lay.cube, f32), shape(lay.cube, f32)],
        compiler_params=pltpu.CompilerParams(vmem_limit_bytes=LOCAL_VMEM * MIB),
        name="scan_local",
    )(received, gh, gl, xh, xl, hs, dl, wide, total, par)


def finish_kernel(lay, in_ref, gh_ref, gl_ref, xh_ref, xl_ref, wide_ref,
                  step_ref, slope_ref, decay_ref, total_ref, par_ref, skip_ref, sent_ref, came_ref,
                  gx_ref, din_ref, dout_ref, r_ref, c_ref, flag_ref,
                  out_ref, pout_ref, reach_ref, col_ref, row_ref):
    chunks, width, cube = lay.chunks, lay.width, lay.cube
    gather = lay.by_head()
    first = flag_ref[0] == 0

    run = jnp.ones(TILE, f32)
    before = []
    for k in range(chunks):
        before.append(run)
        run = run * total_ref[k]
    run = jnp.ones(TILE, f32)
    for k in reversed(range(chunks)):
        run = run * total_ref[k]
        reach_ref[k] = jnp.where(first, run, before[k])

    def store(k, grad_x, d_in, d_out):
        grad_x = grad_x.astype(bf16)
        for j in range(lay.blocks):
            out_ref[k, j * CHUNK : (j + 1) * CHUNK] = grad_x[:, j * LANES : (j + 1) * LANES]
        for j, part in enumerate(split2(d_in) + split2(d_out)):
            out_ref[k, width + j * CHUNK : width + (j + 1) * CHUNK] = part

    def correct(k, keys, high, low):
        uh, ul = split2(lay.to_lanes(reach_ref[k]) * came_ref[...])
        more = mm(along(keys, keys), under(uh, ul))
        d_keys = mm_nt(high, uh) + mm_nt(high, ul) + mm_nt(low, uh)
        ph, plow = split2((high.astype(f32) + low.astype(f32)) * more)
        return more, d_keys, (mm_nt(gather, ph) + mm_nt(gather, plow))[:ROWS]

    @pl.when(first)
    def _():
        def one(k, carry):
            more, d_keys, sums = correct(k, lay.keys(in_ref, k)[0], xh_ref[k], xl_ref[k])
            store(k, gx_ref[k] + wide_ref[k] * more, din_ref[k] + d_keys, dout_ref[k])
            row_ref[k], col_ref[k] = r_ref[k], c_ref[k] + sums
            return carry

        grouped(chunks, one, 0)

    @pl.when(jnp.logical_not(first))
    def _():
        def one(k, carry):
            _, d_keys, sums = correct(k, lay.keys(in_ref, k)[1], gh_ref[k], gl_ref[k])
            store(k, gx_ref[k], din_ref[k], dout_ref[k] + d_keys)
            row_ref[k], col_ref[k] = r_ref[k] + sums, c_ref[k]
            return carry

        grouped(chunks, one, 0)

    spread = lay.spread()
    per_head = lambda row: jnp.sum(spread * row, axis=1, keepdims=True)
    cross = per_head(jnp.sum(sent_ref[...] * came_ref[...], axis=0, keepdims=True))
    later = jnp.broadcast_to(jnp.where(first, cross, 0.0), TILE)
    col = col_ref[...]
    since = one_hot(iota(SQUARE, 0) >= iota(SQUARE, 1))
    suffix = mm_exact((row_ref[...] - col).reshape(lay.flat), since).reshape(cube)
    sums = jnp.broadcast_to(suffix[:, :, :1], cube)
    carried = [None] * chunks
    for k in reversed(range(chunks)):
        carried[k] = later[None]
        later = later + sums[k]
    d_decay = suffix + jnp.concatenate(carried, axis=0)
    rate = -jnp.exp(par_ref[0])
    d_raw = slope_ref[...] * (col / step_ref[...] + rate[None] * d_decay)
    out_ref[:, lay.body :] = jnp.concatenate([d_raw, jnp.zeros(cube, f32)], axis=1).astype(bf16)

    result = jnp.zeros(TILE, f32)
    per = (
        jnp.sum(jnp.sum(d_decay * decay_ref[...], axis=0), axis=1, keepdims=True),
        per_head(jnp.sum(skip_ref[...], axis=0, keepdims=True)),
        jnp.sum(jnp.sum(d_raw, axis=0), axis=1, keepdims=True),
    )
    for i, v in enumerate(per):
        row = jnp.sum(jnp.where(iota(TILE, 0) == iota(TILE, 1), jnp.broadcast_to(v, TILE), 0.0), axis=0, keepdims=True)
        result = jnp.where(iota(TILE, 0) == i, jnp.broadcast_to(row, TILE), result)
    pout_ref[...] = result


def scan_finish(received, own, local, came, flag, lay):
    gh, gl, xh, xl, _, _, wide, step, slope, decay, total, par, skip, sent = own
    vmem = pl.BlockSpec(memory_space=pltpu.VMEM)
    shape = jax.ShapeDtypeStruct
    small = pltpu.VMEM(lay.cube, f32)
    return pl.pallas_call(
        lambda *refs: finish_kernel(lay, *refs),
        in_specs=[vmem] * 19 + [pl.BlockSpec(memory_space=pltpu.SMEM)],
        out_specs=[vmem] * 2,
        out_shape=[shape((lay.chunks, lay.body + 16, LANES), bf16), shape(TILE, f32)],
        scratch_shapes=[small, small, small],
        compiler_params=pltpu.CompilerParams(vmem_limit_bytes=FINISH_VMEM * MIB),
        name="scan_finish",
    )(received, gh, gl, xh, xl, wide, step, slope, decay, total, par, skip, sent, came, *local, flag)


def unpack_kernel(lay, in_ref, x_ref, s_ref, b_ref, c_ref):
    groups, width = in_ref.shape[0], lay.width
    narrow = width // HALVES
    some = lay.heads // HALVES
    for n in range(groups):
        for half in range(HALVES):
            for i in range(narrow // LANES):
                start = (half * groups + n) * narrow + i * LANES
                row = half * narrow + i * CHUNK
                x_ref[:, start : start + LANES] = in_ref[n, row : row + CHUNK]
    part = lambda n, j: in_ref[n, width + j * CHUNK : width + (j + 1) * CHUNK].astype(f32)
    every = range(groups)
    b_ref[...] = sum(part(n, 0) + part(n, 1) for n in every).astype(bf16)
    c_ref[...] = sum(part(n, 2) + part(n, 3) for n in every).astype(bf16)
    picks = [head_pick(16, s_ref.shape[0], n, some, groups) for n in every]
    s_ref[...] = sum(mm_tn(picks[n], in_ref[n, lay.body :]) for n in every).astype(bf16)


def unpack(received, lay):
    groups = received.shape[0]
    shapes = [(CHUNK, groups * lay.width), (groups * lay.heads, CHUNK), (CHUNK, NSTATE), (CHUNK, NSTATE)]
    vmem = pl.BlockSpec(memory_space=pltpu.VMEM)
    return pl.pallas_call(
        lambda *refs: unpack_kernel(lay, *refs),
        in_specs=[vmem],
        out_specs=[vmem] * 4,
        out_shape=[jax.ShapeDtypeStruct(s, bf16) for s in shapes],
        compiler_params=pltpu.CompilerParams(vmem_limit_bytes=24 * MIB),
        name="unpack",
    )(received)


def exchange(v):
    groups = v.shape[0]
    halves = [[half * groups + i for i in range(groups)] for half in range(HALVES)]
    return lax.all_to_all(v, "seq", split_axis=0, concat_axis=0, tiled=True, axis_index_groups=halves)


def from_partner(v):
    groups = lax.axis_size("seq") // HALVES
    return lax.ppermute(v, "seq", [(i, (i + groups) % (2 * groups)) for i in range(2 * groups)])


def pair_sum(v):
    replicas = lax.axis_size("dp")
    if replicas == 1:
        return v
    return v + lax.ppermute(v, "dp", [(i, i ^ 1) for i in range(replicas)])


def line_sum(v):
    half = lax.axis_size("dp") // 2
    if half <= 1:
        return v
    return lax.psum(v, "dp", axis_index_groups=[[2 * i + bit for i in range(half)] for bit in range(2)])


def shards(inputs, raw_step, write_keys, read_keys, grad_out, decay_log, skip_gain, step_bias):
    groups = lax.axis_size("seq") // HALVES
    some = decay_log.shape[0]
    lay = Layout(HALVES * some, groups)
    half = lax.axis_index("seq") // groups
    flag = half.astype(jnp.int32)[None]
    send = pack(inputs[0], grad_out[0], write_keys[0], read_keys[0], raw_step[0].T, groups)
    mine = jnp.stack([decay_log, skip_gain, step_bias])
    send, mine = lax.optimization_barrier((send, mine))
    other = from_partner(mine)
    first = half == 0
    params = jnp.concatenate([jnp.where(first, mine, other), jnp.where(first, other, mine)], axis=1)
    params = jnp.pad(params, ((0, 0), (0, LANES - lay.heads)))

    received = exchange(send)
    own = scan_states(received, params, flag, lay)
    came = from_partner(own[-1])
    local = scan_local(received, own, lay)
    back, per_head = scan_finish(received, own, local, came, flag, lay)
    grad_x, grad_step, grad_write, grad_read = unpack(exchange(back), lay)
    per_head = per_head + from_partner(per_head)
    totals = line_sum(pair_sum(per_head))[:3] / lax.axis_size("dp")
    totals = jnp.where(first, totals[:, :some], totals[:, some : 2 * some])
    return grad_x[None], grad_step.T[None], grad_write[None], grad_read[None], totals


def solution(mesh):
    rows = P("dp", "seq", None)
    heads = P("seq")
    return jax.shard_map(
        shards,
        mesh=mesh,
        in_specs=(rows,) * 5 + (heads,) * 3,
        out_specs=(rows,) * 4 + (P(None, "seq"),),
        check_vma=False,
    )
```

time: 135 us -> 116 us (0.86)
  waiting for transfers between devices: 59.1 us -> 37.1 us
  starting transfers between devices: 15.5 us -> 23.6 us
  Pallas kernels: 24.4 us -> 17.9 us
    all_to_all x2, waiting for transfers between devices: 54 us -> 26.2 us  [exchange(): lax.all_to_all(v, 'seq', split_axis=0, concat_axis=0, tiled=True, axis_in...]
    ppermute x0 -> x3, starting transfers between devices: none -> 7.28 us  [from_partner(): lax.ppermute(v, 'seq', [(i, (i + groups) % (2 * groups)) for i in range(2...]
    pallas_call x3 -> x5, Pallas kernels: 24.4 us -> 17.9 us  [the longest x1 7.49 us: scan_local(): pl.pallas_call(lambda *refs: local_kernel(lay, *refs), in_specs=[vmem] *...]
    ppermute x0 -> x3, waiting for transfers between devices: none -> 5.88 us  [from_partner(): lax.ppermute(v, 'seq', [(i, (i + groups) % (2 * groups)) for i in range(2...]
  transfers between devices with their start and end apart: 3 -> 6, of which waited for: 3 -> 5; matrix products, arithmetic and copies ran while one was open for 0% -> 1% of each run, Pallas kernels for 0% -> 6%
where the time goes in v2:
time: 116 us; the launch traced here: 115 us
  waiting for transfers between devices  37.1 us (32%)
  blocking collectives  33.2 us (29%)
  starting transfers between devices  23.6 us (20%)
  Pallas kernels  17.9 us (15%)
  other arithmetic  1.44 us (1%)
  local copies, waits for them, and re-layouts  1.34 us (1%)
    psum x1, blocking collectives, line_sum(): lax.psum(v, 'dp', axis_index_groups=[[2 * i + bit for i in range(half)] f...  33.2 us
    all_to_all x2, waiting for transfers between devices, exchange(): lax.all_to_all(v, 'seq', split_axis=0, concat_axis=0, tiled=True, axis_in...  26.2 us
    all_to_all x2, starting transfers between devices, exchange(): lax.all_to_all(v, 'seq', split_axis=0, concat_axis=0, tiled=True, axis_in...  14.4 us
    pallas_call x1, Pallas kernels, scan_local(): pl.pallas_call(lambda *refs: local_kernel(lay, *refs), in_specs=[vmem] *...  7.49 us
    ppermute x3, starting transfers between devices, from_partner(): lax.ppermute(v, 'seq', [(i, (i + groups) % (2 * groups)) for i in range(2...  7.28 us
    ppermute x3, waiting for transfers between devices, from_partner(): lax.ppermute(v, 'seq', [(i, (i + groups) % (2 * groups)) for i in range(2...  5.88 us
    ppermute x1, waiting for transfers between devices, pair_sum(): return v + lax.ppermute(v, 'dp', [(i, i ^ 1) for i in range(replicas)])  5.08 us
    pallas_call x1, Pallas kernels, scan_states(): pl.pallas_call(lambda *refs: states_kernel(lay, *refs), in_specs=[vmem, v...  3.23 us
  transfers between devices with their start and end apart: 6, of which 5 were waited for; matrix products, arithmetic and copies ran while one was open for 1% of the time, Pallas kernels for 6%

profile of v2, /device:TPU:2, one launch (start us, length us, event | category | flops | bytes accessed | tf_op | source)
XLA Modules:
  0.0 115.3 jit_solution(7212629037482070234)
XLA Ops:
  0.6 0.7 pad_maximum_fusion
  1.3 3.0 %pack.1 = bf16[8,1296,128]{2,1,0:T(8,128)(2,1)} custom-call(bf16[128,4096]{1,0:T(8,128)(2,1)} %bitcast.17, bf16[128,4096]{1,0:T(8,128)(2,1)} %bitcast.18, bf16[128,4096]{1,0:T(8,128)(2,1)} %bitcast.19, bf16[128,4096]{1,0:T(8,128)(2,1)} %bitcast.20, bf16[128,128]{1,0:T(8,128)(2,1)} %bitcast.21, bf16[128,128]{1,0:T(8,128)(2,1)} %bitcast.22, ...), custom_call_target="tpu_custom_call" | custom-call | tf_op jit(solution)/shard_map/pack/pallas_call | solution.py:96
  4.3 9.4 %all-to-all-start = ((bf16[8,1296,128]{2,1,0:T(8,128)(2,1)}), bf16[8,1296,128]{2,1,0:T(8,128)(2,1)S(1)}, u32[]{:S(2)}, u32[]{:S(2)}) async-start(bf16[8,1296,128]{2,1,0:T(8,128)(2,1)} %pack.1), calls=%async_computation | async-start | bytes 5308416 | tf_op jit(solution)/shard_map/all_to_all | solution.py:427
  13.8 1.9 %collective-permute-start = (f32[3,4]{1,0:T(4,128)S(1)}, f32[3,4]{1,0:T(4,128)S(1)}, u32[]{:S(2)}, u32[]{:S(2)}) collective-permute-start(f32[3,4]{1,0:T(4,128)S(1)} %pad_maximum_fusion), channel_id=1, source_target_pairs={{0,8},{1,9},{2,10},{3,11},{4,12},{5,13},{6,14},{7,15},{8,0},{9,1},... | collective-permute-start | bytes 152 | tf_op jit(solution)/shard_map/ppermute | solution.py:432
  15.7 3.5 %collective-permute-done = f32[3,4]{1,0:T(4,128)S(1)} collective-permute-done((f32[3,4]{1,0:T(4,128)S(1)}, f32[3,4]{1,0:T(4,128)S(1)}, u32[]{:S(2)}, u32[]{:S(2)}) %collective-permute-start) | collective-permute-done | bytes 80 | tf_op jit(solution)/shard_map/ppermute | solution.py:432
  19.2 0.1 select_maximum_fusion.refs_1_
  19.3 26.2 %all-to-all-done.refs_0_ = bf16[8,1296,128]{2,1,0:T(8,128)(2,1)S(1)} async-done(((bf16[8,1296,128]{2,1,0:T(8,128)(2,1)}), bf16[8,1296,128]{2,1,0:T(8,128)(2,1)S(1)}, u32[]{:S(2)}, u32[]{:S(2)}) %all-to-all-start) | async-done | bytes 2654240 | tf_op jit(solution)/shard_map/all_to_all | solution.py:427
  45.5 3.2 %scan_states.1 = (bf16[8,128,512]{2,1,0:T(8,128)(2,1)S(1)}, bf16[8,128,512]{2,1,0:T(8,128)(2,1)S(1)}, bf16[8,128,512]{2,1,0:T(8,128)(2,1)S(1)}, bf16[8,128,512]{...) custom-call(bf16[8,1296,128]{2,1,0:T(8,128)(2,1)S(1)} %all-to-all-do, ...), custom_call_target="tpu_custom_call" | custom-call | tf_op jit(solution)/shard_map/scan_states/pallas_call | solution.py:230
  48.7 1.9 %collective-permute-start.1 = (f32[128,512]{1,0:T(8,128)S(1)}, f32[128,512]{1,0:T(8,128)S(1)}, u32[]{:S(2)}, u32[]{:S(2)}) collective-permute-start(f32[128,512]{1,0:T(8,128)S(1)} %get-tuple-element.45.refs_12_), channel_id=1, source_target_pairs={{0,8},{1,9},{2,10},{3,11},{4,12},{5,13},{6,14},{7,15},{8,0},{9,1},... | collective-permute-start | bytes 786440 | tf_op jit(solution)/shard_map/ppermute | solution.py:432
  50.7 7.5 %scan_local.1 = (f32[8,128,512]{2,1,0:T(8,128)S(1)}, f32[8,128,128]{2,1,0:T(8,128)S(1)}, f32[8,128,128]{2,1,0:T(8,128)S(1)}, f32[8,8,128]{2,1,0:T(8,128)S(1)}, f32[8,8,128]{2,1,0:T(8,128)S(1)}) custom-call(bf16[8,1296,128]{2,1,0:T(8,128)(2,1)S(1)} %all-to-all-done.refs_0_, bf16[8,128,512]{2,1,0:T(8,128)(2,1)S(1)} %get-tuple-element.34.refs_1_, ...), custom_call_target="tpu_custom_call" | custom-call | tf_op jit(solution)/shard_map/scan_local/pallas_call | solution.py:285
  58.2 0.3 collective-permute-done.1.refs_13_
  58.5 2.9 %scan_finish.1 = (bf16[8,1040,128]{2,1,0:T(8,128)(2,1)S(1)}, f32[8,128]{1,0:T(8,128)S(1)}) custom-call(bf16[8,1296,128]{2,1,0:T(8,128)(2,1)S(1)} %all-to-all-done.refs_0_, bf16[8,128,512]{2,1,0:T(8,128)(2,1)S(1)} %get-tuple-element.34.refs_1_, bf16[8,128,512]{2,1,0:T(8,128)(2,1)S(1)} %get-tuple-element.35.refs_2_, ...), custom_call_target="tpu_custom_call" | custom-call | tf_op jit(solution)/shard_map/scan_finish/pallas_call | solution.py:381
  61.4 0.0 copy-start
  61.4 1.3 %copy-done = bf16[8,1040,128]{2,1,0:T(8,128)(2,1)} copy-done((bf16[8,1040,128]{2,1,0:T(8,128)(2,1)}, bf16[8,1040,128]{2,1,0:T(8,128)(2,1)S(1)}, u32[]{:S(2)}) %copy-start) | copy-done | bytes 2129944
  62.7 5.0 %all-to-all-start.1 = ((bf16[8,1040,128]{2,1,0:T(8,128)(2,1)}), bf16[8,1040,128]{2,1,0:T(8,128)(2,1)S(1)}, u32[]{:S(2)}, u32[]{:S(2)}) async-start(bf16[8,1040,128]{2,1,0:T(8,128)(2,1)} %copy-done), calls=%async_computation.1 | async-start | bytes 4259840 | tf_op jit(solution)/shard_map/all_to_all | solution.py:427
  67.7 3.5 %collective-permute-start.2 = (f32[8,128]{1,0:T(8,128)S(1)}, f32[8,128]{1,0:T(8,128)S(1)}, u32[]{:S(2)}, u32[]{:S(2)}) collective-permute-start(f32[8,128]{1,0:T(8,128)S(1)} %get-tuple-element.58), channel_id=1, source_target_pairs={{0,8},{1,9},{2,10},{3,11},{4,12},{5,13},{6,14},{7,15},{8,0},{9,1},... | collective-permute-start | bytes 12296 | tf_op jit(solution)/shard_map/ppermute | solution.py:432
  71.2 2.0 %collective-permute-done.2 = f32[8,128]{1,0:T(8,128)S(1)} collective-permute-done((f32[8,128]{1,0:T(8,128)S(1)}, f32[8,128]{1,0:T(8,128)S(1)}, u32[]{:S(2)}, u32[]{:S(2)}) %collective-permute-start.2) | collective-permute-done | bytes 4128 | tf_op jit(solution)/shard_map/ppermute | solution.py:432
  73.2 1.9 %collective-permute-start.3 = (f32[8,128]{1,0:T(8,128)S(1)}, f32[8,128]{1,0:T(8,128)S(1)}, u32[]{:S(2)}, u32[]{:S(2)}) collective-permute-start(f32[8,128]{1,0:T(8,128)S(1)} %add.11), channel_id=1, source_target_pairs={{0,16},{16,0},{32,48},{48,32},{64,80},{80,64},{96,112},{112,96},{1... | collective-permute-start | bytes 12296 | tf_op jit(solution)/shard_map/ppermute | solution.py:439
  75.1 5.1 %collective-permute-done.3 = f32[8,128]{1,0:T(8,128)S(1)} collective-permute-done((f32[8,128]{1,0:T(8,128)S(1)}, f32[8,128]{1,0:T(8,128)S(1)}, u32[]{:S(2)}, u32[]{:S(2)}) %collective-permute-start.3) | collective-permute-done | bytes 4128 | tf_op jit(solution)/shard_map/ppermute | solution.py:439
  80.2 33.2 %psum.7 = f32[8,128]{1,0:T(8,128)S(1)} all-reduce(f32[8,128]{1,0:T(8,128)S(1)} %add.12), channel_id=1, replica_groups={{0,32,64,96,128,160,192,224,256,288,320,352,384,416,448,480},{16,48,80,..., use_global_device_ids=true, to_apply=%region_0.1 | all-reduce | flops 1024 | bytes 8192 | tf_op jit(solution)/shard_map/psum | solution.py:446
  113.4 0.7 slice_select_fusion
  114.0 0.0 all-to-all-done.1.refs_0_
  114.0 1.3 %unpack.1 = (bf16[128,4096]{1,0:T(8,128)(2,1)}, bf16[64,128]{1,0:T(8,128)(2,1)}, bf16[128,128]{1,0:T(8,128)(2,1)}, bf16[128,128]{1,0:T(8,128)(2,1)}) custom-call(bf16[8,1040,128]{2,1,0:T(8,128)(2,1)S(1)} %all-to-all-done.1.refs_0_), custom_call_target="tpu_custom_call" | custom-call | tf_op jit(solution)/shard_map/unpack/pallas_call | solution.py:414
  (4 shorter events, 0.0 us)
Async XLA Ops:
  4.3 41.2 %all-to-all-start = ((bf16[8,1296,128]{2,1,0:T(8,128)(2,1)}), bf16[8,1296,128]{2,1,0:T(8,128)(2,1)S(1)}, u32[]{:S(2)}, u32[]{:S(2)}) async-start(bf16[8,1296,128]{2,1,0:T(8,128)(2,1)} %pack.1), calls=%async_computation | async-start | bytes 5308416 | tf_op jit(solution)/shard_map/all_to_all | solution.py:427
  13.8 5.5 %collective-permute-start = (f32[3,4]{1,0:T(4,128)S(1)}, f32[3,4]{1,0:T(4,128)S(1)}, u32[]{:S(2)}, u32[]{:S(2)}) collective-permute-start(f32[3,4]{1,0:T(4,128)S(1)} %pad_maximum_fusion), channel_id=1, source_target_pairs={{0,8},{1,9},{2,10},{3,11},{4,12},{5,13},{6,14},{7,15},{8,0},{9,1},... | collective-permute-start | bytes 152 | tf_op jit(solution)/shard_map/ppermute | solution.py:432
  48.7 9.7 %collective-permute-start.1 = (f32[128,512]{1,0:T(8,128)S(1)}, f32[128,512]{1,0:T(8,128)S(1)}, u32[]{:S(2)}, u32[]{:S(2)}) collective-permute-start(f32[128,512]{1,0:T(8,128)S(1)} %get-tuple-element.45.refs_12_), channel_id=1, source_target_pairs={{0,8},{1,9},{2,10},{3,11},{4,12},{5,13},{6,14},{7,15},{8,0},{9,1},... | collective-permute-start | bytes 786440 | tf_op jit(solution)/shard_map/ppermute | solution.py:432
  61.4 1.3 %copy-start = (bf16[8,1040,128]{2,1,0:T(8,128)(2,1)}, bf16[8,1040,128]{2,1,0:T(8,128)(2,1)S(1)}, u32[]{:S(2)}) copy-start(bf16[8,1040,128]{2,1,0:T(8,128)(2,1)S(1)} %get-tuple-element.53) | copy-start | bytes 6389764
  62.7 51.3 %all-to-all-start.1 = ((bf16[8,1040,128]{2,1,0:T(8,128)(2,1)}), bf16[8,1040,128]{2,1,0:T(8,128)(2,1)S(1)}, u32[]{:S(2)}, u32[]{:S(2)}) async-start(bf16[8,1040,128]{2,1,0:T(8,128)(2,1)} %copy-done), calls=%async_computation.1 | async-start | bytes 4259840 | tf_op jit(solution)/shard_map/all_to_all | solution.py:427
  67.7 5.5 %collective-permute-start.2 = (f32[8,128]{1,0:T(8,128)S(1)}, f32[8,128]{1,0:T(8,128)S(1)}, u32[]{:S(2)}, u32[]{:S(2)}) collective-permute-start(f32[8,128]{1,0:T(8,128)S(1)} %get-tuple-element.58), channel_id=1, source_target_pairs={{0,8},{1,9},{2,10},{3,11},{4,12},{5,13},{6,14},{7,15},{8,0},{9,1},... | collective-permute-start | bytes 12296 | tf_op jit(solution)/shard_map/ppermute | solution.py:432
  73.2 7.0 %collective-permute-start.3 = (f32[8,128]{1,0:T(8,128)S(1)}, f32[8,128]{1,0:T(8,128)S(1)}, u32[]{:S(2)}, u32[]{:S(2)}) collective-permute-start(f32[8,128]{1,0:T(8,128)S(1)} %add.11), channel_id=1, source_target_pairs={{0,16},{16,0},{32,48},{48,32},{64,80},{80,64},{96,112},{112,96},{1... | collective-permute-start | bytes 12296 | tf_op jit(solution)/shard_map/ppermute | solution.py:439

commit v3 on v2

--- a/solution.py
+++ b/solution.py
@@ -292,10 +292,10 @@
     )(received, gh, gl, xh, xl, hs, dl, wide, total, par)
 
 
-def finish_kernel(lay, in_ref, gh_ref, gl_ref, xh_ref, xl_ref, wide_ref,
+def finish_kernel(lay, in_ref, gh_ref, gl_ref, xh_ref, xl_ref,
                   step_ref, slope_ref, decay_ref, total_ref, par_ref, skip_ref, sent_ref, came_ref,
-                  gx_ref, din_ref, dout_ref, r_ref, c_ref, flag_ref,
-                  out_ref, pout_ref, reach_ref, col_ref, row_ref):
+                  r_ref, c_ref, flag_ref, dstep_ref, pout_ref, uh_ref, ul_ref, more_ref,
+                  reach_ref, col_ref, row_ref):
     chunks, width, cube = lay.chunks, lay.width, lay.cube
     gather = lay.by_head()
     first = flag_ref[0] == 0
@@ -310,39 +310,28 @@
         run = run * total_ref[k]
         reach_ref[k] = jnp.where(first, run, before[k])
 
-    def store(k, grad_x, d_in, d_out):
-        grad_x = grad_x.astype(bf16)
-        for j in range(lay.blocks):
-            out_ref[k, j * CHUNK : (j + 1) * CHUNK] = grad_x[:, j * LANES : (j + 1) * LANES]
-        for j, part in enumerate(split2(d_in) + split2(d_out)):
-            out_ref[k, width + j * CHUNK : width + (j + 1) * CHUNK] = part
-
-    def correct(k, keys, high, low):
-        uh, ul = split2(lay.to_lanes(reach_ref[k]) * came_ref[...])
-        more = mm(along(keys, keys), under(uh, ul))
-        d_keys = mm_nt(high, uh) + mm_nt(high, ul) + mm_nt(low, uh)
-        ph, plow = split2((high.astype(f32) + low.astype(f32)) * more)
-        return more, d_keys, (mm_nt(gather, ph) + mm_nt(gather, plow))[:ROWS]
+    def correct(keys_at, high_ref, low_ref, old_ref, new_ref):
+        def one(k, carry):
+            uh, ul = split2(lay.to_lanes(reach_ref[k]) * came_ref[...])
+            uh_ref[k], ul_ref[k] = uh, ul
+            keys = in_ref[k, keys_at : keys_at + CHUNK]
+            more = mm(along(keys, keys), under(uh, ul))
+            more_ref[k] = more
+            ph, plow = split2((high_ref[k].astype(f32) + low_ref[k].astype(f32)) * more)
+            new_ref[k] = old_ref[k] + (mm_nt(gather, ph) + mm_nt(gather, plow))[:ROWS]
+            return carry
+
+        grouped(chunks, one, 0)
 
     @pl.when(first)
     def _():
-        def one(k, carry):
-            more, d_keys, sums = correct(k, lay.keys(in_ref, k)[0], xh_ref[k], xl_ref[k])
-            store(k, gx_ref[k] + wide_ref[k] * more, din_ref[k] + d_keys, dout_ref[k])
-            row_ref[k], col_ref[k] = r_ref[k], c_ref[k] + sums
-            return carry
-
-        grouped(chunks, one, 0)
+        row_ref[...] = r_ref[...]
+        correct(lay.at_b, xh_ref, xl_ref, c_ref, col_ref)
 
     @pl.when(jnp.logical_not(first))
     def _():
-        def one(k, carry):
-            _, d_keys, sums = correct(k, lay.keys(in_ref, k)[1], gh_ref[k], gl_ref[k])
-            store(k, gx_ref[k], din_ref[k], dout_ref[k] + d_keys)
-            row_ref[k], col_ref[k] = r_ref[k] + sums, c_ref[k]
-            return carry
-
-        grouped(chunks, one, 0)
+        col_ref[...] = c_ref[...]
+        correct(lay.at_c, gh_ref, gl_ref, r_ref, row_ref)
 
     spread = lay.spread()
     per_head = lambda row: jnp.sum(spread * row, axis=1, keepdims=True)
@@ -359,7 +348,7 @@
     d_decay = suffix + jnp.concatenate(carried, axis=0)
     rate = -jnp.exp(par_ref[0])
     d_raw = slope_ref[...] * (col / step_ref[...] + rate[None] * d_decay)
-    out_ref[:, lay.body :] = jnp.concatenate([d_raw, jnp.zeros(cube, f32)], axis=1).astype(bf16)
+    dstep_ref[...] = jnp.concatenate([d_raw, jnp.zeros(cube, f32)], axis=1).astype(bf16)
 
     result = jnp.zeros(TILE, f32)
     per = (
@@ -373,20 +362,70 @@
     pout_ref[...] = result
 
 
-def scan_finish(received, own, local, came, flag, lay):
-    gh, gl, xh, xl, _, _, wide, step, slope, decay, total, par, skip, sent = own
+def scan_finish(received, own, r, c, came, flag, lay):
+    gh, gl, xh, xl, _, _, _, step, slope, decay, total, par, skip, sent = own
     vmem = pl.BlockSpec(memory_space=pltpu.VMEM)
     shape = jax.ShapeDtypeStruct
     small = pltpu.VMEM(lay.cube, f32)
     return pl.pallas_call(
         lambda *refs: finish_kernel(lay, *refs),
-        in_specs=[vmem] * 19 + [pl.BlockSpec(memory_space=pltpu.SMEM)],
-        out_specs=[vmem] * 2,
-        out_shape=[shape((lay.chunks, lay.body + 16, LANES), bf16), shape(TILE, f32)],
+        in_specs=[vmem] * 15 + [pl.BlockSpec(memory_space=pltpu.SMEM)],
+        out_specs=[vmem] * 5,
+        out_shape=[shape((lay.chunks, 16, LANES), bf16), shape(TILE, f32), shape(lay.wide, bf16), shape(lay.wide, bf16),
+                   shape(lay.wide, f32)],
         scratch_shapes=[small, small, small],
         compiler_params=pltpu.CompilerParams(vmem_limit_bytes=FINISH_VMEM * MIB),
         name="scan_finish",
-    )(received, gh, gl, xh, xl, wide, step, slope, decay, total, par, skip, sent, came, *local, flag)
+    )(received, gh, gl, xh, xl, step, slope, decay, total, par, skip, sent, came, r, c, flag)
+
+
+def message_kernel(lay, gh_ref, gl_ref, xh_ref, xl_ref, wide_ref, gx_ref, din_ref, dout_ref,
+                   dstep_ref, uh_ref, ul_ref, more_ref, flag_ref, out_ref):
+    width = lay.width
+    first = flag_ref[0] == 0
+    out_ref[:, lay.body :] = dstep_ref[...]
+
+    def d_keys(k, high_ref, low_ref):
+        high, low = high_ref[k], low_ref[k]
+        return mm_nt(high, uh_ref[k]) + mm_nt(high, ul_ref[k]) + mm_nt(low, uh_ref[k])
+
+    def store(k, grad_x, d_in, d_out):
+        grad_x = grad_x.astype(bf16)
+        for j in range(lay.blocks):
+            out_ref[k, j * CHUNK : (j + 1) * CHUNK] = grad_x[:, j * LANES : (j + 1) * LANES]
+        for j, part in enumerate(split2(d_in) + split2(d_out)):
+            out_ref[k, width + j * CHUNK : width + (j + 1) * CHUNK] = part
+
+    @pl.when(first)
+    def _():
+        def one(k, carry):
+            store(k, gx_ref[k] + wide_ref[k] * more_ref[k], din_ref[k] + d_keys(k, xh_ref, xl_ref), dout_ref[k])
+            return carry
+
+        grouped(lay.chunks, one, 0)
+
+    @pl.when(jnp.logical_not(first))
+    def _():
+        def one(k, carry):
+            store(k, gx_ref[k], din_ref[k], dout_ref[k] + d_keys(k, gh_ref, gl_ref))
+            return carry
+
+        grouped(lay.chunks, one, 0)
+
+
+def message(own, local, finish, flag, lay):
+    gh, gl, xh, xl, _, _, wide, *_ = own
+    dstep, _, uh, ul, more = finish
+    vmem = pl.BlockSpec(memory_space=pltpu.VMEM)
+    return pl.pallas_call(
+        lambda *refs: message_kernel(lay, *refs),
+        in_specs=[vmem] * 12 + [pl.BlockSpec(memory_space=pltpu.SMEM)],
+        out_specs=vmem,
+        out_shape=jax.ShapeDtypeStruct((lay.chunks, lay.body + 16, LANES), bf16),
+        compiler_params=pltpu.CompilerParams(vmem_limit_bytes=FINISH_VMEM * MIB),
+        cost_estimate=pl.CostEstimate(flops=400_000_000, bytes_accessed=20_000_000, transcendentals=0),
+        name="message",
+    )(gh, gl, xh, xl, wide, *local[:3], dstep, uh, ul, more, flag)
 
 
 def unpack_kernel(lay, in_ref, x_ref, s_ref, b_ref, c_ref):
@@ -432,18 +471,25 @@
     return lax.ppermute(v, "seq", [(i, (i + groups) % (2 * groups)) for i in range(2 * groups)])
 
 
-def pair_sum(v):
-    replicas = lax.axis_size("dp")
+def near_sum(v):
+    replicas, shards = lax.axis_size("dp"), lax.axis_size("seq")
     if replicas == 1:
-        return v
-    return v + lax.ppermute(v, "dp", [(i, i ^ 1) for i in range(replicas)])
+        return v + from_partner(v)
+    halves = lambda i: (i + shards // HALVES) % shards
+    across = [(r * shards + i, (r ^ 1) * shards + halves(i)) for r in range(replicas) for i in range(shards)]
+    pair = lax.ppermute(v, "dp", [(r, r ^ 1) for r in range(replicas)])
+    return (v + from_partner(v)) + (pair + lax.ppermute(v, ("dp", "seq"), across))
 
 
 def line_sum(v):
     half = lax.axis_size("dp") // 2
     if half <= 1:
         return v
-    return lax.psum(v, "dp", axis_index_groups=[[2 * i + bit for i in range(half)] for bit in range(2)])
+    v = v + lax.ppermute(v, "dp", [(i, i ^ 2) for i in range(2 * half)])
+    if half == 2:
+        return v
+    lines = [[2 * i + bit for i in range(odd, half, 2)] for odd in range(2) for bit in range(2)]
+    return lax.psum(v, "dp", axis_index_groups=lines)
 
 
 def shards(inputs, raw_step, write_keys, read_keys, grad_out, decay_log, skip_gain, step_bias):
@@ -453,8 +499,8 @@
     half = lax.axis_index("seq") // groups
     flag = half.astype(jnp.int32)[None]
     send = pack(inputs[0], grad_out[0], write_keys[0], read_keys[0], raw_step[0].T, groups)
-    mine = jnp.stack([decay_log, skip_gain, step_bias])
-    send, mine = lax.optimization_barrier((send, mine))
+    send, *mine = lax.optimization_barrier((send, decay_log, skip_gain, step_bias))
+    mine = jnp.stack(mine)
     other = from_partner(mine)
     first = half == 0
     params = jnp.concatenate([jnp.where(first, mine, other), jnp.where(first, other, mine)], axis=1)
@@ -464,10 +510,11 @@
     own = scan_states(received, params, flag, lay)
     came = from_partner(own[-1])
     local = scan_local(received, own, lay)
-    back, per_head = scan_finish(received, own, local, came, flag, lay)
+    finish = scan_finish(received, own, local[3], local[4], came, flag, lay)
+    back = message(own, local, finish, flag, lay)
+    back, per_head = lax.optimization_barrier((back, near_sum(finish[1])))
     grad_x, grad_step, grad_write, grad_read = unpack(exchange(back), lay)
-    per_head = per_head + from_partner(per_head)
-    totals = line_sum(pair_sum(per_head))[:3] / lax.axis_size("dp")
+    totals = line_sum(per_head)[:3] / lax.axis_size("dp")
     totals = jnp.where(first, totals[:, :some], totals[:, some : 2 * some])
     return grad_x[None], grad_step.T[None], grad_write[None], grad_read[None], totals
 

time: 116 us -> 108 us (0.931)
  blocking collectives: 33.2 us -> 22 us
  starting transfers between devices: 23.6 us -> 30.1 us
  waiting for transfers between devices: 37.1 us -> 34.1 us
  Pallas kernels: 17.9 us -> 20.3 us
  local copies, waits for them, and re-layouts: 1.34 us -> 0.01 us
    psum x1, blocking collectives: 33.2 us -> 22 us  [line_sum(): return lax.psum(v, 'dp', axis_index_groups=lines)]
    ppermute x1 -> x3, starting transfers between devices: 1.91 us -> 9.54 us  [the longest x1 5.72 us: near_sum(): pair = lax.ppermute(v, 'dp', [(r, r ^ 1) for r in range(replicas)])]
    pallas_call x0 -> x1, Pallas kernels: none -> 2.77 us  [message(): pl.pallas_call(lambda *refs: message_kernel(lay, *refs), in_specs=[vmem]...]
    ppermute x1 -> x3, waiting for transfers between devices: 5.08 us -> 3.58 us  [the longest x1 3.57 us: line_sum(): v = v + lax.ppermute(v, 'dp', [(i, i ^ 2) for i in range(2 * half)])]
    ppermute x3, waiting for transfers between devices: 5.88 us -> 4.39 us  [from_partner(): lax.ppermute(v, 'seq', [(i, (i + groups) % (2 * groups)) for i in range(2...]
    unnamed x2 -> x6, local copies, waits for them, and re-layouts: 1.34 us -> 0.01 us
    ppermute x3, starting transfers between devices: 7.28 us -> 6.02 us  [from_partner(): lax.ppermute(v, 'seq', [(i, (i + groups) % (2 * groups)) for i in range(2...]
  transfers between devices with their start and end apart: 6 -> 8, of which waited for: 5 -> 5; matrix products, arithmetic and copies ran while one was open for 1% -> 1% of each run, Pallas kernels for 6% -> 10%
where the time goes in v3:
time: 108 us
  waiting for transfers between devices  34.1 us (32%)
  starting transfers between devices  30.1 us (28%)
  blocking collectives  22 us (20%)
  Pallas kernels  20.3 us (19%)
    all_to_all x2, waiting for transfers between devices, exchange(): lax.all_to_all(v, 'seq', split_axis=0, concat_axis=0, tiled=True, axis_in...  26.1 us
    psum x1, blocking collectives, line_sum(): return lax.psum(v, 'dp', axis_index_groups=lines)  22 us
    all_to_all x2, starting transfers between devices, exchange(): lax.all_to_all(v, 'seq', split_axis=0, concat_axis=0, tiled=True, axis_in...  14.5 us
    pallas_call x1, Pallas kernels, scan_local(): pl.pallas_call(lambda *refs: local_kernel(lay, *refs), in_specs=[vmem] *...  7.49 us
    ppermute x3, starting transfers between devices, from_partner(): lax.ppermute(v, 'seq', [(i, (i + groups) % (2 * groups)) for i in range(2...  6.02 us
    ppermute x1, starting transfers between devices, near_sum(): pair = lax.ppermute(v, 'dp', [(r, r ^ 1) for r in range(replicas)])  5.72 us
    ppermute x3, waiting for transfers between devices, from_partner(): lax.ppermute(v, 'seq', [(i, (i + groups) % (2 * groups)) for i in range(2...  4.39 us
    ppermute x1, waiting for transfers between devices, line_sum(): v = v + lax.ppermute(v, 'dp', [(i, i ^ 2) for i in range(2 * half)])  3.57 us
  transfers between devices with their start and end apart: 8, of which 5 were waited for; matrix products, arithmetic and copies ran while one was open for 1% of the time, Pallas kernels for 10%

profile of v3, /device:TPU:2, one launch (start us, length us, event | category | flops | bytes accessed | tf_op | source)
XLA Modules:
  0.0 108.0 jit_solution(16847476435415332839)
XLA Ops:
  0.6 3.0 %pack.1 = bf16[8,1296,128]{2,1,0:T(8,128)(2,1)} custom-call(bf16[128,4096]{1,0:T(8,128)(2,1)} %bitcast.17, bf16[128,4096]{1,0:T(8,128)(2,1)} %bitcast.18, bf16[128,4096]{1,0:T(8,128)(2,1)} %bitcast.19, bf16[128,4096]{1,0:T(8,128)(2,1)} %bitcast.20, bf16[128,128]{1,0:T(8,128)(2,1)} %bitcast.21, bf16[128,128]{1,0:T(8,128)(2,1)} %bitcast.22, ...), custom_call_target="tpu_custom_call" | custom-call | tf_op jit(solution)/shard_map/pack/pallas_call | solution.py:96
  3.6 0.0 copy-start
  3.6 0.0 copy-start.1
  3.6 0.0 copy-start.2
  3.6 9.6 %all-to-all-start = ((bf16[8,1296,128]{2,1,0:T(8,128)(2,1)}), bf16[8,1296,128]{2,1,0:T(8,128)(2,1)S(1)}, u32[]{:S(2)}, u32[]{:S(2)}) async-start(bf16[8,1296,128]{2,1,0:T(8,128)(2,1)} %pack.1), calls=%async_computation | async-start | bytes 5308416 | tf_op jit(solution)/shard_map/all_to_all | solution.py:466
  13.2 0.0 copy-done
  13.2 0.0 copy-done.1
  13.2 0.0 copy-done.2
  13.2 1.9 %collective-permute-start = (f32[3,4]{1,0:T(4,128)S(1)}, f32[3,4]{1,0:T(4,128)S(1)}, u32[]{:S(2)}, u32[]{:S(2)}) collective-permute-start(f32[3,4]{1,0:T(4,128)S(1)} %pad_maximum_fusion), channel_id=1, source_target_pairs={{0,8},{1,9},{2,10},{3,11},{4,12},{5,13},{6,14},{7,15},{8,0},{9,1},... | collective-permute-start | bytes 152 | tf_op jit(solution)/shard_map/ppermute | solution.py:471
  15.2 3.5 %collective-permute-done = f32[3,4]{1,0:T(4,128)S(1)} collective-permute-done((f32[3,4]{1,0:T(4,128)S(1)}, f32[3,4]{1,0:T(4,128)S(1)}, u32[]{:S(2)}, u32[]{:S(2)}) %collective-permute-start) | collective-permute-done | bytes 80 | tf_op jit(solution)/shard_map/ppermute | solution.py:471
  18.7 0.1 select_maximum_fusion.refs_1_
  18.8 26.1 %all-to-all-done.refs_0_ = bf16[8,1296,128]{2,1,0:T(8,128)(2,1)S(1)} async-done(((bf16[8,1296,128]{2,1,0:T(8,128)(2,1)}), bf16[8,1296,128]{2,1,0:T(8,128)(2,1)S(1)}, u32[]{:S(2)}, u32[]{:S(2)}) %all-to-all-start) | async-done | bytes 2654240 | tf_op jit(solution)/shard_map/all_to_all | solution.py:466
  44.9 3.2 %scan_states.1 = (bf16[8,128,512]{2,1,0:T(8,128)(2,1)S(1)}, bf16[8,128,512]{2,1,0:T(8,128)(2,1)S(1)}, bf16[8,128,512]{2,1,0:T(8,128)(2,1)S(1)}, bf16[8,128,512]{...) custom-call(bf16[8,1296,128]{2,1,0:T(8,128)(2,1)S(1)} %all-to-all-do, ...), custom_call_target="tpu_custom_call" | custom-call | tf_op jit(solution)/shard_map/scan_states/pallas_call | solution.py:230
  48.2 1.9 %collective-permute-start.1 = (f32[128,512]{1,0:T(8,128)S(1)}, f32[128,512]{1,0:T(8,128)S(1)}, u32[]{:S(2)}, u32[]{:S(2)}) collective-permute-start(f32[128,512]{1,0:T(8,128)S(1)} %get-tuple-element.59.refs_11_), channel_id=1, source_target_pairs={{0,8},{1,9},{2,10},{3,11},{4,12},{5,13},{6,14},{7,15},{8,0},{9,1},... | collective-permute-start | bytes 786440 | tf_op jit(solution)/shard_map/ppermute | solution.py:471
  50.1 7.5 %scan_local.1 = (f32[8,128,512]{2,1,0:T(8,128)S(1)}, f32[8,128,128]{2,1,0:T(8,128)S(1)}, f32[8,128,128]{2,1,0:T(8,128)S(1)}, f32[8,8,128]{2,1,0:T(8,128)S(1)}, f32[8,8,128]{2,1,0:T(8,128)S(1)}) custom-call(bf16[8,1296,128]{2,1,0:T(8,128)(2,1)S(1)} %all-to-all-done.refs_0_, bf16[8,128,512]{2,1,0:T(8,128)(2,1)S(1)} %get-tuple-element.43.refs_1_.refs_0_, ...), custom_call_target="tpu_custom_call" | custom-call | tf_op jit(solution)/shard_map/scan_local/pallas_call | solution.py:285
  57.6 0.3 collective-permute-done.1.refs_12_
  57.9 2.6 %scan_finish.1 = (bf16[8,16,128]{2,1,0:T(8,128)(2,1)S(1)}, f32[8,128]{1,0:T(8,128)S(1)}, bf16[8,128,512]{2,1,0:T(8,128)(2,1)S(1)}, bf16[8,128,512]{2,1,0:T(8,128)(2,1)S(1)}, f32[8,128,512]{2,1,0:T(8,128)S(1)}) custom-call(bf16[8,1296,128]{2,1,0:T(8,128)(2,1)S(1)} %all-to-all-done.refs_0_, bf16[8,128,512]{2,1,0:T(8,128)(2,1)S(1)} %get-tuple-element.43.refs_1_.refs_0_, ...), custom_call_target="tpu_custom_call" | custom-call | tf_op jit(solution)/shard_map/scan_finish/pallas_call | solution.py:370
  60.5 1.9 %collective-permute-start.4 = (f32[8,128]{1,0:T(8,128)S(1)}, f32[8,128]{1,0:T(8,128)S(1)}, u32[]{:S(2)}, u32[]{:S(2)}) collective-permute-start(f32[8,128]{1,0:T(8,128)S(1)} %get-tuple-element.66), channel_id=1, source_target_pairs={{0,24},{1,25},{2,26},{3,27},{4,28},{5,29},{6,30},{7,31},{8,16},{9,... | collective-permute-start | bytes 12296 | tf_op jit(solution)/shard_map/ppermute | solution.py:481
  62.4 5.7 %collective-permute-start.3 = (f32[8,128]{1,0:T(8,128)S(1)}, f32[8,128]{1,0:T(8,128)S(1)}, u32[]{:S(2)}, u32[]{:S(2)}) collective-permute-start(f32[8,128]{1,0:T(8,128)S(1)} %get-tuple-element.66), channel_id=1, source_target_pairs={{0,16},{16,0},{32,48},{48,32},{64,80},{80,64},{96,112},{112,96},{1... | collective-permute-start | bytes 12296 | tf_op jit(solution)/shard_map/ppermute | solution.py:480
  68.1 2.2 %collective-permute-start.2 = (f32[8,128]{1,0:T(8,128)S(1)}, f32[8,128]{1,0:T(8,128)S(1)}, u32[]{:S(2)}, u32[]{:S(2)}) collective-permute-start(f32[8,128]{1,0:T(8,128)S(1)} %get-tuple-element.66), channel_id=1, source_target_pairs={{0,8},{1,9},{2,10},{3,11},{4,12},{5,13},{6,14},{7,15},{8,0},{9,1},... | collective-permute-start | bytes 12296 | tf_op jit(solution)/shard_map/ppermute | solution.py:471
  70.3 2.8 %message.1 = bf16[8,1040,128]{2,1,0:T(8,128)(2,1)} custom-call(bf16[8,128,512]{2,1,0:T(8,128)(2,1)S(1)} %get-tuple-element.43.refs_1_.refs_0_, bf16[8,128,512]{2,1,0:T(8,128)(2,1)S(1)} %get-tuple-element.44.refs_2_.refs_1_, bf16[8,128,512]{2,1,0:T(8,128)(2,1)S(1)} %get-tuple-element.45.refs_3_.refs_2_, ...), custom_call_target="tpu_custom_call" | custom-call | flops 400000000 | bytes 20000000 | tf_op jit(solution)/shard_map/message/pallas_call | solution.py:420
  73.1 0.0 collective-permute-done.4
  73.1 0.0 collective-permute-done.3
  73.1 0.5 collective-permute-done.2
  73.6 5.0 %all-to-all-start.1 = ((bf16[8,1040,128]{2,1,0:T(8,128)(2,1)}), bf16[8,1040,128]{2,1,0:T(8,128)(2,1)S(1)}, u32[]{:S(2)}, u32[]{:S(2)}) async-start(bf16[8,1040,128]{2,1,0:T(8,128)(2,1)} %message.1), calls=%async_computation.1 | async-start | bytes 4259840 | tf_op jit(solution)/shard_map/all_to_all | solution.py:466
  78.6 1.9 %collective-permute-start.5 = (f32[8,128]{1,0:T(8,128)S(1)}, f32[8,128]{1,0:T(8,128)S(1)}, u32[]{:S(2)}, u32[]{:S(2)}) collective-permute-start(f32[8,128]{1,0:T(8,128)S(1)} %add_add_fusion), channel_id=1, source_target_pairs={{0,32},{16,48},{32,0},{48,16},{64,96},{80,112},{96,64},{112,80},{1... | collective-permute-start | bytes 12296 | tf_op jit(solution)/shard_map/ppermute | solution.py:488
  80.5 3.6 %collective-permute-done.5 = f32[8,128]{1,0:T(8,128)S(1)} collective-permute-done((f32[8,128]{1,0:T(8,128)S(1)}, f32[8,128]{1,0:T(8,128)S(1)}, u32[]{:S(2)}, u32[]{:S(2)}) %collective-permute-start.5) | collective-permute-done | bytes 4128 | tf_op jit(solution)/shard_map/ppermute | solution.py:488
  84.1 22.0 %psum.7 = f32[8,128]{1,0:T(8,128)S(1)} all-reduce(f32[8,128]{1,0:T(8,128)S(1)} %add.20), channel_id=1, replica_groups={{0,64,128,192,256,320,384,448},{16,80,144,208,272,336,400,464},{32,96,1..., use_global_device_ids=true, to_apply=%region_0.1 | all-reduce | flops 1024 | bytes 8192 | tf_op jit(solution)/shard_map/psum | solution.py:492
  106.1 0.7 slice_select_fusion
  106.8 0.0 all-to-all-done.1.refs_0_
  106.8 1.3 %unpack.1 = (bf16[128,4096]{1,0:T(8,128)(2,1)}, bf16[64,128]{1,0:T(8,128)(2,1)}, bf16[128,128]{1,0:T(8,128)(2,1)}, bf16[128,128]{1,0:T(8,128)(2,1)}) custom-call(bf16[8,1040,128]{2,1,0:T(8,128)(2,1)S(1)} %all-to-all-done.1.refs_0_), custom_call_target="tpu_custom_call" | custom-call | tf_op jit(solution)/shard_map/unpack/pallas_call | solution.py:453
  (5 shorter events, 0.0 us)
Async XLA Ops:
  3.6 9.6 %copy-start = (f32[4]{0:T(128)S(1)}, f32[4]{0:T(128)}, u32[]{:S(2)}) copy-start(f32[4]{0:T(128)} %param.15) | copy-start | bytes 52
  3.6 9.6 %copy-start.1 = (f32[4]{0:T(128)S(1)}, f32[4]{0:T(128)}, u32[]{:S(2)}) copy-start(f32[4]{0:T(128)} %param.14) | copy-start | bytes 52
  3.6 9.6 %copy-start.2 = (f32[4]{0:T(128)S(1)}, f32[4]{0:T(128)}, u32[]{:S(2)}) copy-start(f32[4]{0:T(128)} %param.13) | copy-start | bytes 52
  3.6 41.3 %all-to-all-start = ((bf16[8,1296,128]{2,1,0:T(8,128)(2,1)}), bf16[8,1296,128]{2,1,0:T(8,128)(2,1)S(1)}, u32[]{:S(2)}, u32[]{:S(2)}) async-start(bf16[8,1296,128]{2,1,0:T(8,128)(2,1)} %pack.1), calls=%async_computation | async-start | bytes 5308416 | tf_op jit(solution)/shard_map/all_to_all | solution.py:466
  13.2 5.5 %collective-permute-start = (f32[3,4]{1,0:T(4,128)S(1)}, f32[3,4]{1,0:T(4,128)S(1)}, u32[]{:S(2)}, u32[]{:S(2)}) collective-permute-start(f32[3,4]{1,0:T(4,128)S(1)} %pad_maximum_fusion), channel_id=1, source_target_pairs={{0,8},{1,9},{2,10},{3,11},{4,12},{5,13},{6,14},{7,15},{8,0},{9,1},... | collective-permute-start | bytes 152 | tf_op jit(solution)/shard_map/ppermute | solution.py:471
  48.2 9.7 %collective-permute-start.1 = (f32[128,512]{1,0:T(8,128)S(1)}, f32[128,512]{1,0:T(8,128)S(1)}, u32[]{:S(2)}, u32[]{:S(2)}) collective-permute-start(f32[128,512]{1,0:T(8,128)S(1)} %get-tuple-element.59.refs_11_), channel_id=1, source_target_pairs={{0,8},{1,9},{2,10},{3,11},{4,12},{5,13},{6,14},{7,15},{8,0},{9,1},... | collective-permute-start | bytes 786440 | tf_op jit(solution)/shard_map/ppermute | solution.py:471
  60.5 12.6 %collective-permute-start.4 = (f32[8,128]{1,0:T(8,128)S(1)}, f32[8,128]{1,0:T(8,128)S(1)}, u32[]{:S(2)}, u32[]{:S(2)}) collective-permute-start(f32[8,128]{1,0:T(8,128)S(1)} %get-tuple-element.66), channel_id=1, source_target_pairs={{0,24},{1,25},{2,26},{3,27},{4,28},{5,29},{6,30},{7,31},{8,16},{9,... | collective-permute-start | bytes 12296 | tf_op jit(solution)/shard_map/ppermute | solution.py:481
  62.4 10.7 %collective-permute-start.3 = (f32[8,128]{1,0:T(8,128)S(1)}, f32[8,128]{1,0:T(8,128)S(1)}, u32[]{:S(2)}, u32[]{:S(2)}) collective-permute-start(f32[8,128]{1,0:T(8,128)S(1)} %get-tuple-element.66), channel_id=1, source_target_pairs={{0,16},{16,0},{32,48},{48,32},{64,80},{80,64},{96,112},{112,96},{1... | collective-permute-start | bytes 12296 | tf_op jit(solution)/shard_map/ppermute | solution.py:480
  68.1 5.5 %collective-permute-start.2 = (f32[8,128]{1,0:T(8,128)S(1)}, f32[8,128]{1,0:T(8,128)S(1)}, u32[]{:S(2)}, u32[]{:S(2)}) collective-permute-start(f32[8,128]{1,0:T(8,128)S(1)} %get-tuple-element.66), channel_id=1, source_target_pairs={{0,8},{1,9},{2,10},{3,11},{4,12},{5,13},{6,14},{7,15},{8,0},{9,1},... | collective-permute-start | bytes 12296 | tf_op jit(solution)/shard_map/ppermute | solution.py:471
  73.6 33.1 %all-to-all-start.1 = ((bf16[8,1040,128]{2,1,0:T(8,128)(2,1)}), bf16[8,1040,128]{2,1,0:T(8,128)(2,1)S(1)}, u32[]{:S(2)}, u32[]{:S(2)}) async-start(bf16[8,1040,128]{2,1,0:T(8,128)(2,1)} %message.1), calls=%async_computation.1 | async-start | bytes 4259840 | tf_op jit(solution)/shard_map/all_to_all | solution.py:466
  78.6 5.5 %collective-permute-start.5 = (f32[8,128]{1,0:T(8,128)S(1)}, f32[8,128]{1,0:T(8,128)S(1)}, u32[]{:S(2)}, u32[]{:S(2)}) collective-permute-start(f32[8,128]{1,0:T(8,128)S(1)} %add_add_fusion), channel_id=1, source_target_pairs={{0,32},{16,48},{32,0},{48,16},{64,96},{80,112},{96,64},{112,80},{1... | collective-permute-start | bytes 12296 | tf_op jit(solution)/shard_map/ppermute | solution.py:488

commit v4 on v2

--- a/solution.py
+++ b/solution.py
@@ -14,7 +14,7 @@
 PACK_STEPS = 2
 HALVES = 2
 PER_TILE = LANES // (2 * ROWS)
-UNROLL = 4
+UNROLL = 8
 STATES_VMEM = 24
 LOCAL_VMEM = 24
 FINISH_VMEM = 24
@@ -432,18 +432,25 @@
     return lax.ppermute(v, "seq", [(i, (i + groups) % (2 * groups)) for i in range(2 * groups)])
 
 
-def pair_sum(v):
-    replicas = lax.axis_size("dp")
+def near_sum(v):
+    replicas, shards = lax.axis_size("dp"), lax.axis_size("seq")
     if replicas == 1:
-        return v
-    return v + lax.ppermute(v, "dp", [(i, i ^ 1) for i in range(replicas)])
+        return v + from_partner(v)
+    halves = lambda i: (i + shards // HALVES) % shards
+    across = [(r * shards + i, (r ^ 1) * shards + halves(i)) for r in range(replicas) for i in range(shards)]
+    pair = lax.ppermute(v, "dp", [(r, r ^ 1) for r in range(replicas)])
+    return (v + from_partner(v)) + (pair + lax.ppermute(v, ("dp", "seq"), across))
 
 
 def line_sum(v):
     half = lax.axis_size("dp") // 2
     if half <= 1:
         return v
-    return lax.psum(v, "dp", axis_index_groups=[[2 * i + bit for i in range(half)] for bit in range(2)])
+    v = v + lax.ppermute(v, "dp", [(i, i ^ 2) for i in range(2 * half)])
+    if half == 2:
+        return v
+    lines = [[2 * i + bit for i in range(odd, half, 2)] for odd in range(2) for bit in range(2)]
+    return lax.psum(v, "dp", axis_index_groups=lines)
 
 
 def shards(inputs, raw_step, write_keys, read_keys, grad_out, decay_log, skip_gain, step_bias):
@@ -453,8 +460,8 @@
     half = lax.axis_index("seq") // groups
     flag = half.astype(jnp.int32)[None]
     send = pack(inputs[0], grad_out[0], write_keys[0], read_keys[0], raw_step[0].T, groups)
-    mine = jnp.stack([decay_log, skip_gain, step_bias])
-    send, mine = lax.optimization_barrier((send, mine))
+    send, *mine = lax.optimization_barrier((send, decay_log, skip_gain, step_bias))
+    mine = jnp.stack(mine)
     other = from_partner(mine)
     first = half == 0
     params = jnp.concatenate([jnp.where(first, mine, other), jnp.where(first, other, mine)], axis=1)
@@ -466,8 +473,7 @@
     local = scan_local(received, own, lay)
     back, per_head = scan_finish(received, own, local, came, flag, lay)
     grad_x, grad_step, grad_write, grad_read = unpack(exchange(back), lay)
-    per_head = per_head + from_partner(per_head)
-    totals = line_sum(pair_sum(per_head))[:3] / lax.axis_size("dp")
+    totals = line_sum(near_sum(per_head))[:3] / lax.axis_size("dp")
     totals = jnp.where(first, totals[:, :some], totals[:, some : 2 * some])
     return grad_x[None], grad_step.T[None], grad_write[None], grad_read[None], totals
 

time: 116 us -> 111 us (0.957)
  blocking collectives: 33.2 us -> 24.3 us
  starting transfers between devices: 23.6 us -> 31 us
  waiting for transfers between devices: 37.1 us -> 35.1 us
    psum x1, blocking collectives: 33.2 us -> 24.3 us  [line_sum(): return lax.psum(v, 'dp', axis_index_groups=lines)]
    ppermute x1 -> x3, starting transfers between devices: 1.91 us -> 9.43 us  [the longest x1 5.3 us: near_sum(): return v + from_partner(v) + (pair + lax.ppermute(v, ('dp', 'seq'), across))]
    ppermute x3, waiting for transfers between devices: 5.88 us -> 4.15 us  [from_partner(): lax.ppermute(v, 'seq', [(i, (i + groups) % (2 * groups)) for i in range(2...]
    ppermute x1 -> x3, waiting for transfers between devices: 5.08 us -> 4.83 us  [the longest x1 3.27 us: line_sum(): v = v + lax.ppermute(v, 'dp', [(i, i ^ 2) for i in range(2 * half)])]
  transfers between devices with their start and end apart: 6 -> 8, of which waited for: 5 -> 5; matrix products, arithmetic and copies ran while one was open for 1% -> 1% of each run, Pallas kernels for 6% -> 7%
where the time goes in v4:
time: 111 us
  waiting for transfers between devices  35.1 us (32%)
  starting transfers between devices  31 us (28%)
  blocking collectives  24.3 us (22%)
  Pallas kernels  17.3 us (16%)
  local copies, waits for them, and re-layouts  1.37 us (1%)
    all_to_all x2, waiting for transfers between devices, exchange(): lax.all_to_all(v, 'seq', split_axis=0, concat_axis=0, tiled=True, axis_in...  26.1 us
    psum x1, blocking collectives, line_sum(): return lax.psum(v, 'dp', axis_index_groups=lines)  24.3 us
    all_to_all x2, starting transfers between devices, exchange(): lax.all_to_all(v, 'seq', split_axis=0, concat_axis=0, tiled=True, axis_in...  14.5 us
    pallas_call x1, Pallas kernels, scan_local(): pl.pallas_call(lambda *refs: local_kernel(lay, *refs), in_specs=[vmem] *...  7.2 us
    ppermute x3, starting transfers between devices, from_partner(): lax.ppermute(v, 'seq', [(i, (i + groups) % (2 * groups)) for i in range(2...  7.04 us
    ppermute x1, starting transfers between devices, near_sum(): return v + from_partner(v) + (pair + lax.ppermute(v, ('dp', 'seq'), across))  5.3 us
    ppermute x3, waiting for transfers between devices, from_partner(): lax.ppermute(v, 'seq', [(i, (i + groups) % (2 * groups)) for i in range(2...  4.15 us
    ppermute x1, waiting for transfers between devices, line_sum(): v = v + lax.ppermute(v, 'dp', [(i, i ^ 2) for i in range(2 * half)])  3.27 us
  transfers between devices with their start and end apart: 8, of which 5 were waited for; matrix products, arithmetic and copies ran while one was open for 1% of the time, Pallas kernels for 7%

profile of v4, /device:TPU:2, one launch (start us, length us, event | category | flops | bytes accessed | tf_op | source)
XLA Modules:
  0.0 110.6 jit_solution(17260053150988195633)
XLA Ops:
  0.6 3.0 %pack.1 = bf16[8,1296,128]{2,1,0:T(8,128)(2,1)} custom-call(bf16[128,4096]{1,0:T(8,128)(2,1)} %bitcast.17, bf16[128,4096]{1,0:T(8,128)(2,1)} %bitcast.18, bf16[128,4096]{1,0:T(8,128)(2,1)} %bitcast.19, bf16[128,4096]{1,0:T(8,128)(2,1)} %bitcast.20, bf16[128,128]{1,0:T(8,128)(2,1)} %bitcast.21, bf16[128,128]{1,0:T(8,128)(2,1)} %bitcast.22, ...), custom_call_target="tpu_custom_call" | custom-call | tf_op jit(solution)/shard_map/pack/pallas_call | solution.py:96
  3.6 0.0 copy-start.1
  3.6 0.0 copy-start.2
  3.6 0.0 copy-start.3
  3.6 9.6 %all-to-all-start = ((bf16[8,1296,128]{2,1,0:T(8,128)(2,1)}), bf16[8,1296,128]{2,1,0:T(8,128)(2,1)S(1)}, u32[]{:S(2)}, u32[]{:S(2)}) async-start(bf16[8,1296,128]{2,1,0:T(8,128)(2,1)} %pack.1), calls=%async_computation | async-start | bytes 5308416 | tf_op jit(solution)/shard_map/all_to_all | solution.py:427
  13.2 0.0 copy-done.1
  13.2 0.0 copy-done.2
  13.2 0.0 copy-done.3
  13.2 1.9 %collective-permute-start = (f32[3,4]{1,0:T(4,128)S(1)}, f32[3,4]{1,0:T(4,128)S(1)}, u32[]{:S(2)}, u32[]{:S(2)}) collective-permute-start(f32[3,4]{1,0:T(4,128)S(1)} %pad_maximum_fusion), channel_id=1, source_target_pairs={{0,8},{1,9},{2,10},{3,11},{4,12},{5,13},{6,14},{7,15},{8,0},{9,1},... | collective-permute-start | bytes 152 | tf_op jit(solution)/shard_map/ppermute | solution.py:432
  15.2 3.5 %collective-permute-done = f32[3,4]{1,0:T(4,128)S(1)} collective-permute-done((f32[3,4]{1,0:T(4,128)S(1)}, f32[3,4]{1,0:T(4,128)S(1)}, u32[]{:S(2)}, u32[]{:S(2)}) %collective-permute-start) | collective-permute-done | bytes 80 | tf_op jit(solution)/shard_map/ppermute | solution.py:432
  18.7 0.1 select_maximum_fusion.refs_1_
  18.8 26.1 %all-to-all-done.refs_0_ = bf16[8,1296,128]{2,1,0:T(8,128)(2,1)S(1)} async-done(((bf16[8,1296,128]{2,1,0:T(8,128)(2,1)}), bf16[8,1296,128]{2,1,0:T(8,128)(2,1)S(1)}, u32[]{:S(2)}, u32[]{:S(2)}) %all-to-all-start) | async-done | bytes 2654240 | tf_op jit(solution)/shard_map/all_to_all | solution.py:427
  45.0 3.0 %scan_states.1 = (bf16[8,128,512]{2,1,0:T(8,128)(2,1)S(1)}, bf16[8,128,512]{2,1,0:T(8,128)(2,1)S(1)}, bf16[8,128,512]{2,1,0:T(8,128)(2,1)S(1)}, bf16[8,128,512]{...) custom-call(bf16[8,1296,128]{2,1,0:T(8,128)(2,1)S(1)} %all-to-all-do, ...), custom_call_target="tpu_custom_call" | custom-call | tf_op jit(solution)/shard_map/scan_states/pallas_call | solution.py:230
  48.0 1.9 %collective-permute-start.1 = (f32[128,512]{1,0:T(8,128)S(1)}, f32[128,512]{1,0:T(8,128)S(1)}, u32[]{:S(2)}, u32[]{:S(2)}) collective-permute-start(f32[128,512]{1,0:T(8,128)S(1)} %get-tuple-element.49.refs_12_), channel_id=1, source_target_pairs={{0,8},{1,9},{2,10},{3,11},{4,12},{5,13},{6,14},{7,15},{8,0},{9,1},... | collective-permute-start | bytes 786440 | tf_op jit(solution)/shard_map/ppermute | solution.py:432
  49.9 7.2 %scan_local.1 = (f32[8,128,512]{2,1,0:T(8,128)S(1)}, f32[8,128,128]{2,1,0:T(8,128)S(1)}, f32[8,128,128]{2,1,0:T(8,128)S(1)}, f32[8,8,128]{2,1,0:T(8,128)S(1)}, f32[8,8,128]{2,1,0:T(8,128)S(1)}) custom-call(bf16[8,1296,128]{2,1,0:T(8,128)(2,1)S(1)} %all-to-all-done.refs_0_, bf16[8,128,512]{2,1,0:T(8,128)(2,1)S(1)} %get-tuple-element.38.refs_1_, ...), custom_call_target="tpu_custom_call" | custom-call | tf_op jit(solution)/shard_map/scan_local/pallas_call | solution.py:285
  57.1 0.6 collective-permute-done.1.refs_13_
  57.7 2.9 %scan_finish.1 = (bf16[8,1040,128]{2,1,0:T(8,128)(2,1)S(1)}, f32[8,128]{1,0:T(8,128)S(1)}) custom-call(bf16[8,1296,128]{2,1,0:T(8,128)(2,1)S(1)} %all-to-all-done.refs_0_, bf16[8,128,512]{2,1,0:T(8,128)(2,1)S(1)} %get-tuple-element.38.refs_1_, bf16[8,128,512]{2,1,0:T(8,128)(2,1)S(1)} %get-tuple-element.39.refs_2_, ...), custom_call_target="tpu_custom_call" | custom-call | tf_op jit(solution)/shard_map/scan_finish/pallas_call | solution.py:381
  60.6 0.0 copy-start
  60.6 1.4 %copy-done = bf16[8,1040,128]{2,1,0:T(8,128)(2,1)} copy-done((bf16[8,1040,128]{2,1,0:T(8,128)(2,1)}, bf16[8,1040,128]{2,1,0:T(8,128)(2,1)S(1)}, u32[]{:S(2)}) %copy-start) | copy-done | bytes 2129944
  62.0 5.0 %all-to-all-start.1 = ((bf16[8,1040,128]{2,1,0:T(8,128)(2,1)}), bf16[8,1040,128]{2,1,0:T(8,128)(2,1)S(1)}, u32[]{:S(2)}, u32[]{:S(2)}) async-start(bf16[8,1040,128]{2,1,0:T(8,128)(2,1)} %copy-done), calls=%async_computation.1 | async-start | bytes 4259840 | tf_op jit(solution)/shard_map/all_to_all | solution.py:427
  66.9 3.2 %collective-permute-start.2 = (f32[8,128]{1,0:T(8,128)S(1)}, f32[8,128]{1,0:T(8,128)S(1)}, u32[]{:S(2)}, u32[]{:S(2)}) collective-permute-start(f32[8,128]{1,0:T(8,128)S(1)} %get-tuple-element.62), channel_id=1, source_target_pairs={{0,8},{1,9},{2,10},{3,11},{4,12},{5,13},{6,14},{7,15},{8,0},{9,1},... | collective-permute-start | bytes 12296 | tf_op jit(solution)/shard_map/ppermute | solution.py:432
  70.1 1.9 %collective-permute-start.3 = (f32[8,128]{1,0:T(8,128)S(1)}, f32[8,128]{1,0:T(8,128)S(1)}, u32[]{:S(2)}, u32[]{:S(2)}) collective-permute-start(f32[8,128]{1,0:T(8,128)S(1)} %get-tuple-element.62), channel_id=1, source_target_pairs={{0,16},{16,0},{32,48},{48,32},{64,80},{80,64},{96,112},{112,96},{1... | collective-permute-start | bytes 12296 | tf_op jit(solution)/shard_map/ppermute | solution.py:441
  72.0 5.3 %collective-permute-start.4 = (f32[8,128]{1,0:T(8,128)S(1)}, f32[8,128]{1,0:T(8,128)S(1)}, u32[]{:S(2)}, u32[]{:S(2)}) collective-permute-start(f32[8,128]{1,0:T(8,128)S(1)} %get-tuple-element.62), channel_id=1, source_target_pairs={{0,24},{1,25},{2,26},{3,27},{4,28},{5,29},{6,30},{7,31},{8,16},{9,... | collective-permute-start | bytes 12296 | tf_op jit(solution)/shard_map/ppermute | solution.py:442
  77.3 0.0 collective-permute-done.2
  77.4 0.0 collective-permute-done.3
  77.4 1.6 %collective-permute-done.4 = f32[8,128]{1,0:T(8,128)S(1)} collective-permute-done((f32[8,128]{1,0:T(8,128)S(1)}, f32[8,128]{1,0:T(8,128)S(1)}, u32[]{:S(2)}, u32[]{:S(2)}) %collective-permute-start.4) | collective-permute-done | bytes 4128 | tf_op jit(solution)/shard_map/ppermute | solution.py:442
  78.9 2.2 %collective-permute-start.5 = (f32[8,128]{1,0:T(8,128)S(1)}, f32[8,128]{1,0:T(8,128)S(1)}, u32[]{:S(2)}, u32[]{:S(2)}) collective-permute-start(f32[8,128]{1,0:T(8,128)S(1)} %add_add_fusion), channel_id=1, source_target_pairs={{0,32},{16,48},{32,0},{48,16},{64,96},{80,112},{96,64},{112,80},{1... | collective-permute-start | bytes 12296 | tf_op jit(solution)/shard_map/ppermute | solution.py:449
  81.1 3.3 %collective-permute-done.5 = f32[8,128]{1,0:T(8,128)S(1)} collective-permute-done((f32[8,128]{1,0:T(8,128)S(1)}, f32[8,128]{1,0:T(8,128)S(1)}, u32[]{:S(2)}, u32[]{:S(2)}) %collective-permute-start.5) | collective-permute-done | bytes 4128 | tf_op jit(solution)/shard_map/ppermute | solution.py:449
  84.4 24.3 %psum.7 = f32[8,128]{1,0:T(8,128)S(1)} all-reduce(f32[8,128]{1,0:T(8,128)S(1)} %add.20), channel_id=1, replica_groups={{0,64,128,192,256,320,384,448},{16,80,144,208,272,336,400,464},{32,96,1..., use_global_device_ids=true, to_apply=%region_0.1 | all-reduce | flops 1024 | bytes 8192 | tf_op jit(solution)/shard_map/psum | solution.py:453
  108.7 0.7 slice_select_fusion
  109.3 0.0 all-to-all-done.1.refs_0_
  109.3 1.3 %unpack.1 = (bf16[128,4096]{1,0:T(8,128)(2,1)}, bf16[64,128]{1,0:T(8,128)(2,1)}, bf16[128,128]{1,0:T(8,128)(2,1)}, bf16[128,128]{1,0:T(8,128)(2,1)}) custom-call(bf16[8,1040,128]{2,1,0:T(8,128)(2,1)S(1)} %all-to-all-done.1.refs_0_), custom_call_target="tpu_custom_call" | custom-call | tf_op jit(solution)/shard_map/unpack/pallas_call | solution.py:414
  (5 shorter events, 0.0 us)
Async XLA Ops:
  3.6 9.6 %copy-start.1 = (f32[4]{0:T(128)S(1)}, f32[4]{0:T(128)}, u32[]{:S(2)}) copy-start(f32[4]{0:T(128)} %param.15) | copy-start | bytes 52
  3.6 9.6 %copy-start.2 = (f32[4]{0:T(128)S(1)}, f32[4]{0:T(128)}, u32[]{:S(2)}) copy-start(f32[4]{0:T(128)} %param.14) | copy-start | bytes 52
  3.6 9.6 %copy-start.3 = (f32[4]{0:T(128)S(1)}, f32[4]{0:T(128)}, u32[]{:S(2)}) copy-start(f32[4]{0:T(128)} %param.13) | copy-start | bytes 52
  3.6 41.3 %all-to-all-start = ((bf16[8,1296,128]{2,1,0:T(8,128)(2,1)}), bf16[8,1296,128]{2,1,0:T(8,128)(2,1)S(1)}, u32[]{:S(2)}, u32[]{:S(2)}) async-start(bf16[8,1296,128]{2,1,0:T(8,128)(2,1)} %pack.1), calls=%async_computation | async-start | bytes 5308416 | tf_op jit(solution)/shard_map/all_to_all | solution.py:427
  13.2 5.5 %collective-permute-start = (f32[3,4]{1,0:T(4,128)S(1)}, f32[3,4]{1,0:T(4,128)S(1)}, u32[]{:S(2)}, u32[]{:S(2)}) collective-permute-start(f32[3,4]{1,0:T(4,128)S(1)} %pad_maximum_fusion), channel_id=1, source_target_pairs={{0,8},{1,9},{2,10},{3,11},{4,12},{5,13},{6,14},{7,15},{8,0},{9,1},... | collective-permute-start | bytes 152 | tf_op jit(solution)/shard_map/ppermute | solution.py:432
  48.0 9.7 %collective-permute-start.1 = (f32[128,512]{1,0:T(8,128)S(1)}, f32[128,512]{1,0:T(8,128)S(1)}, u32[]{:S(2)}, u32[]{:S(2)}) collective-permute-start(f32[128,512]{1,0:T(8,128)S(1)} %get-tuple-element.49.refs_12_), channel_id=1, source_target_pairs={{0,8},{1,9},{2,10},{3,11},{4,12},{5,13},{6,14},{7,15},{8,0},{9,1},... | collective-permute-start | bytes 786440 | tf_op jit(solution)/shard_map/ppermute | solution.py:432
  60.6 1.4 %copy-start = (bf16[8,1040,128]{2,1,0:T(8,128)(2,1)}, bf16[8,1040,128]{2,1,0:T(8,128)(2,1)S(1)}, u32[]{:S(2)}) copy-start(bf16[8,1040,128]{2,1,0:T(8,128)(2,1)S(1)} %get-tuple-element.57) | copy-start | bytes 6389764
  62.0 47.4 %all-to-all-start.1 = ((bf16[8,1040,128]{2,1,0:T(8,128)(2,1)}), bf16[8,1040,128]{2,1,0:T(8,128)(2,1)S(1)}, u32[]{:S(2)}, u32[]{:S(2)}) async-start(bf16[8,1040,128]{2,1,0:T(8,128)(2,1)} %copy-done), calls=%async_computation.1 | async-start | bytes 4259840 | tf_op jit(solution)/shard_map/all_to_all | solution.py:427
  66.9 10.4 %collective-permute-start.2 = (f32[8,128]{1,0:T(8,128)S(1)}, f32[8,128]{1,0:T(8,128)S(1)}, u32[]{:S(2)}, u32[]{:S(2)}) collective-permute-start(f32[8,128]{1,0:T(8,128)S(1)} %get-tuple-element.62), channel_id=1, source_target_pairs={{0,8},{1,9},{2,10},{3,11},{4,12},{5,13},{6,14},{7,15},{8,0},{9,1},... | collective-permute-start | bytes 12296 | tf_op jit(solution)/shard_map/ppermute | solution.py:432
  70.1 7.2 %collective-permute-start.3 = (f32[8,128]{1,0:T(8,128)S(1)}, f32[8,128]{1,0:T(8,128)S(1)}, u32[]{:S(2)}, u32[]{:S(2)}) collective-permute-start(f32[8,128]{1,0:T(8,128)S(1)} %get-tuple-element.62), channel_id=1, source_target_pairs={{0,16},{16,0},{32,48},{48,32},{64,80},{80,64},{96,112},{112,96},{1... | collective-permute-start | bytes 12296 | tf_op jit(solution)/shard_map/ppermute | solution.py:441
  72.0 6.9 %collective-permute-start.4 = (f32[8,128]{1,0:T(8,128)S(1)}, f32[8,128]{1,0:T(8,128)S(1)}, u32[]{:S(2)}, u32[]{:S(2)}) collective-permute-start(f32[8,128]{1,0:T(8,128)S(1)} %get-tuple-element.62), channel_id=1, source_target_pairs={{0,24},{1,25},{2,26},{3,27},{4,28},{5,29},{6,30},{7,31},{8,16},{9,... | collective-permute-start | bytes 12296 | tf_op jit(solution)/shard_map/ppermute | solution.py:442
  78.9 5.5 %collective-permute-start.5 = (f32[8,128]{1,0:T(8,128)S(1)}, f32[8,128]{1,0:T(8,128)S(1)}, u32[]{:S(2)}, u32[]{:S(2)}) collective-permute-start(f32[8,128]{1,0:T(8,128)S(1)} %add_add_fusion), channel_id=1, source_target_pairs={{0,32},{16,48},{32,0},{48,16},{64,96},{80,112},{96,64},{112,80},{1... | collective-permute-start | bytes 12296 | tf_op jit(solution)/shard_map/ppermute | solution.py:449

commit v5 on v3

--- a/solution.py
+++ b/solution.py
@@ -14,7 +14,7 @@
 PACK_STEPS = 2
 HALVES = 2
 PER_TILE = LANES // (2 * ROWS)
-UNROLL = 4
+UNROLL = 8
 STATES_VMEM = 24
 LOCAL_VMEM = 24
 FINISH_VMEM = 24
@@ -380,10 +380,10 @@
 
 
 def message_kernel(lay, gh_ref, gl_ref, xh_ref, xl_ref, wide_ref, gx_ref, din_ref, dout_ref,
-                   dstep_ref, uh_ref, ul_ref, more_ref, flag_ref, out_ref):
+                   dstep_ref, uh_ref, ul_ref, more_ref, flag_ref, out_hbm, out_ref, sem):
     width = lay.width
     first = flag_ref[0] == 0
-    out_ref[:, lay.body :] = dstep_ref[...]
+    put = lambda k: pltpu.make_async_copy(out_ref.at[k], out_hbm.at[k], sem.at[k])
 
     def d_keys(k, high_ref, low_ref):
         high, low = high_ref[k], low_ref[k]
@@ -395,6 +395,8 @@
             out_ref[k, j * CHUNK : (j + 1) * CHUNK] = grad_x[:, j * LANES : (j + 1) * LANES]
         for j, part in enumerate(split2(d_in) + split2(d_out)):
             out_ref[k, width + j * CHUNK : width + (j + 1) * CHUNK] = part
+        out_ref[k, lay.body :] = dstep_ref[k]
+        put(k).start()
 
     @pl.when(first)
     def _():
@@ -411,6 +413,9 @@
             return carry
 
         grouped(lay.chunks, one, 0)
+
+    for k in range(lay.chunks):
+        put(k).wait()
 
 
 def message(own, local, finish, flag, lay):
@@ -420,15 +425,19 @@
     return pl.pallas_call(
         lambda *refs: message_kernel(lay, *refs),
         in_specs=[vmem] * 12 + [pl.BlockSpec(memory_space=pltpu.SMEM)],
-        out_specs=vmem,
+        out_specs=pl.BlockSpec(memory_space=pl.ANY),
         out_shape=jax.ShapeDtypeStruct((lay.chunks, lay.body + 16, LANES), bf16),
+        scratch_shapes=[
+            pltpu.VMEM((lay.chunks, lay.body + 16, LANES), bf16),
+            pltpu.SemaphoreType.DMA((lay.chunks,)),
+        ],
         compiler_params=pltpu.CompilerParams(vmem_limit_bytes=FINISH_VMEM * MIB),
         cost_estimate=pl.CostEstimate(flops=400_000_000, bytes_accessed=20_000_000, transcendentals=0),
         name="message",
     )(gh, gl, xh, xl, wide, *local[:3], dstep, uh, ul, more, flag)
 
 
-def unpack_kernel(lay, in_ref, x_ref, s_ref, b_ref, c_ref):
+def unpack_kernel(lay, replicas, in_ref, sums_ref, flag_ref, x_ref, s_ref, b_ref, c_ref, p_ref):
     groups, width = in_ref.shape[0], lay.width
     narrow = width // HALVES
     some = lay.heads // HALVES
@@ -444,20 +453,23 @@
     c_ref[...] = sum(part(n, 2) + part(n, 3) for n in every).astype(bf16)
     picks = [head_pick(16, s_ref.shape[0], n, some, groups) for n in every]
     s_ref[...] = sum(mm_tn(picks[n], in_ref[n, lay.body :]) for n in every).astype(bf16)
-
-
-def unpack(received, lay):
+    mean = sums_ref[:3] / replicas
+    p_ref[...] = jnp.where(flag_ref[0] == 0, mean[:, :some], mean[:, some : 2 * some])
+
+
+def unpack(received, sums, flag, replicas, lay):
     groups = received.shape[0]
     shapes = [(CHUNK, groups * lay.width), (groups * lay.heads, CHUNK), (CHUNK, NSTATE), (CHUNK, NSTATE)]
     vmem = pl.BlockSpec(memory_space=pltpu.VMEM)
     return pl.pallas_call(
-        lambda *refs: unpack_kernel(lay, *refs),
-        in_specs=[vmem],
-        out_specs=[vmem] * 4,
-        out_shape=[jax.ShapeDtypeStruct(s, bf16) for s in shapes],
+        lambda *refs: unpack_kernel(lay, replicas, *refs),
+        in_specs=[vmem, vmem, pl.BlockSpec(memory_space=pltpu.SMEM)],
+        out_specs=[vmem] * 5,
+        out_shape=[jax.ShapeDtypeStruct(s, bf16) for s in shapes]
+        + [jax.ShapeDtypeStruct((3, lay.heads // HALVES), f32)],
         compiler_params=pltpu.CompilerParams(vmem_limit_bytes=24 * MIB),
         name="unpack",
-    )(received)
+    )(received, sums, flag)
 
 
 def exchange(v):
@@ -473,12 +485,12 @@
 
 def near_sum(v):
     replicas, shards = lax.axis_size("dp"), lax.axis_size("seq")
+    v = v + from_partner(v)
     if replicas == 1:
-        return v + from_partner(v)
+        return v
     halves = lambda i: (i + shards // HALVES) % shards
     across = [(r * shards + i, (r ^ 1) * shards + halves(i)) for r in range(replicas) for i in range(shards)]
-    pair = lax.ppermute(v, "dp", [(r, r ^ 1) for r in range(replicas)])
-    return (v + from_partner(v)) + (pair + lax.ppermute(v, ("dp", "seq"), across))
+    return v + lax.ppermute(v, ("dp", "seq"), across)
 
 
 def line_sum(v):
@@ -513,9 +525,8 @@
     finish = scan_finish(received, own, local[3], local[4], came, flag, lay)
     back = message(own, local, finish, flag, lay)
     back, per_head = lax.optimization_barrier((back, near_sum(finish[1])))
-    grad_x, grad_step, grad_write, grad_read = unpack(exchange(back), lay)
-    totals = line_sum(per_head)[:3] / lax.axis_size("dp")
-    totals = jnp.where(first, totals[:, :some], totals[:, some : 2 * some])
+    sums = line_sum(per_head)
+    grad_x, grad_step, grad_write, grad_read, totals = unpack(exchange(back), sums, flag, lax.axis_size("dp"), lay)
     return grad_x[None], grad_step.T[None], grad_write[None], grad_read[None], totals
 
 

time: 108 us -> 107 us (level)
  starting transfers between devices: 30.1 us -> 25.6 us
  waiting for transfers between devices: 34.1 us -> 38.5 us
    ppermute x2 -> x1, starting transfers between devices: 7.63 us -> 1.91 us  [near_sum(): return v + lax.ppermute(v, ('dp', 'seq'), across)]
    ppermute x2 -> x1, waiting for transfers between devices: 0.01 us -> 2.46 us  [near_sum(): return v + lax.ppermute(v, ('dp', 'seq'), across)]
    ppermute x3, waiting for transfers between devices: 4.39 us -> 6.28 us  [from_partner(): lax.ppermute(v, 'seq', [(i, (i + groups) % (2 * groups)) for i in range(2...]
    ppermute x3, starting transfers between devices: 6.02 us -> 7.19 us  [from_partner(): lax.ppermute(v, 'seq', [(i, (i + groups) % (2 * groups)) for i in range(2...]
  transfers between devices with their start and end apart: 8 -> 7, of which waited for: 5 -> 6; matrix products, arithmetic and copies ran while one was open for 1% -> 0% of each run, Pallas kernels for 10% -> 9%
where the time goes in v5:
time: 107 us; the launch traced here: 106 us
  waiting for transfers between devices  38.5 us (36%)
  starting transfers between devices  25.6 us (24%)
  blocking collectives  22.2 us (21%)
  Pallas kernels  19.3 us (18%)
    all_to_all x2, waiting for transfers between devices, exchange(): lax.all_to_all(v, 'seq', split_axis=0, concat_axis=0, tiled=True, axis_in...  26.1 us
    psum x1, blocking collectives, line_sum(): return lax.psum(v, 'dp', axis_index_groups=lines)  22.2 us
    all_to_all x2, starting transfers between devices, exchange(): lax.all_to_all(v, 'seq', split_axis=0, concat_axis=0, tiled=True, axis_in...  14.6 us
    pallas_call x1, Pallas kernels, scan_local(): pl.pallas_call(lambda *refs: local_kernel(lay, *refs), in_specs=[vmem] *...  7.2 us
    ppermute x3, starting transfers between devices, from_partner(): lax.ppermute(v, 'seq', [(i, (i + groups) % (2 * groups)) for i in range(2...  7.19 us
    ppermute x3, waiting for transfers between devices, from_partner(): lax.ppermute(v, 'seq', [(i, (i + groups) % (2 * groups)) for i in range(2...  6.28 us
    ppermute x1, waiting for transfers between devices, line_sum(): v = v + lax.ppermute(v, 'dp', [(i, i ^ 2) for i in range(2 * half)])  3.57 us
    pallas_call x1, Pallas kernels, scan_states(): pl.pallas_call(lambda *refs: states_kernel(lay, *refs), in_specs=[vmem, v...  3.01 us
  transfers between devices with their start and end apart: 7, of which 6 were waited for; matrix products, arithmetic and copies ran while one was open for 0% of the time, Pallas kernels for 9%

profile of v5, /device:TPU:2, one launch (start us, length us, event | category | flops | bytes accessed | tf_op | source)
XLA Modules:
  0.0 106.4 jit_solution(144472354088711047)
XLA Ops:
  0.6 3.0 %pack.1 = bf16[8,1296,128]{2,1,0:T(8,128)(2,1)} custom-call(bf16[128,4096]{1,0:T(8,128)(2,1)} %bitcast.17, bf16[128,4096]{1,0:T(8,128)(2,1)} %bitcast.18, bf16[128,4096]{1,0:T(8,128)(2,1)} %bitcast.19, bf16[128,4096]{1,0:T(8,128)(2,1)} %bitcast.20, bf16[128,128]{1,0:T(8,128)(2,1)} %bitcast.21, bf16[128,128]{1,0:T(8,128)(2,1)} %bitcast.22, ...), custom_call_target="tpu_custom_call" | custom-call | tf_op jit(solution)/shard_map/pack/pallas_call | solution.py:96
  3.6 0.0 copy-start
  3.6 0.0 copy-start.1
  3.6 0.0 copy-start.2
  3.6 9.6 %all-to-all-start = ((bf16[8,1296,128]{2,1,0:T(8,128)(2,1)}), bf16[8,1296,128]{2,1,0:T(8,128)(2,1)S(1)}, u32[]{:S(2)}, u32[]{:S(2)}) async-start(bf16[8,1296,128]{2,1,0:T(8,128)(2,1)} %pack.1), calls=%async_computation | async-start | bytes 5308416 | tf_op jit(solution)/shard_map/all_to_all | solution.py:478
  13.2 0.0 copy-done
  13.2 0.0 copy-done.1
  13.2 0.0 copy-done.2
  13.2 1.9 %collective-permute-start = (f32[3,4]{1,0:T(4,128)S(1)}, f32[3,4]{1,0:T(4,128)S(1)}, u32[]{:S(2)}, u32[]{:S(2)}) collective-permute-start(f32[3,4]{1,0:T(4,128)S(1)} %pad_maximum_fusion), channel_id=1, source_target_pairs={{0,8},{1,9},{2,10},{3,11},{4,12},{5,13},{6,14},{7,15},{8,0},{9,1},... | collective-permute-start | bytes 152 | tf_op jit(solution)/shard_map/ppermute | solution.py:483
  15.2 3.5 %collective-permute-done = f32[3,4]{1,0:T(4,128)S(1)} collective-permute-done((f32[3,4]{1,0:T(4,128)S(1)}, f32[3,4]{1,0:T(4,128)S(1)}, u32[]{:S(2)}, u32[]{:S(2)}) %collective-permute-start) | collective-permute-done | bytes 80 | tf_op jit(solution)/shard_map/ppermute | solution.py:483
  18.7 0.1 select_maximum_fusion.refs_1_
  18.8 26.1 %all-to-all-done.refs_0_ = bf16[8,1296,128]{2,1,0:T(8,128)(2,1)S(1)} async-done(((bf16[8,1296,128]{2,1,0:T(8,128)(2,1)}), bf16[8,1296,128]{2,1,0:T(8,128)(2,1)S(1)}, u32[]{:S(2)}, u32[]{:S(2)}) %all-to-all-start) | async-done | bytes 2654240 | tf_op jit(solution)/shard_map/all_to_all | solution.py:478
  44.9 3.0 %scan_states.1 = (bf16[8,128,512]{2,1,0:T(8,128)(2,1)S(1)}, bf16[8,128,512]{2,1,0:T(8,128)(2,1)S(1)}, bf16[8,128,512]{2,1,0:T(8,128)(2,1)S(1)}, bf16[8,128,512]{...) custom-call(bf16[8,1296,128]{2,1,0:T(8,128)(2,1)S(1)} %all-to-all-do, ...), custom_call_target="tpu_custom_call" | custom-call | tf_op jit(solution)/shard_map/scan_states/pallas_call | solution.py:230
  48.0 1.9 %collective-permute-start.1 = (f32[128,512]{1,0:T(8,128)S(1)}, f32[128,512]{1,0:T(8,128)S(1)}, u32[]{:S(2)}, u32[]{:S(2)}) collective-permute-start(f32[128,512]{1,0:T(8,128)S(1)} %get-tuple-element.60.refs_11_), channel_id=1, source_target_pairs={{0,8},{1,9},{2,10},{3,11},{4,12},{5,13},{6,14},{7,15},{8,0},{9,1},... | collective-permute-start | bytes 786440 | tf_op jit(solution)/shard_map/ppermute | solution.py:483
  49.9 7.2 %scan_local.1 = (f32[8,128,512]{2,1,0:T(8,128)S(1)}, f32[8,128,128]{2,1,0:T(8,128)S(1)}, f32[8,128,128]{2,1,0:T(8,128)S(1)}, f32[8,8,128]{2,1,0:T(8,128)S(1)}, f32[8,8,128]{2,1,0:T(8,128)S(1)}) custom-call(bf16[8,1296,128]{2,1,0:T(8,128)(2,1)S(1)} %all-to-all-done.refs_0_, bf16[8,128,512]{2,1,0:T(8,128)(2,1)S(1)} %get-tuple-element.44.refs_1_.refs_0_, ...), custom_call_target="tpu_custom_call" | custom-call | tf_op jit(solution)/shard_map/scan_local/pallas_call | solution.py:285
  57.1 0.6 collective-permute-done.1.refs_12_
  57.7 2.4 %scan_finish.1 = (bf16[8,16,128]{2,1,0:T(8,128)(2,1)S(1)}, f32[8,128]{1,0:T(8,128)S(1)}, bf16[8,128,512]{2,1,0:T(8,128)(2,1)S(1)}, bf16[8,128,512]{2,1,0:T(8,128)(2,1)S(1)}, f32[8,128,512]{2,1,0:T(8,128)S(1)}) custom-call(bf16[8,1296,128]{2,1,0:T(8,128)(2,1)S(1)} %all-to-all-done.refs_0_, bf16[8,128,512]{2,1,0:T(8,128)(2,1)S(1)} %get-tuple-element.44.refs_1_.refs_0_, ...), custom_call_target="tpu_custom_call" | custom-call | tf_op jit(solution)/shard_map/scan_finish/pallas_call | solution.py:370
  60.1 3.4 %collective-permute-start.2 = (f32[8,128]{1,0:T(8,128)S(1)}, f32[8,128]{1,0:T(8,128)S(1)}, u32[]{:S(2)}, u32[]{:S(2)}) collective-permute-start(f32[8,128]{1,0:T(8,128)S(1)} %get-tuple-element.67), channel_id=1, source_target_pairs={{0,8},{1,9},{2,10},{3,11},{4,12},{5,13},{6,14},{7,15},{8,0},{9,1},... | collective-permute-start | bytes 12296 | tf_op jit(solution)/shard_map/ppermute | solution.py:483
  63.5 2.1 %collective-permute-done.2 = f32[8,128]{1,0:T(8,128)S(1)} collective-permute-done((f32[8,128]{1,0:T(8,128)S(1)}, f32[8,128]{1,0:T(8,128)S(1)}, u32[]{:S(2)}, u32[]{:S(2)}) %collective-permute-start.2) | collective-permute-done | bytes 4128 | tf_op jit(solution)/shard_map/ppermute | solution.py:483
  65.6 1.9 %collective-permute-start.3 = (f32[8,128]{1,0:T(8,128)S(1)}, f32[8,128]{1,0:T(8,128)S(1)}, u32[]{:S(2)}, u32[]{:S(2)}) collective-permute-start(f32[8,128]{1,0:T(8,128)S(1)} %add.14), channel_id=1, source_target_pairs={{0,24},{1,25},{2,26},{3,27},{4,28},{5,29},{6,30},{7,31},{8,16},{9,... | collective-permute-start | bytes 12296 | tf_op jit(solution)/shard_map/ppermute | solution.py:493
  67.5 2.3 %message.1 = bf16[8,1040,128]{2,1,0:T(8,128)(2,1)} custom-call(bf16[8,128,512]{2,1,0:T(8,128)(2,1)S(1)} %get-tuple-element.44.refs_1_.refs_0_, bf16[8,128,512]{2,1,0:T(8,128)(2,1)S(1)} %get-tuple-element.45.refs_2_.refs_1_, bf16[8,128,512]{2,1,0:T(8,128)(2,1)S(1)} %get-tuple-element.46.refs_3_.refs_2_, ...), custom_call_target="tpu_custom_call" | custom-call | flops 400000000 | bytes 20000000 | tf_op jit(solution)/shard_map/message/pallas_call | solution.py:425
  69.8 2.5 %collective-permute-done.3 = f32[8,128]{1,0:T(8,128)S(1)} collective-permute-done((f32[8,128]{1,0:T(8,128)S(1)}, f32[8,128]{1,0:T(8,128)S(1)}, u32[]{:S(2)}, u32[]{:S(2)}) %collective-permute-start.3) | collective-permute-done | bytes 4128 | tf_op jit(solution)/shard_map/ppermute | solution.py:493
  72.3 5.0 %all-to-all-start.1 = ((bf16[8,1040,128]{2,1,0:T(8,128)(2,1)}), bf16[8,1040,128]{2,1,0:T(8,128)(2,1)S(1)}, u32[]{:S(2)}, u32[]{:S(2)}) async-start(bf16[8,1040,128]{2,1,0:T(8,128)(2,1)} %message.1), calls=%async_computation.1 | async-start | bytes 4259840 | tf_op jit(solution)/shard_map/all_to_all | solution.py:478
  77.3 1.9 %collective-permute-start.4 = (f32[8,128]{1,0:T(8,128)S(1)}, f32[8,128]{1,0:T(8,128)S(1)}, u32[]{:S(2)}, u32[]{:S(2)}) collective-permute-start(f32[8,128]{1,0:T(8,128)S(1)} %add.15), channel_id=1, source_target_pairs={{0,32},{16,48},{32,0},{48,16},{64,96},{80,112},{96,64},{112,80},{1... | collective-permute-start | bytes 12296 | tf_op jit(solution)/shard_map/ppermute | solution.py:500
  79.2 3.6 %collective-permute-done.4 = f32[8,128]{1,0:T(8,128)S(1)} collective-permute-done((f32[8,128]{1,0:T(8,128)S(1)}, f32[8,128]{1,0:T(8,128)S(1)}, u32[]{:S(2)}, u32[]{:S(2)}) %collective-permute-start.4) | collective-permute-done | bytes 4128 | tf_op jit(solution)/shard_map/ppermute | solution.py:500
  82.8 22.2 %psum.7.refs_1_ = f32[8,128]{1,0:T(8,128)S(1)} all-reduce(f32[8,128]{1,0:T(8,128)S(1)} %add.16), channel_id=1, replica_groups={{0,64,128,192,256,320,384,448},{16,80,144,208,272,336,400,464},{32,96,1..., use_global_device_ids=true, to_apply=%region_0.1 | all-reduce | flops 1024 | bytes 8192 | tf_op jit(solution)/shard_map/psum | solution.py:504
  105.0 0.0 all-to-all-done.1.refs_0_
  105.0 1.4 %unpack.1 = (bf16[128,4096]{1,0:T(8,128)(2,1)}, bf16[64,128]{1,0:T(8,128)(2,1)}, bf16[128,128]{1,0:T(8,128)(2,1)}, bf16[128,128]{1,0:T(8,128)(2,1)}, f32[3,4]{1,0:T(4,128)}) custom-call(bf16[8,1040,128]{2,1,0:T(8,128)(2,1)S(1)} %all-to-all-done.1.refs_0_, f32[8,128]{1,0:T(8,128)S(1)} %psum.7.refs_1_, s32[1]{0:T(128)} %bitcast.9.refs_2_.refs_15_.refs_12_), custom_call_target="tpu_custom_call" | custom-call | tf_op jit(solution)/shard_map/unpack/pallas_call | solution.py:464
  (5 shorter events, 0.0 us)
Async XLA Ops:
  3.6 9.6 %copy-start = (f32[4]{0:T(128)S(1)}, f32[4]{0:T(128)}, u32[]{:S(2)}) copy-start(f32[4]{0:T(128)} %param.15) | copy-start | bytes 52
  3.6 9.6 %copy-start.1 = (f32[4]{0:T(128)S(1)}, f32[4]{0:T(128)}, u32[]{:S(2)}) copy-start(f32[4]{0:T(128)} %param.14) | copy-start | bytes 52
  3.6 9.6 %copy-start.2 = (f32[4]{0:T(128)S(1)}, f32[4]{0:T(128)}, u32[]{:S(2)}) copy-start(f32[4]{0:T(128)} %param.13) | copy-start | bytes 52
  3.6 41.3 %all-to-all-start = ((bf16[8,1296,128]{2,1,0:T(8,128)(2,1)}), bf16[8,1296,128]{2,1,0:T(8,128)(2,1)S(1)}, u32[]{:S(2)}, u32[]{:S(2)}) async-start(bf16[8,1296,128]{2,1,0:T(8,128)(2,1)} %pack.1), calls=%async_computation | async-start | bytes 5308416 | tf_op jit(solution)/shard_map/all_to_all | solution.py:478
  13.2 5.5 %collective-permute-start = (f32[3,4]{1,0:T(4,128)S(1)}, f32[3,4]{1,0:T(4,128)S(1)}, u32[]{:S(2)}, u32[]{:S(2)}) collective-permute-start(f32[3,4]{1,0:T(4,128)S(1)} %pad_maximum_fusion), channel_id=1, source_target_pairs={{0,8},{1,9},{2,10},{3,11},{4,12},{5,13},{6,14},{7,15},{8,0},{9,1},... | collective-permute-start | bytes 152 | tf_op jit(solution)/shard_map/ppermute | solution.py:483
  48.0 9.7 %collective-permute-start.1 = (f32[128,512]{1,0:T(8,128)S(1)}, f32[128,512]{1,0:T(8,128)S(1)}, u32[]{:S(2)}, u32[]{:S(2)}) collective-permute-start(f32[128,512]{1,0:T(8,128)S(1)} %get-tuple-element.60.refs_11_), channel_id=1, source_target_pairs={{0,8},{1,9},{2,10},{3,11},{4,12},{5,13},{6,14},{7,15},{8,0},{9,1},... | collective-permute-start | bytes 786440 | tf_op jit(solution)/shard_map/ppermute | solution.py:483
  60.1 5.5 %collective-permute-start.2 = (f32[8,128]{1,0:T(8,128)S(1)}, f32[8,128]{1,0:T(8,128)S(1)}, u32[]{:S(2)}, u32[]{:S(2)}) collective-permute-start(f32[8,128]{1,0:T(8,128)S(1)} %get-tuple-element.67), channel_id=1, source_target_pairs={{0,8},{1,9},{2,10},{3,11},{4,12},{5,13},{6,14},{7,15},{8,0},{9,1},... | collective-permute-start | bytes 12296 | tf_op jit(solution)/shard_map/ppermute | solution.py:483
  65.6 6.7 %collective-permute-start.3 = (f32[8,128]{1,0:T(8,128)S(1)}, f32[8,128]{1,0:T(8,128)S(1)}, u32[]{:S(2)}, u32[]{:S(2)}) collective-permute-start(f32[8,128]{1,0:T(8,128)S(1)} %add.14), channel_id=1, source_target_pairs={{0,24},{1,25},{2,26},{3,27},{4,28},{5,29},{6,30},{7,31},{8,16},{9,... | collective-permute-start | bytes 12296 | tf_op jit(solution)/shard_map/ppermute | solution.py:493
  72.3 32.7 %all-to-all-start.1 = ((bf16[8,1040,128]{2,1,0:T(8,128)(2,1)}), bf16[8,1040,128]{2,1,0:T(8,128)(2,1)S(1)}, u32[]{:S(2)}, u32[]{:S(2)}) async-start(bf16[8,1040,128]{2,1,0:T(8,128)(2,1)} %message.1), calls=%async_computation.1 | async-start | bytes 4259840 | tf_op jit(solution)/shard_map/all_to_all | solution.py:478
  77.3 5.5 %collective-permute-start.4 = (f32[8,128]{1,0:T(8,128)S(1)}, f32[8,128]{1,0:T(8,128)S(1)}, u32[]{:S(2)}, u32[]{:S(2)}) collective-permute-start(f32[8,128]{1,0:T(8,128)S(1)} %add.15), channel_id=1, source_target_pairs={{0,32},{16,48},{32,0},{48,16},{64,96},{80,112},{96,64},{112,80},{1... | collective-permute-start | bytes 12296 | tf_op jit(solution)/shard_map/ppermute | solution.py:500

commit v6 on v5

--- a/solution.py
+++ b/solution.py
@@ -483,9 +483,8 @@
     return lax.ppermute(v, "seq", [(i, (i + groups) % (2 * groups)) for i in range(2 * groups)])
 
 
-def near_sum(v):
+def across_sum(v):
     replicas, shards = lax.axis_size("dp"), lax.axis_size("seq")
-    v = v + from_partner(v)
     if replicas == 1:
         return v
     halves = lambda i: (i + shards // HALVES) % shards
@@ -524,8 +523,9 @@
     local = scan_local(received, own, lay)
     finish = scan_finish(received, own, local[3], local[4], came, flag, lay)
     back = message(own, local, finish, flag, lay)
-    back, per_head = lax.optimization_barrier((back, near_sum(finish[1])))
-    sums = line_sum(per_head)
+    per_head = finish[1] + from_partner(finish[1])
+    back, per_head = lax.optimization_barrier((back, per_head))
+    sums = line_sum(across_sum(per_head))
     grad_x, grad_step, grad_write, grad_read, totals = unpack(exchange(back), sums, flag, lax.axis_size("dp"), lay)
     return grad_x[None], grad_step.T[None], grad_write[None], grad_read[None], totals
 

time: 107 us -> 107 us (level)
    ppermute x1, waiting for transfers between devices: 2.46 us -> 4.78 us  [across_sum(): return v + lax.ppermute(v, ('dp', 'seq'), across)]
    ppermute x3, waiting for transfers between devices: 6.28 us -> 4.15 us  [from_partner(): lax.ppermute(v, 'seq', [(i, (i + groups) % (2 * groups)) for i in range(2...]
  transfers between devices with their start and end apart: 7 -> 7, of which waited for: 6 -> 5; matrix products, arithmetic and copies ran while one was open for 0% -> 0% of each run, Pallas kernels for 9% -> 9%
where the time goes in v6:
time: 107 us; the launch traced here: 106 us
  waiting for transfers between devices  38.6 us (36%)
  starting transfers between devices  25.6 us (24%)
  blocking collectives  22 us (21%)
  Pallas kernels  19.3 us (18%)
    all_to_all x2, waiting for transfers between devices, exchange(): lax.all_to_all(v, 'seq', split_axis=0, concat_axis=0, tiled=True, axis_in...  26.1 us
    psum x1, blocking collectives, line_sum(): return lax.psum(v, 'dp', axis_index_groups=lines)  22 us
    all_to_all x2, starting transfers between devices, exchange(): lax.all_to_all(v, 'seq', split_axis=0, concat_axis=0, tiled=True, axis_in...  14.6 us
    pallas_call x1, Pallas kernels, scan_local(): pl.pallas_call(lambda *refs: local_kernel(lay, *refs), in_specs=[vmem] *...  7.2 us
    ppermute x3, starting transfers between devices, from_partner(): lax.ppermute(v, 'seq', [(i, (i + groups) % (2 * groups)) for i in range(2...  7.19 us
    ppermute x1, waiting for transfers between devices, across_sum(): return v + lax.ppermute(v, ('dp', 'seq'), across)  4.78 us
    ppermute x3, waiting for transfers between devices, from_partner(): lax.ppermute(v, 'seq', [(i, (i + groups) % (2 * groups)) for i in range(2...  4.15 us
    ppermute x1, waiting for transfers between devices, line_sum(): v = v + lax.ppermute(v, 'dp', [(i, i ^ 2) for i in range(2 * half)])  3.57 us
  transfers between devices with their start and end apart: 7, of which 5 were waited for; matrix products, arithmetic and copies ran while one was open for 0% of the time, Pallas kernels for 9%

profile of v6, /device:TPU:2, one launch (start us, length us, event | category | flops | bytes accessed | tf_op | source)
XLA Modules:
  0.0 106.4 jit_solution(18166163197105410602)
XLA Ops:
  0.6 3.0 %pack.1 = bf16[8,1296,128]{2,1,0:T(8,128)(2,1)} custom-call(bf16[128,4096]{1,0:T(8,128)(2,1)} %bitcast.17, bf16[128,4096]{1,0:T(8,128)(2,1)} %bitcast.18, bf16[128,4096]{1,0:T(8,128)(2,1)} %bitcast.19, bf16[128,4096]{1,0:T(8,128)(2,1)} %bitcast.20, bf16[128,128]{1,0:T(8,128)(2,1)} %bitcast.21, bf16[128,128]{1,0:T(8,128)(2,1)} %bitcast.22, ...), custom_call_target="tpu_custom_call" | custom-call | tf_op jit(solution)/shard_map/pack/pallas_call | solution.py:96
  3.6 0.0 copy-start
  3.6 0.0 copy-start.1
  3.6 0.0 copy-start.2
  3.6 9.6 %all-to-all-start = ((bf16[8,1296,128]{2,1,0:T(8,128)(2,1)}), bf16[8,1296,128]{2,1,0:T(8,128)(2,1)S(1)}, u32[]{:S(2)}, u32[]{:S(2)}) async-start(bf16[8,1296,128]{2,1,0:T(8,128)(2,1)} %pack.1), calls=%async_computation | async-start | bytes 5308416 | tf_op jit(solution)/shard_map/all_to_all | solution.py:478
  13.2 0.0 copy-done
  13.2 0.0 copy-done.1
  13.2 0.0 copy-done.2
  13.2 1.9 %collective-permute-start = (f32[3,4]{1,0:T(4,128)S(1)}, f32[3,4]{1,0:T(4,128)S(1)}, u32[]{:S(2)}, u32[]{:S(2)}) collective-permute-start(f32[3,4]{1,0:T(4,128)S(1)} %pad_maximum_fusion), channel_id=1, source_target_pairs={{0,8},{1,9},{2,10},{3,11},{4,12},{5,13},{6,14},{7,15},{8,0},{9,1},... | collective-permute-start | bytes 152 | tf_op jit(solution)/shard_map/ppermute | solution.py:483
  15.2 3.5 %collective-permute-done = f32[3,4]{1,0:T(4,128)S(1)} collective-permute-done((f32[3,4]{1,0:T(4,128)S(1)}, f32[3,4]{1,0:T(4,128)S(1)}, u32[]{:S(2)}, u32[]{:S(2)}) %collective-permute-start) | collective-permute-done | bytes 80 | tf_op jit(solution)/shard_map/ppermute | solution.py:483
  18.7 0.1 select_maximum_fusion.refs_1_
  18.8 26.1 %all-to-all-done.refs_0_ = bf16[8,1296,128]{2,1,0:T(8,128)(2,1)S(1)} async-done(((bf16[8,1296,128]{2,1,0:T(8,128)(2,1)}), bf16[8,1296,128]{2,1,0:T(8,128)(2,1)S(1)}, u32[]{:S(2)}, u32[]{:S(2)}) %all-to-all-start) | async-done | bytes 2654240 | tf_op jit(solution)/shard_map/all_to_all | solution.py:478
  44.9 3.0 %scan_states.1 = (bf16[8,128,512]{2,1,0:T(8,128)(2,1)S(1)}, bf16[8,128,512]{2,1,0:T(8,128)(2,1)S(1)}, bf16[8,128,512]{2,1,0:T(8,128)(2,1)S(1)}, bf16[8,128,512]{...) custom-call(bf16[8,1296,128]{2,1,0:T(8,128)(2,1)S(1)} %all-to-all-do, ...), custom_call_target="tpu_custom_call" | custom-call | tf_op jit(solution)/shard_map/scan_states/pallas_call | solution.py:230
  48.0 1.9 %collective-permute-start.1 = (f32[128,512]{1,0:T(8,128)S(1)}, f32[128,512]{1,0:T(8,128)S(1)}, u32[]{:S(2)}, u32[]{:S(2)}) collective-permute-start(f32[128,512]{1,0:T(8,128)S(1)} %get-tuple-element.60.refs_11_), channel_id=1, source_target_pairs={{0,8},{1,9},{2,10},{3,11},{4,12},{5,13},{6,14},{7,15},{8,0},{9,1},... | collective-permute-start | bytes 786440 | tf_op jit(solution)/shard_map/ppermute | solution.py:483
  49.9 7.2 %scan_local.1 = (f32[8,128,512]{2,1,0:T(8,128)S(1)}, f32[8,128,128]{2,1,0:T(8,128)S(1)}, f32[8,128,128]{2,1,0:T(8,128)S(1)}, f32[8,8,128]{2,1,0:T(8,128)S(1)}, f32[8,8,128]{2,1,0:T(8,128)S(1)}) custom-call(bf16[8,1296,128]{2,1,0:T(8,128)(2,1)S(1)} %all-to-all-done.refs_0_, bf16[8,128,512]{2,1,0:T(8,128)(2,1)S(1)} %get-tuple-element.44.refs_1_.refs_0_, ...), custom_call_target="tpu_custom_call" | custom-call | tf_op jit(solution)/shard_map/scan_local/pallas_call | solution.py:285
  57.1 0.6 collective-permute-done.1.refs_12_
  57.7 2.4 %scan_finish.1 = (bf16[8,16,128]{2,1,0:T(8,128)(2,1)S(1)}, f32[8,128]{1,0:T(8,128)S(1)}, bf16[8,128,512]{2,1,0:T(8,128)(2,1)S(1)}, bf16[8,128,512]{2,1,0:T(8,128)(2,1)S(1)}, f32[8,128,512]{2,1,0:T(8,128)S(1)}) custom-call(bf16[8,1296,128]{2,1,0:T(8,128)(2,1)S(1)} %all-to-all-done.refs_0_, bf16[8,128,512]{2,1,0:T(8,128)(2,1)S(1)} %get-tuple-element.44.refs_1_.refs_0_, ...), custom_call_target="tpu_custom_call" | custom-call | tf_op jit(solution)/shard_map/scan_finish/pallas_call | solution.py:370
  60.1 3.4 %collective-permute-start.2 = (f32[8,128]{1,0:T(8,128)S(1)}, f32[8,128]{1,0:T(8,128)S(1)}, u32[]{:S(2)}, u32[]{:S(2)}) collective-permute-start(f32[8,128]{1,0:T(8,128)S(1)} %get-tuple-element.67), channel_id=1, source_target_pairs={{0,8},{1,9},{2,10},{3,11},{4,12},{5,13},{6,14},{7,15},{8,0},{9,1},... | collective-permute-start | bytes 12296 | tf_op jit(solution)/shard_map/ppermute | solution.py:483
  63.5 2.3 %message.1 = bf16[8,1040,128]{2,1,0:T(8,128)(2,1)} custom-call(bf16[8,128,512]{2,1,0:T(8,128)(2,1)S(1)} %get-tuple-element.44.refs_1_.refs_0_, bf16[8,128,512]{2,1,0:T(8,128)(2,1)S(1)} %get-tuple-element.45.refs_2_.refs_1_, bf16[8,128,512]{2,1,0:T(8,128)(2,1)S(1)} %get-tuple-element.46.refs_3_.refs_2_, ...), custom_call_target="tpu_custom_call" | custom-call | flops 400000000 | bytes 20000000 | tf_op jit(solution)/shard_map/message/pallas_call | solution.py:425
  65.8 0.0 collective-permute-done.2
  65.8 5.0 %all-to-all-start.1 = ((bf16[8,1040,128]{2,1,0:T(8,128)(2,1)}), bf16[8,1040,128]{2,1,0:T(8,128)(2,1)S(1)}, u32[]{:S(2)}, u32[]{:S(2)}) async-start(bf16[8,1040,128]{2,1,0:T(8,128)(2,1)} %message.1), calls=%async_computation.1 | async-start | bytes 4259840 | tf_op jit(solution)/shard_map/all_to_all | solution.py:478
  70.8 1.9 %collective-permute-start.3 = (f32[8,128]{1,0:T(8,128)S(1)}, f32[8,128]{1,0:T(8,128)S(1)}, u32[]{:S(2)}, u32[]{:S(2)}) collective-permute-start(f32[8,128]{1,0:T(8,128)S(1)} %add.14), channel_id=1, source_target_pairs={{0,24},{1,25},{2,26},{3,27},{4,28},{5,29},{6,30},{7,31},{8,16},{9,... | collective-permute-start | bytes 12296 | tf_op jit(solution)/shard_map/ppermute | solution.py:492
  72.7 4.8 %collective-permute-done.3 = f32[8,128]{1,0:T(8,128)S(1)} collective-permute-done((f32[8,128]{1,0:T(8,128)S(1)}, f32[8,128]{1,0:T(8,128)S(1)}, u32[]{:S(2)}, u32[]{:S(2)}) %collective-permute-start.3) | collective-permute-done | bytes 4128 | tf_op jit(solution)/shard_map/ppermute | solution.py:492
  77.5 1.9 %collective-permute-start.4 = (f32[8,128]{1,0:T(8,128)S(1)}, f32[8,128]{1,0:T(8,128)S(1)}, u32[]{:S(2)}, u32[]{:S(2)}) collective-permute-start(f32[8,128]{1,0:T(8,128)S(1)} %add.15), channel_id=1, source_target_pairs={{0,32},{16,48},{32,0},{48,16},{64,96},{80,112},{96,64},{112,80},{1... | collective-permute-start | bytes 12296 | tf_op jit(solution)/shard_map/ppermute | solution.py:499
  79.4 3.6 %collective-permute-done.4 = f32[8,128]{1,0:T(8,128)S(1)} collective-permute-done((f32[8,128]{1,0:T(8,128)S(1)}, f32[8,128]{1,0:T(8,128)S(1)}, u32[]{:S(2)}, u32[]{:S(2)}) %collective-permute-start.4) | collective-permute-done | bytes 4128 | tf_op jit(solution)/shard_map/ppermute | solution.py:499
  83.0 22.0 %psum.7.refs_1_ = f32[8,128]{1,0:T(8,128)S(1)} all-reduce(f32[8,128]{1,0:T(8,128)S(1)} %add.16), channel_id=1, replica_groups={{0,64,128,192,256,320,384,448},{16,80,144,208,272,336,400,464},{32,96,1..., use_global_device_ids=true, to_apply=%region_0.1 | all-reduce | flops 1024 | bytes 8192 | tf_op jit(solution)/shard_map/psum | solution.py:503
  105.0 0.0 all-to-all-done.1.refs_0_
  105.0 1.4 %unpack.1 = (bf16[128,4096]{1,0:T(8,128)(2,1)}, bf16[64,128]{1,0:T(8,128)(2,1)}, bf16[128,128]{1,0:T(8,128)(2,1)}, bf16[128,128]{1,0:T(8,128)(2,1)}, f32[3,4]{1,0:T(4,128)}) custom-call(bf16[8,1040,128]{2,1,0:T(8,128)(2,1)S(1)} %all-to-all-done.1.refs_0_, f32[8,128]{1,0:T(8,128)S(1)} %psum.7.refs_1_, s32[1]{0:T(128)} %bitcast.9.refs_2_.refs_15_.refs_12_), custom_call_target="tpu_custom_call" | custom-call | tf_op jit(solution)/shard_map/unpack/pallas_call | solution.py:464
  (5 shorter events, 0.0 us)
Async XLA Ops:
  3.6 9.6 %copy-start = (f32[4]{0:T(128)S(1)}, f32[4]{0:T(128)}, u32[]{:S(2)}) copy-start(f32[4]{0:T(128)} %param.15) | copy-start | bytes 52
  3.6 9.6 %copy-start.1 = (f32[4]{0:T(128)S(1)}, f32[4]{0:T(128)}, u32[]{:S(2)}) copy-start(f32[4]{0:T(128)} %param.14) | copy-start | bytes 52
  3.6 9.6 %copy-start.2 = (f32[4]{0:T(128)S(1)}, f32[4]{0:T(128)}, u32[]{:S(2)}) copy-start(f32[4]{0:T(128)} %param.13) | copy-start | bytes 52
  3.6 41.3 %all-to-all-start = ((bf16[8,1296,128]{2,1,0:T(8,128)(2,1)}), bf16[8,1296,128]{2,1,0:T(8,128)(2,1)S(1)}, u32[]{:S(2)}, u32[]{:S(2)}) async-start(bf16[8,1296,128]{2,1,0:T(8,128)(2,1)} %pack.1), calls=%async_computation | async-start | bytes 5308416 | tf_op jit(solution)/shard_map/all_to_all | solution.py:478
  13.2 5.5 %collective-permute-start = (f32[3,4]{1,0:T(4,128)S(1)}, f32[3,4]{1,0:T(4,128)S(1)}, u32[]{:S(2)}, u32[]{:S(2)}) collective-permute-start(f32[3,4]{1,0:T(4,128)S(1)} %pad_maximum_fusion), channel_id=1, source_target_pairs={{0,8},{1,9},{2,10},{3,11},{4,12},{5,13},{6,14},{7,15},{8,0},{9,1},... | collective-permute-start | bytes 152 | tf_op jit(solution)/shard_map/ppermute | solution.py:483
  48.0 9.7 %collective-permute-start.1 = (f32[128,512]{1,0:T(8,128)S(1)}, f32[128,512]{1,0:T(8,128)S(1)}, u32[]{:S(2)}, u32[]{:S(2)}) collective-permute-start(f32[128,512]{1,0:T(8,128)S(1)} %get-tuple-element.60.refs_11_), channel_id=1, source_target_pairs={{0,8},{1,9},{2,10},{3,11},{4,12},{5,13},{6,14},{7,15},{8,0},{9,1},... | collective-permute-start | bytes 786440 | tf_op jit(solution)/shard_map/ppermute | solution.py:483
  60.1 5.7 %collective-permute-start.2 = (f32[8,128]{1,0:T(8,128)S(1)}, f32[8,128]{1,0:T(8,128)S(1)}, u32[]{:S(2)}, u32[]{:S(2)}) collective-permute-start(f32[8,128]{1,0:T(8,128)S(1)} %get-tuple-element.67), channel_id=1, source_target_pairs={{0,8},{1,9},{2,10},{3,11},{4,12},{5,13},{6,14},{7,15},{8,0},{9,1},... | collective-permute-start | bytes 12296 | tf_op jit(solution)/shard_map/ppermute | solution.py:483
  65.8 39.2 %all-to-all-start.1 = ((bf16[8,1040,128]{2,1,0:T(8,128)(2,1)}), bf16[8,1040,128]{2,1,0:T(8,128)(2,1)S(1)}, u32[]{:S(2)}, u32[]{:S(2)}) async-start(bf16[8,1040,128]{2,1,0:T(8,128)(2,1)} %message.1), calls=%async_computation.1 | async-start | bytes 4259840 | tf_op jit(solution)/shard_map/all_to_all | solution.py:478
  70.8 6.7 %collective-permute-start.3 = (f32[8,128]{1,0:T(8,128)S(1)}, f32[8,128]{1,0:T(8,128)S(1)}, u32[]{:S(2)}, u32[]{:S(2)}) collective-permute-start(f32[8,128]{1,0:T(8,128)S(1)} %add.14), channel_id=1, source_target_pairs={{0,24},{1,25},{2,26},{3,27},{4,28},{5,29},{6,30},{7,31},{8,16},{9,... | collective-permute-start | bytes 12296 | tf_op jit(solution)/shard_map/ppermute | solution.py:492
  77.5 5.5 %collective-permute-start.4 = (f32[8,128]{1,0:T(8,128)S(1)}, f32[8,128]{1,0:T(8,128)S(1)}, u32[]{:S(2)}, u32[]{:S(2)}) collective-permute-start(f32[8,128]{1,0:T(8,128)S(1)} %add.15), channel_id=1, source_target_pairs={{0,32},{16,48},{32,0},{48,16},{64,96},{80,112},{96,64},{112,80},{1... | collective-permute-start | bytes 12296 | tf_op jit(solution)/shard_map/ppermute | solution.py:499

commit v7 on v6

--- a/solution.py
+++ b/solution.py
@@ -483,21 +483,24 @@
     return lax.ppermute(v, "seq", [(i, (i + groups) % (2 * groups)) for i in range(2 * groups)])
 
 
-def across_sum(v):
+def near_sum(v):
     replicas, shards = lax.axis_size("dp"), lax.axis_size("seq")
     if replicas == 1:
         return v
     halves = lambda i: (i + shards // HALVES) % shards
-    across = [(r * shards + i, (r ^ 1) * shards + halves(i)) for r in range(replicas) for i in range(shards)]
-    return v + lax.ppermute(v, ("dp", "seq"), across)
+
+    def across(bits):
+        pairs = [(r * shards + i, (r ^ bits) * shards + halves(i)) for r in range(replicas) for i in range(shards)]
+        return lax.ppermute(v, ("dp", "seq"), pairs)
+
+    if replicas == 2:
+        return v + across(1)
+    return (v + across(1)) + (lax.ppermute(v, "dp", [(r, r ^ 2) for r in range(replicas)]) + across(3))
 
 
 def line_sum(v):
     half = lax.axis_size("dp") // 2
-    if half <= 1:
-        return v
-    v = v + lax.ppermute(v, "dp", [(i, i ^ 2) for i in range(2 * half)])
-    if half == 2:
+    if half <= 2:
         return v
     lines = [[2 * i + bit for i in range(odd, half, 2)] for odd in range(2) for bit in range(2)]
     return lax.psum(v, "dp", axis_index_groups=lines)
@@ -525,7 +528,7 @@
     back = message(own, local, finish, flag, lay)
     per_head = finish[1] + from_partner(finish[1])
     back, per_head = lax.optimization_barrier((back, per_head))
-    sums = line_sum(across_sum(per_head))
+    sums = line_sum(near_sum(per_head))
     grad_x, grad_step, grad_write, grad_read, totals = unpack(exchange(back), sums, flag, lax.axis_size("dp"), lay)
     return grad_x[None], grad_step.T[None], grad_write[None], grad_read[None], totals
 

time: 107 us -> 109 us (1.019)
  waiting for transfers between devices: 38.6 us -> 31.9 us
  starting transfers between devices: 25.6 us -> 32.1 us
  blocking collectives: 22 us -> 24.2 us
    ppermute x2 -> x3, waiting for transfers between devices: 8.36 us -> 1.56 us  [the longest x2 1.55 us: across(): return lax.ppermute(v, ('dp', 'seq'), pairs)]
    ppermute x2 -> x3, starting transfers between devices: 3.82 us -> 10.4 us  [the longest x2 8.49 us: across(): return lax.ppermute(v, ('dp', 'seq'), pairs)]
    psum x1, blocking collectives: 22 us -> 24.2 us  [line_sum(): return lax.psum(v, 'dp', axis_index_groups=lines)]
  transfers between devices with their start and end apart: 7 -> 8, of which waited for: 5 -> 4; matrix products, arithmetic and copies ran while one was open for 0% -> 0% of each run, Pallas kernels for 9% -> 9%
where the time goes in v7:
time: 109 us; the launch traced here: 108 us
  starting transfers between devices  32.1 us (29%)
  waiting for transfers between devices  31.9 us (29%)
  blocking collectives  24.2 us (22%)
  Pallas kernels  19.3 us (18%)
    all_to_all x2, waiting for transfers between devices, exchange(): lax.all_to_all(v, 'seq', split_axis=0, concat_axis=0, tiled=True, axis_in...  26.1 us
    psum x1, blocking collectives, line_sum(): return lax.psum(v, 'dp', axis_index_groups=lines)  24.2 us
    all_to_all x2, starting transfers between devices, exchange(): lax.all_to_all(v, 'seq', split_axis=0, concat_axis=0, tiled=True, axis_in...  14.6 us
    ppermute x2, starting transfers between devices, across(): return lax.ppermute(v, ('dp', 'seq'), pairs)  8.49 us
    pallas_call x1, Pallas kernels, scan_local(): pl.pallas_call(lambda *refs: local_kernel(lay, *refs), in_specs=[vmem] *...  7.2 us
    ppermute x3, starting transfers between devices, from_partner(): lax.ppermute(v, 'seq', [(i, (i + groups) % (2 * groups)) for i in range(2...  7.18 us
    ppermute x3, waiting for transfers between devices, from_partner(): lax.ppermute(v, 'seq', [(i, (i + groups) % (2 * groups)) for i in range(2...  4.16 us
    pallas_call x1, Pallas kernels, scan_states(): pl.pallas_call(lambda *refs: states_kernel(lay, *refs), in_specs=[vmem, v...  3.01 us
  transfers between devices with their start and end apart: 8, of which 4 were waited for; matrix products, arithmetic and copies ran while one was open for 0% of the time, Pallas kernels for 9%

profile of v7, /device:TPU:2, one launch (start us, length us, event | category | flops | bytes accessed | tf_op | source)
XLA Modules:
  0.0 108.4 jit_solution(1287893470910602655)
XLA Ops:
  0.6 3.0 %pack.1 = bf16[8,1296,128]{2,1,0:T(8,128)(2,1)} custom-call(bf16[128,4096]{1,0:T(8,128)(2,1)} %bitcast.17, bf16[128,4096]{1,0:T(8,128)(2,1)} %bitcast.18, bf16[128,4096]{1,0:T(8,128)(2,1)} %bitcast.19, bf16[128,4096]{1,0:T(8,128)(2,1)} %bitcast.20, bf16[128,128]{1,0:T(8,128)(2,1)} %bitcast.21, bf16[128,128]{1,0:T(8,128)(2,1)} %bitcast.22, ...), custom_call_target="tpu_custom_call" | custom-call | tf_op jit(solution)/shard_map/pack/pallas_call | solution.py:96
  3.6 0.0 copy-start
  3.6 0.0 copy-start.1
  3.6 0.0 copy-start.2
  3.6 9.6 %all-to-all-start = ((bf16[8,1296,128]{2,1,0:T(8,128)(2,1)}), bf16[8,1296,128]{2,1,0:T(8,128)(2,1)S(1)}, u32[]{:S(2)}, u32[]{:S(2)}) async-start(bf16[8,1296,128]{2,1,0:T(8,128)(2,1)} %pack.1), calls=%async_computation | async-start | bytes 5308416 | tf_op jit(solution)/shard_map/all_to_all | solution.py:478
  13.2 0.0 copy-done
  13.2 0.0 copy-done.1
  13.2 0.0 copy-done.2
  13.2 1.9 %collective-permute-start = (f32[3,4]{1,0:T(4,128)S(1)}, f32[3,4]{1,0:T(4,128)S(1)}, u32[]{:S(2)}, u32[]{:S(2)}) collective-permute-start(f32[3,4]{1,0:T(4,128)S(1)} %pad_maximum_fusion), channel_id=1, source_target_pairs={{0,8},{1,9},{2,10},{3,11},{4,12},{5,13},{6,14},{7,15},{8,0},{9,1},... | collective-permute-start | bytes 152 | tf_op jit(solution)/shard_map/ppermute | solution.py:483
  15.2 3.5 %collective-permute-done = f32[3,4]{1,0:T(4,128)S(1)} collective-permute-done((f32[3,4]{1,0:T(4,128)S(1)}, f32[3,4]{1,0:T(4,128)S(1)}, u32[]{:S(2)}, u32[]{:S(2)}) %collective-permute-start) | collective-permute-done | bytes 80 | tf_op jit(solution)/shard_map/ppermute | solution.py:483
  18.7 0.1 select_maximum_fusion.refs_1_
  18.8 26.1 %all-to-all-done.refs_0_ = bf16[8,1296,128]{2,1,0:T(8,128)(2,1)S(1)} async-done(((bf16[8,1296,128]{2,1,0:T(8,128)(2,1)}), bf16[8,1296,128]{2,1,0:T(8,128)(2,1)S(1)}, u32[]{:S(2)}, u32[]{:S(2)}) %all-to-all-start) | async-done | bytes 2654240 | tf_op jit(solution)/shard_map/all_to_all | solution.py:478
  44.9 3.0 %scan_states.1 = (bf16[8,128,512]{2,1,0:T(8,128)(2,1)S(1)}, bf16[8,128,512]{2,1,0:T(8,128)(2,1)S(1)}, bf16[8,128,512]{2,1,0:T(8,128)(2,1)S(1)}, bf16[8,128,512]{...) custom-call(bf16[8,1296,128]{2,1,0:T(8,128)(2,1)S(1)} %all-to-all-do, ...), custom_call_target="tpu_custom_call" | custom-call | tf_op jit(solution)/shard_map/scan_states/pallas_call | solution.py:230
  48.0 1.9 %collective-permute-start.1 = (f32[128,512]{1,0:T(8,128)S(1)}, f32[128,512]{1,0:T(8,128)S(1)}, u32[]{:S(2)}, u32[]{:S(2)}) collective-permute-start(f32[128,512]{1,0:T(8,128)S(1)} %get-tuple-element.60.refs_11_), channel_id=1, source_target_pairs={{0,8},{1,9},{2,10},{3,11},{4,12},{5,13},{6,14},{7,15},{8,0},{9,1},... | collective-permute-start | bytes 786440 | tf_op jit(solution)/shard_map/ppermute | solution.py:483
  49.9 7.2 %scan_local.1 = (f32[8,128,512]{2,1,0:T(8,128)S(1)}, f32[8,128,128]{2,1,0:T(8,128)S(1)}, f32[8,128,128]{2,1,0:T(8,128)S(1)}, f32[8,8,128]{2,1,0:T(8,128)S(1)}, f32[8,8,128]{2,1,0:T(8,128)S(1)}) custom-call(bf16[8,1296,128]{2,1,0:T(8,128)(2,1)S(1)} %all-to-all-done.refs_0_, bf16[8,128,512]{2,1,0:T(8,128)(2,1)S(1)} %get-tuple-element.44.refs_1_.refs_0_, ...), custom_call_target="tpu_custom_call" | custom-call | tf_op jit(solution)/shard_map/scan_local/pallas_call | solution.py:285
  57.1 0.6 collective-permute-done.1.refs_12_
  57.7 2.4 %scan_finish.1 = (bf16[8,16,128]{2,1,0:T(8,128)(2,1)S(1)}, f32[8,128]{1,0:T(8,128)S(1)}, bf16[8,128,512]{2,1,0:T(8,128)(2,1)S(1)}, bf16[8,128,512]{2,1,0:T(8,128)(2,1)S(1)}, f32[8,128,512]{2,1,0:T(8,128)S(1)}) custom-call(bf16[8,1296,128]{2,1,0:T(8,128)(2,1)S(1)} %all-to-all-done.refs_0_, bf16[8,128,512]{2,1,0:T(8,128)(2,1)S(1)} %get-tuple-element.44.refs_1_.refs_0_, ...), custom_call_target="tpu_custom_call" | custom-call | tf_op jit(solution)/shard_map/scan_finish/pallas_call | solution.py:370
  60.1 3.3 %collective-permute-start.2 = (f32[8,128]{1,0:T(8,128)S(1)}, f32[8,128]{1,0:T(8,128)S(1)}, u32[]{:S(2)}, u32[]{:S(2)}) collective-permute-start(f32[8,128]{1,0:T(8,128)S(1)} %get-tuple-element.67), channel_id=1, source_target_pairs={{0,8},{1,9},{2,10},{3,11},{4,12},{5,13},{6,14},{7,15},{8,0},{9,1},... | collective-permute-start | bytes 12296 | tf_op jit(solution)/shard_map/ppermute | solution.py:483
  63.5 2.3 %message.1 = bf16[8,1040,128]{2,1,0:T(8,128)(2,1)} custom-call(bf16[8,128,512]{2,1,0:T(8,128)(2,1)S(1)} %get-tuple-element.44.refs_1_.refs_0_, bf16[8,128,512]{2,1,0:T(8,128)(2,1)S(1)} %get-tuple-element.45.refs_2_.refs_1_, bf16[8,128,512]{2,1,0:T(8,128)(2,1)S(1)} %get-tuple-element.46.refs_3_.refs_2_, ...), custom_call_target="tpu_custom_call" | custom-call | flops 400000000 | bytes 20000000 | tf_op jit(solution)/shard_map/message/pallas_call | solution.py:425
  65.8 0.0 collective-permute-done.2
  65.8 5.0 %all-to-all-start.1 = ((bf16[8,1040,128]{2,1,0:T(8,128)(2,1)}), bf16[8,1040,128]{2,1,0:T(8,128)(2,1)S(1)}, u32[]{:S(2)}, u32[]{:S(2)}) async-start(bf16[8,1040,128]{2,1,0:T(8,128)(2,1)} %message.1), calls=%async_computation.1 | async-start | bytes 4259840 | tf_op jit(solution)/shard_map/all_to_all | solution.py:478
  70.8 1.9 %collective-permute-start.5 = (f32[8,128]{1,0:T(8,128)S(1)}, f32[8,128]{1,0:T(8,128)S(1)}, u32[]{:S(2)}, u32[]{:S(2)}) collective-permute-start(f32[8,128]{1,0:T(8,128)S(1)} %add.17), channel_id=1, source_target_pairs={{0,56},{1,57},{2,58},{3,59},{4,60},{5,61},{6,62},{7,63},{8,48},{9,... | collective-permute-start | bytes 12296 | tf_op jit(solution)/shard_map/ppermute | solution.py:494
  72.7 1.9 %collective-permute-start.4 = (f32[8,128]{1,0:T(8,128)S(1)}, f32[8,128]{1,0:T(8,128)S(1)}, u32[]{:S(2)}, u32[]{:S(2)}) collective-permute-start(f32[8,128]{1,0:T(8,128)S(1)} %add.17), channel_id=1, source_target_pairs={{0,32},{16,48},{32,0},{48,16},{64,96},{80,112},{96,64},{112,80},{1... | collective-permute-start | bytes 12296 | tf_op jit(solution)/shard_map/ppermute | solution.py:498
  74.6 6.6 %collective-permute-start.3 = (f32[8,128]{1,0:T(8,128)S(1)}, f32[8,128]{1,0:T(8,128)S(1)}, u32[]{:S(2)}, u32[]{:S(2)}) collective-permute-start(f32[8,128]{1,0:T(8,128)S(1)} %add.17), channel_id=1, source_target_pairs={{0,24},{1,25},{2,26},{3,27},{4,28},{5,29},{6,30},{7,31},{8,16},{9,... | collective-permute-start | bytes 12296 | tf_op jit(solution)/shard_map/ppermute | solution.py:494
  81.2 0.0 collective-permute-done.5
  81.2 0.0 collective-permute-done.4
  81.2 1.6 %collective-permute-done.3 = f32[8,128]{1,0:T(8,128)S(1)} collective-permute-done((f32[8,128]{1,0:T(8,128)S(1)}, f32[8,128]{1,0:T(8,128)S(1)}, u32[]{:S(2)}, u32[]{:S(2)}) %collective-permute-start.3) | collective-permute-done | bytes 4128 | tf_op jit(solution)/shard_map/ppermute | solution.py:494
  82.8 24.2 %psum.7.refs_1_ = f32[8,128]{1,0:T(8,128)S(1)} all-reduce(f32[8,128]{1,0:T(8,128)S(1)} %add_add_fusion), channel_id=1, replica_groups={{0,64,128,192,256,320,384,448},{16,80,144,208,272,336,400,464},{32,96,1..., use_global_device_ids=true, to_apply=%region_0.1 | all-reduce | flops 1024 | bytes 8192 | tf_op jit(solution)/shard_map/psum | solution.py:506
  107.0 0.0 all-to-all-done.1.refs_0_
  107.0 1.4 %unpack.1 = (bf16[128,4096]{1,0:T(8,128)(2,1)}, bf16[64,128]{1,0:T(8,128)(2,1)}, bf16[128,128]{1,0:T(8,128)(2,1)}, bf16[128,128]{1,0:T(8,128)(2,1)}, f32[3,4]{1,0:T(4,128)}) custom-call(bf16[8,1040,128]{2,1,0:T(8,128)(2,1)S(1)} %all-to-all-done.1.refs_0_, f32[8,128]{1,0:T(8,128)S(1)} %psum.7.refs_1_, s32[1]{0:T(128)} %bitcast.9.refs_2_.refs_15_.refs_12_), custom_call_target="tpu_custom_call" | custom-call | tf_op jit(solution)/shard_map/unpack/pallas_call | solution.py:464
  (4 shorter events, 0.0 us)
Async XLA Ops:
  3.6 9.6 %copy-start = (f32[4]{0:T(128)S(1)}, f32[4]{0:T(128)}, u32[]{:S(2)}) copy-start(f32[4]{0:T(128)} %param.15) | copy-start | bytes 52
  3.6 9.6 %copy-start.1 = (f32[4]{0:T(128)S(1)}, f32[4]{0:T(128)}, u32[]{:S(2)}) copy-start(f32[4]{0:T(128)} %param.14) | copy-start | bytes 52
  3.6 9.6 %copy-start.2 = (f32[4]{0:T(128)S(1)}, f32[4]{0:T(128)}, u32[]{:S(2)}) copy-start(f32[4]{0:T(128)} %param.13) | copy-start | bytes 52
  3.6 41.3 %all-to-all-start = ((bf16[8,1296,128]{2,1,0:T(8,128)(2,1)}), bf16[8,1296,128]{2,1,0:T(8,128)(2,1)S(1)}, u32[]{:S(2)}, u32[]{:S(2)}) async-start(bf16[8,1296,128]{2,1,0:T(8,128)(2,1)} %pack.1), calls=%async_computation | async-start | bytes 5308416 | tf_op jit(solution)/shard_map/all_to_all | solution.py:478
  13.2 5.5 %collective-permute-start = (f32[3,4]{1,0:T(4,128)S(1)}, f32[3,4]{1,0:T(4,128)S(1)}, u32[]{:S(2)}, u32[]{:S(2)}) collective-permute-start(f32[3,4]{1,0:T(4,128)S(1)} %pad_maximum_fusion), channel_id=1, source_target_pairs={{0,8},{1,9},{2,10},{3,11},{4,12},{5,13},{6,14},{7,15},{8,0},{9,1},... | collective-permute-start | bytes 152 | tf_op jit(solution)/shard_map/ppermute | solution.py:483
  48.0 9.7 %collective-permute-start.1 = (f32[128,512]{1,0:T(8,128)S(1)}, f32[128,512]{1,0:T(8,128)S(1)}, u32[]{:S(2)}, u32[]{:S(2)}) collective-permute-start(f32[128,512]{1,0:T(8,128)S(1)} %get-tuple-element.60.refs_11_), channel_id=1, source_target_pairs={{0,8},{1,9},{2,10},{3,11},{4,12},{5,13},{6,14},{7,15},{8,0},{9,1},... | collective-permute-start | bytes 786440 | tf_op jit(solution)/shard_map/ppermute | solution.py:483
  60.1 5.7 %collective-permute-start.2 = (f32[8,128]{1,0:T(8,128)S(1)}, f32[8,128]{1,0:T(8,128)S(1)}, u32[]{:S(2)}, u32[]{:S(2)}) collective-permute-start(f32[8,128]{1,0:T(8,128)S(1)} %get-tuple-element.67), channel_id=1, source_target_pairs={{0,8},{1,9},{2,10},{3,11},{4,12},{5,13},{6,14},{7,15},{8,0},{9,1},... | collective-permute-start | bytes 12296 | tf_op jit(solution)/shard_map/ppermute | solution.py:483
  65.8 41.2 %all-to-all-start.1 = ((bf16[8,1040,128]{2,1,0:T(8,128)(2,1)}), bf16[8,1040,128]{2,1,0:T(8,128)(2,1)S(1)}, u32[]{:S(2)}, u32[]{:S(2)}) async-start(bf16[8,1040,128]{2,1,0:T(8,128)(2,1)} %message.1), calls=%async_computation.1 | async-start | bytes 4259840 | tf_op jit(solution)/shard_map/all_to_all | solution.py:478
  70.8 10.4 %collective-permute-start.5 = (f32[8,128]{1,0:T(8,128)S(1)}, f32[8,128]{1,0:T(8,128)S(1)}, u32[]{:S(2)}, u32[]{:S(2)}) collective-permute-start(f32[8,128]{1,0:T(8,128)S(1)} %add.17), channel_id=1, source_target_pairs={{0,56},{1,57},{2,58},{3,59},{4,60},{5,61},{6,62},{7,63},{8,48},{9,... | collective-permute-start | bytes 12296 | tf_op jit(solution)/shard_map/ppermute | solution.py:494
  72.7 8.5 %collective-permute-start.4 = (f32[8,128]{1,0:T(8,128)S(1)}, f32[8,128]{1,0:T(8,128)S(1)}, u32[]{:S(2)}, u32[]{:S(2)}) collective-permute-start(f32[8,128]{1,0:T(8,128)S(1)} %add.17), channel_id=1, source_target_pairs={{0,32},{16,48},{32,0},{48,16},{64,96},{80,112},{96,64},{112,80},{1... | collective-permute-start | bytes 12296 | tf_op jit(solution)/shard_map/ppermute | solution.py:498
  74.6 8.2 %collective-permute-start.3 = (f32[8,128]{1,0:T(8,128)S(1)}, f32[8,128]{1,0:T(8,128)S(1)}, u32[]{:S(2)}, u32[]{:S(2)}) collective-permute-start(f32[8,128]{1,0:T(8,128)S(1)} %add.17), channel_id=1, source_target_pairs={{0,24},{1,25},{2,26},{3,27},{4,28},{5,29},{6,30},{7,31},{8,16},{9,... | collective-permute-start | bytes 12296 | tf_op jit(solution)/shard_map/ppermute | solution.py:494

commit v8 on v6

--- a/solution.py
+++ b/solution.py
@@ -525,7 +525,8 @@
     back = message(own, local, finish, flag, lay)
     per_head = finish[1] + from_partner(finish[1])
     back, per_head = lax.optimization_barrier((back, per_head))
-    sums = line_sum(across_sum(per_head))
+    back, per_head = lax.optimization_barrier((back, across_sum(per_head)))
+    sums = line_sum(per_head)
     grad_x, grad_step, grad_write, grad_read, totals = unpack(exchange(back), sums, flag, lax.axis_size("dp"), lay)
     return grad_x[None], grad_step.T[None], grad_write[None], grad_read[None], totals
 

time: 107 us -> 107 us (level)
  the two profiles are of different devices: /device:TPU:2 before, /device:TPU:1 now
where the time goes in v8:
time: 107 us
  waiting for transfers between devices  39.9 us (37%)
  starting transfers between devices  27.6 us (26%)
  Pallas kernels  19.4 us (18%)
  blocking collectives  18.8 us (18%)
    all_to_all x2, waiting for transfers between devices, exchange(): lax.all_to_all(v, 'seq', split_axis=0, concat_axis=0, tiled=True, axis_in...  30.8 us
    psum x1, blocking collectives, line_sum(): return lax.psum(v, 'dp', axis_index_groups=lines)  18.8 us
    all_to_all x2, starting transfers between devices, exchange(): lax.all_to_all(v, 'seq', split_axis=0, concat_axis=0, tiled=True, axis_in...  16.6 us
    pallas_call x1, Pallas kernels, scan_local(): pl.pallas_call(lambda *refs: local_kernel(lay, *refs), in_specs=[vmem] *...  7.2 us
    ppermute x3, starting transfers between devices, from_partner(): lax.ppermute(v, 'seq', [(i, (i + groups) % (2 * groups)) for i in range(2...  7.19 us
    ppermute x1, waiting for transfers between devices, across_sum(): return v + lax.ppermute(v, ('dp', 'seq'), across)  3.63 us
    pallas_call x1, Pallas kernels, scan_states(): pl.pallas_call(lambda *refs: states_kernel(lay, *refs), in_specs=[vmem, v...  3.03 us
    pallas_call x1, Pallas kernels, pack(): pl.pallas_call(lambda *refs: pack_kernel(groups, *refs), grid=(PACK_STEPS...  2.96 us
  transfers between devices with their start and end apart: 7, of which 5 were waited for; matrix products, arithmetic and copies ran while one was open for 0% of the time, Pallas kernels for 9%

profile of v8, /device:TPU:1, one launch (start us, length us, event | category | flops | bytes accessed | tf_op | source)
XLA Modules:
  0.0 106.6 jit_solution(247120584022747559)
XLA Ops:
  0.6 3.0 %pack.1 = bf16[8,1296,128]{2,1,0:T(8,128)(2,1)} custom-call(bf16[128,4096]{1,0:T(8,128)(2,1)} %bitcast.17, bf16[128,4096]{1,0:T(8,128)(2,1)} %bitcast.18, bf16[128,4096]{1,0:T(8,128)(2,1)} %bitcast.19, bf16[128,4096]{1,0:T(8,128)(2,1)} %bitcast.20, bf16[128,128]{1,0:T(8,128)(2,1)} %bitcast.21, bf16[128,128]{1,0:T(8,128)(2,1)} %bitcast.22, ...), custom_call_target="tpu_custom_call" | custom-call | tf_op jit(solution)/shard_map/pack/pallas_call | solution.py:96
  3.6 0.0 copy-start
  3.6 0.0 copy-start.1
  3.6 0.0 copy-start.2
  3.6 10.6 %all-to-all-start = ((bf16[8,1296,128]{2,1,0:T(8,128)(2,1)}), bf16[8,1296,128]{2,1,0:T(8,128)(2,1)S(1)}, u32[]{:S(2)}, u32[]{:S(2)}) async-start(bf16[8,1296,128]{2,1,0:T(8,128)(2,1)} %pack.1), calls=%async_computation | async-start | bytes 5308416 | tf_op jit(solution)/shard_map/all_to_all | solution.py:478
  14.2 0.0 copy-done
  14.2 0.0 copy-done.1
  14.2 0.0 copy-done.2
  14.2 1.9 %collective-permute-start = (f32[3,4]{1,0:T(4,128)S(1)}, f32[3,4]{1,0:T(4,128)S(1)}, u32[]{:S(2)}, u32[]{:S(2)}) collective-permute-start(f32[3,4]{1,0:T(4,128)S(1)} %pad_maximum_fusion), channel_id=1, source_target_pairs={{0,8},{1,9},{2,10},{3,11},{4,12},{5,13},{6,14},{7,15},{8,0},{9,1},... | collective-permute-start | bytes 152 | tf_op jit(solution)/shard_map/ppermute | solution.py:483
  16.1 2.7 %collective-permute-done = f32[3,4]{1,0:T(4,128)S(1)} collective-permute-done((f32[3,4]{1,0:T(4,128)S(1)}, f32[3,4]{1,0:T(4,128)S(1)}, u32[]{:S(2)}, u32[]{:S(2)}) %collective-permute-start) | collective-permute-done | bytes 80 | tf_op jit(solution)/shard_map/ppermute | solution.py:483
  18.8 0.1 select_maximum_fusion.refs_1_
  18.9 27.6 %all-to-all-done.refs_0_ = bf16[8,1296,128]{2,1,0:T(8,128)(2,1)S(1)} async-done(((bf16[8,1296,128]{2,1,0:T(8,128)(2,1)}), bf16[8,1296,128]{2,1,0:T(8,128)(2,1)S(1)}, u32[]{:S(2)}, u32[]{:S(2)}) %all-to-all-start) | async-done | bytes 2654240 | tf_op jit(solution)/shard_map/all_to_all | solution.py:478
  46.5 3.0 %scan_states.1 = (bf16[8,128,512]{2,1,0:T(8,128)(2,1)S(1)}, bf16[8,128,512]{2,1,0:T(8,128)(2,1)S(1)}, bf16[8,128,512]{2,1,0:T(8,128)(2,1)S(1)}, bf16[8,128,512]{...) custom-call(bf16[8,1296,128]{2,1,0:T(8,128)(2,1)S(1)} %all-to-all-do, ...), custom_call_target="tpu_custom_call" | custom-call | tf_op jit(solution)/shard_map/scan_states/pallas_call | solution.py:230
  49.5 1.9 %collective-permute-start.1 = (f32[128,512]{1,0:T(8,128)S(1)}, f32[128,512]{1,0:T(8,128)S(1)}, u32[]{:S(2)}, u32[]{:S(2)}) collective-permute-start(f32[128,512]{1,0:T(8,128)S(1)} %get-tuple-element.62.refs_11_), channel_id=1, source_target_pairs={{0,8},{1,9},{2,10},{3,11},{4,12},{5,13},{6,14},{7,15},{8,0},{9,1},... | collective-permute-start | bytes 786440 | tf_op jit(solution)/shard_map/ppermute | solution.py:483
  51.5 7.2 %scan_local.1 = (f32[8,128,512]{2,1,0:T(8,128)S(1)}, f32[8,128,128]{2,1,0:T(8,128)S(1)}, f32[8,128,128]{2,1,0:T(8,128)S(1)}, f32[8,8,128]{2,1,0:T(8,128)S(1)}, f32[8,8,128]{2,1,0:T(8,128)S(1)}) custom-call(bf16[8,1296,128]{2,1,0:T(8,128)(2,1)S(1)} %all-to-all-done.refs_0_, bf16[8,128,512]{2,1,0:T(8,128)(2,1)S(1)} %get-tuple-element.46.refs_1_.refs_0_, ...), custom_call_target="tpu_custom_call" | custom-call | tf_op jit(solution)/shard_map/scan_local/pallas_call | solution.py:285
  58.7 0.0 collective-permute-done.1.refs_12_
  58.7 2.5 %scan_finish.1 = (bf16[8,16,128]{2,1,0:T(8,128)(2,1)S(1)}, f32[8,128]{1,0:T(8,128)S(1)}, bf16[8,128,512]{2,1,0:T(8,128)(2,1)S(1)}, bf16[8,128,512]{2,1,0:T(8,128)(2,1)S(1)}, f32[8,128,512]{2,1,0:T(8,128)S(1)}) custom-call(bf16[8,1296,128]{2,1,0:T(8,128)(2,1)S(1)} %all-to-all-done.refs_0_, bf16[8,128,512]{2,1,0:T(8,128)(2,1)S(1)} %get-tuple-element.46.refs_1_.refs_0_, ...), custom_call_target="tpu_custom_call" | custom-call | tf_op jit(solution)/shard_map/scan_finish/pallas_call | solution.py:370
  61.1 3.4 %collective-permute-start.2 = (f32[8,128]{1,0:T(8,128)S(1)}, f32[8,128]{1,0:T(8,128)S(1)}, u32[]{:S(2)}, u32[]{:S(2)}) collective-permute-start(f32[8,128]{1,0:T(8,128)S(1)} %get-tuple-element.69), channel_id=1, source_target_pairs={{0,8},{1,9},{2,10},{3,11},{4,12},{5,13},{6,14},{7,15},{8,0},{9,1},... | collective-permute-start | bytes 12296 | tf_op jit(solution)/shard_map/ppermute | solution.py:483
  64.5 2.3 %message.1 = bf16[8,1040,128]{2,1,0:T(8,128)(2,1)} custom-call(bf16[8,128,512]{2,1,0:T(8,128)(2,1)S(1)} %get-tuple-element.46.refs_1_.refs_0_, bf16[8,128,512]{2,1,0:T(8,128)(2,1)S(1)} %get-tuple-element.47.refs_2_.refs_1_, bf16[8,128,512]{2,1,0:T(8,128)(2,1)S(1)} %get-tuple-element.48.refs_3_.refs_2_, ...), custom_call_target="tpu_custom_call" | custom-call | flops 400000000 | bytes 20000000 | tf_op jit(solution)/shard_map/message/pallas_call | solution.py:425
  66.8 0.0 collective-permute-done.2
  66.8 1.9 %collective-permute-start.3 = (f32[8,128]{1,0:T(8,128)S(1)}, f32[8,128]{1,0:T(8,128)S(1)}, u32[]{:S(2)}, u32[]{:S(2)}) collective-permute-start(f32[8,128]{1,0:T(8,128)S(1)} %add.14), channel_id=1, source_target_pairs={{0,24},{1,25},{2,26},{3,27},{4,28},{5,29},{6,30},{7,31},{8,16},{9,... | collective-permute-start | bytes 12296 | tf_op jit(solution)/shard_map/ppermute | solution.py:492
  68.8 3.6 %collective-permute-done.3 = f32[8,128]{1,0:T(8,128)S(1)} collective-permute-done((f32[8,128]{1,0:T(8,128)S(1)}, f32[8,128]{1,0:T(8,128)S(1)}, u32[]{:S(2)}, u32[]{:S(2)}) %collective-permute-start.3) | collective-permute-done | bytes 4128 | tf_op jit(solution)/shard_map/ppermute | solution.py:492
  72.4 6.1 %all-to-all-start.1 = ((bf16[8,1040,128]{2,1,0:T(8,128)(2,1)}), bf16[8,1040,128]{2,1,0:T(8,128)(2,1)S(1)}, u32[]{:S(2)}, u32[]{:S(2)}) async-start(bf16[8,1040,128]{2,1,0:T(8,128)(2,1)} %message.1), calls=%async_computation.1 | async-start | bytes 4259840 | tf_op jit(solution)/shard_map/all_to_all | solution.py:478
  78.5 1.9 %collective-permute-start.4 = (f32[8,128]{1,0:T(8,128)S(1)}, f32[8,128]{1,0:T(8,128)S(1)}, u32[]{:S(2)}, u32[]{:S(2)}) collective-permute-start(f32[8,128]{1,0:T(8,128)S(1)} %add.15), channel_id=1, source_target_pairs={{0,32},{16,48},{32,0},{48,16},{64,96},{80,112},{96,64},{112,80},{1... | collective-permute-start | bytes 12296 | tf_op jit(solution)/shard_map/ppermute | solution.py:499
  80.4 2.7 %collective-permute-done.4 = f32[8,128]{1,0:T(8,128)S(1)} collective-permute-done((f32[8,128]{1,0:T(8,128)S(1)}, f32[8,128]{1,0:T(8,128)S(1)}, u32[]{:S(2)}, u32[]{:S(2)}) %collective-permute-start.4) | collective-permute-done | bytes 4128 | tf_op jit(solution)/shard_map/ppermute | solution.py:499
  83.1 18.8 %psum.7.refs_1_ = f32[8,128]{1,0:T(8,128)S(1)} all-reduce(f32[8,128]{1,0:T(8,128)S(1)} %add.16), channel_id=1, replica_groups={{0,64,128,192,256,320,384,448},{16,80,144,208,272,336,400,464},{32,96,1..., use_global_device_ids=true, to_apply=%region_0.1 | all-reduce | flops 1024 | bytes 8192 | tf_op jit(solution)/shard_map/psum | solution.py:503
  101.9 3.2 %all-to-all-done.1.refs_0_ = bf16[8,1040,128]{2,1,0:T(8,128)(2,1)S(1)} async-done(((bf16[8,1040,128]{2,1,0:T(8,128)(2,1)}), bf16[8,1040,128]{2,1,0:T(8,128)(2,1)S(1)}, u32[]{:S(2)}, u32[]{:S(2)}) %all-to-all-start.1) | async-done | bytes 2129952 | tf_op jit(solution)/shard_map/all_to_all | solution.py:478
  105.2 1.4 %unpack.1 = (bf16[128,4096]{1,0:T(8,128)(2,1)}, bf16[64,128]{1,0:T(8,128)(2,1)}, bf16[128,128]{1,0:T(8,128)(2,1)}, bf16[128,128]{1,0:T(8,128)(2,1)}, f32[3,4]{1,0:T(4,128)}) custom-call(bf16[8,1040,128]{2,1,0:T(8,128)(2,1)S(1)} %all-to-all-done.1.refs_0_, f32[8,128]{1,0:T(8,128)S(1)} %psum.7.refs_1_, s32[1]{0:T(128)} %bitcast.9.refs_2_.refs_15_.refs_12_), custom_call_target="tpu_custom_call" | custom-call | tf_op jit(solution)/shard_map/unpack/pallas_call | solution.py:464
  (5 shorter events, 0.0 us)
Async XLA Ops:
  3.6 10.6 %copy-start = (f32[4]{0:T(128)S(1)}, f32[4]{0:T(128)}, u32[]{:S(2)}) copy-start(f32[4]{0:T(128)} %param.15) | copy-start | bytes 52
  3.6 10.6 %copy-start.1 = (f32[4]{0:T(128)S(1)}, f32[4]{0:T(128)}, u32[]{:S(2)}) copy-start(f32[4]{0:T(128)} %param.14) | copy-start | bytes 52
  3.6 10.6 %copy-start.2 = (f32[4]{0:T(128)S(1)}, f32[4]{0:T(128)}, u32[]{:S(2)}) copy-start(f32[4]{0:T(128)} %param.13) | copy-start | bytes 52
  3.6 42.9 %all-to-all-start = ((bf16[8,1296,128]{2,1,0:T(8,128)(2,1)}), bf16[8,1296,128]{2,1,0:T(8,128)(2,1)S(1)}, u32[]{:S(2)}, u32[]{:S(2)}) async-start(bf16[8,1296,128]{2,1,0:T(8,128)(2,1)} %pack.1), calls=%async_computation | async-start | bytes 5308416 | tf_op jit(solution)/shard_map/all_to_all | solution.py:478
  14.2 4.6 %collective-permute-start = (f32[3,4]{1,0:T(4,128)S(1)}, f32[3,4]{1,0:T(4,128)S(1)}, u32[]{:S(2)}, u32[]{:S(2)}) collective-permute-start(f32[3,4]{1,0:T(4,128)S(1)} %pad_maximum_fusion), channel_id=1, source_target_pairs={{0,8},{1,9},{2,10},{3,11},{4,12},{5,13},{6,14},{7,15},{8,0},{9,1},... | collective-permute-start | bytes 152 | tf_op jit(solution)/shard_map/ppermute | solution.py:483
  49.5 9.1 %collective-permute-start.1 = (f32[128,512]{1,0:T(8,128)S(1)}, f32[128,512]{1,0:T(8,128)S(1)}, u32[]{:S(2)}, u32[]{:S(2)}) collective-permute-start(f32[128,512]{1,0:T(8,128)S(1)} %get-tuple-element.62.refs_11_), channel_id=1, source_target_pairs={{0,8},{1,9},{2,10},{3,11},{4,12},{5,13},{6,14},{7,15},{8,0},{9,1},... | collective-permute-start | bytes 786440 | tf_op jit(solution)/shard_map/ppermute | solution.py:483
  61.1 5.7 %collective-permute-start.2 = (f32[8,128]{1,0:T(8,128)S(1)}, f32[8,128]{1,0:T(8,128)S(1)}, u32[]{:S(2)}, u32[]{:S(2)}) collective-permute-start(f32[8,128]{1,0:T(8,128)S(1)} %get-tuple-element.69), channel_id=1, source_target_pairs={{0,8},{1,9},{2,10},{3,11},{4,12},{5,13},{6,14},{7,15},{8,0},{9,1},... | collective-permute-start | bytes 12296 | tf_op jit(solution)/shard_map/ppermute | solution.py:483
  66.8 5.6 %collective-permute-start.3 = (f32[8,128]{1,0:T(8,128)S(1)}, f32[8,128]{1,0:T(8,128)S(1)}, u32[]{:S(2)}, u32[]{:S(2)}) collective-permute-start(f32[8,128]{1,0:T(8,128)S(1)} %add.14), channel_id=1, source_target_pairs={{0,24},{1,25},{2,26},{3,27},{4,28},{5,29},{6,30},{7,31},{8,16},{9,... | collective-permute-start | bytes 12296 | tf_op jit(solution)/shard_map/ppermute | solution.py:492
  72.4 32.8 %all-to-all-start.1 = ((bf16[8,1040,128]{2,1,0:T(8,128)(2,1)}), bf16[8,1040,128]{2,1,0:T(8,128)(2,1)S(1)}, u32[]{:S(2)}, u32[]{:S(2)}) async-start(bf16[8,1040,128]{2,1,0:T(8,128)(2,1)} %message.1), calls=%async_computation.1 | async-start | bytes 4259840 | tf_op jit(solution)/shard_map/all_to_all | solution.py:478
  78.5 4.6 %collective-permute-start.4 = (f32[8,128]{1,0:T(8,128)S(1)}, f32[8,128]{1,0:T(8,128)S(1)}, u32[]{:S(2)}, u32[]{:S(2)}) collective-permute-start(f32[8,128]{1,0:T(8,128)S(1)} %add.15), channel_id=1, source_target_pairs={{0,32},{16,48},{32,0},{48,16},{64,96},{80,112},{96,64},{112,80},{1... | collective-permute-start | bytes 12296 | tf_op jit(solution)/shard_map/ppermute | solution.py:499
